TPU v7x, 32 devices: a whole 2x2x4 slice. The times are simulated.
32 devices in a mesh: row: 4 (over x, core), col: 8 (over z, y).
Axes of the slice: x: 2, y: 2, z: 4, core: 2. Of those that a mesh axis runs over, the one named last changes fastest.
Arguments:
- inputs: float32 [1500, 10240], P('row', 'col'), may hold values from -6 to 6
- lengths: int32 [8], P('row'), may hold values from 375 to 1500, as said below
- cotangent: bfloat16 [1500, 10240], P('row', 'col'), may hold values from -6 to 6
- ln1_gain: float32 [1280], P('col'), may hold values from 0.1 to 1.9
- ln1_bias: float32 [1280], P('col'), may hold values from -1.75 to 1.75
- w_query: float32 [1280, 1280], P('row', 'col'), may hold values from -0.15625 to 0.15625
- b_query: float32 [1280], P('col'), may hold values from -3 to 3
- w_key: float32 [1280, 1280], P('row', 'col'), may hold values from -0.15625 to 0.15625
- w_value: float32 [1280, 1280], P('row', 'col'), may hold values from -0.15625 to 0.15625
- b_value: float32 [1280], P('col'), may hold values from -0.3125 to 0.3125
- w_attn_out: float32 [1280, 1280], P('col', 'row'), may hold values from -2 to 2
- b_attn_out: float32 [1280], P('col'), may hold values from -1.75 to 1.75
- ln2_gain: float32 [1280], P('col'), may hold values from 0.1 to 1.9
- ln2_bias: float32 [1280], P('col'), may hold values from -1.75 to 1.75
- w_in: float32 [1280, 5120], P('row', 'col'), may hold values from -0.15625 to 0.15625
- b_in: float32 [5120], P('col'), may hold values from -3 to 3
- w_out: float32 [5120, 1280], P('col', 'row'), may hold values from -0.078125 to 0.078125
- b_out: float32 [1280], P('col'), may hold values from -1.75 to 1.75
Outputs:
- layer_out: float32 [1500, 10240], P('row', 'col')
- input_grad: float32 [1500, 10240], P('row', 'col')
- ln1_gain_grad: float32 [1280], P('col')
- ln1_bias_grad: float32 [1280], P('col')
- w_query_grad: float32 [1280, 1280], P('row', 'col')
- b_query_grad: float32 [1280], P('col')
- w_key_grad: float32 [1280, 1280], P('row', 'col')
- w_value_grad: float32 [1280, 1280], P('row', 'col')
- b_value_grad: float32 [1280], P('col')
- w_attn_out_grad: float32 [1280, 1280], P('col', 'row')
- b_attn_out_grad: float32 [1280], P('col')
- ln2_gain_grad: float32 [1280], P('col')
- ln2_bias_grad: float32 [1280], P('col')
- w_in_grad: float32 [1280, 5120], P('row', 'col')
- b_in_grad: float32 [5120], P('col')
- w_out_grad: float32 [5120, 1280], P('col', 'row')
- b_out_grad: float32 [1280], P('col')
Inputs may be any that keep to these rules, and one draw needn't show every extreme that they name: `lengths`: valid tokens of a clip; some clip in every draw has all 1500.
All inputs are finite; a program needn't handle non-finite values.
Results may differ from a plain program's by a relative error of at most 0.015.
Values may be sent and summed in bfloat16 or wider, within the bound.
No kernel may reach another device: no remote copies, remote signals or barrier semaphores. Data moves between devices by JAX's collectives and lax.ppermute only.
A program may use at most 192 MiB of HBM per device.

v0:
```python
import jax
import jax.numpy as jnp
from jax import lax
from jax.sharding import PartitionSpec as P

HEADS = 16


EPSILON = 1e-05


def to_half(tensor):
    return tensor.astype(jnp.bfloat16)


def dot_plain(first, second):
    return jnp.dot(first, second, preferred_element_type=jnp.float32)


def dot_left(first, second):
    return lax.dot_general(
        first, second, (((0,), (0,)), ((), ())), preferred_element_type=jnp.float32
    )


def dot_right(first, second):
    return lax.dot_general(
        first, second, (((1,), (1,)), ((), ())), preferred_element_type=jnp.float32
    )


def unpack_rows(tensor):
    packed_rows, packed_width = tensor.shape
    part_width = packed_width // 8
    return (
        tensor.reshape(packed_rows, part_width, 8)
        .transpose(0, 2, 1)
        .reshape(packed_rows * 8, part_width)
    )


def pack_rows(tensor):
    row_count, part_width = tensor.shape
    return (
        tensor.reshape(row_count // 8, 8, part_width)
        .transpose(0, 2, 1)
        .reshape(row_count // 8, part_width * 8)
    )


def row_sums(first, second):
    return lax.psum((jnp.sum(first, axis=1), jnp.sum(second, axis=1)), "col")


def gather_rows(tensor):
    return lax.all_gather(tensor, "col", axis=1, tiled=True)


def reduce_rows(tensor):
    return lax.psum_scatter(tensor, "col", scatter_dimension=1, tiled=True)


def norm_forward(tensor, norm_gain, norm_shift, full_width):
    row_total, row_squares = row_sums(tensor, tensor * tensor)
    row_mean = row_total / full_width
    spread = row_squares / full_width - row_mean * row_mean
    row_scale = lax.rsqrt(spread + EPSILON)
    normal = (tensor - row_mean[:, None]) * row_scale[:, None]
    return (normal, row_scale, normal * norm_gain + norm_shift)


def norm_backward(grad_normed, normal, row_scale, norm_gain, full_width):
    grad_normal = grad_normed * norm_gain
    row_total, inner_sum = row_sums(grad_normal, grad_normal * normal)
    centered = (
        grad_normal - row_total[:, None] / full_width - normal * (inner_sum[:, None] / full_width)
    )
    return row_scale[:, None] * centered


def clip_scores(query_rows, key_rows, clip_lengths, clip_shape, head_dim):
    queries = query_rows.reshape(clip_shape)
    key_parts = key_rows.reshape(clip_shape)
    scores = jnp.einsum(
        "gqhd,gkhd->ghqk", queries, key_parts, preferred_element_type=jnp.float32
    ) * head_dim ** (-0.5)
    valid_keys = jnp.arange(clip_shape[1])[None, :] < clip_lengths[:, None]
    return jnp.where(valid_keys[:, None, None, :], scores, -1e30)


def attend(query_rows, key_rows, value_rows, clip_lengths, clip_shape, head_dim):
    scores = clip_scores(query_rows, key_rows, clip_lengths, clip_shape, head_dim)
    row_top = jnp.max(scores, axis=-1, keepdims=True)
    exp_scores = jnp.exp(scores - row_top)
    row_total = jnp.sum(exp_scores, axis=-1, keepdims=True)
    weights = to_half(exp_scores / row_total)
    context = jnp.einsum(
        "ghqk,gkhd->gqhd",
        weights,
        value_rows.reshape(clip_shape),
        preferred_element_type=jnp.float32,
    )
    return (to_half(context.reshape(query_rows.shape)), row_top + jnp.log(row_total))


def attend_back(
    query_rows, key_rows, value_rows, clip_lengths, log_total, grad_context, clip_shape, head_dim
):
    scores = clip_scores(query_rows, key_rows, clip_lengths, clip_shape, head_dim)
    probabilities = jnp.exp(scores - log_total)
    weights = to_half(probabilities)
    grad_parts = grad_context.reshape(clip_shape)
    grad_weights = jnp.einsum(
        "gqhd,gkhd->ghqk",
        grad_parts,
        value_rows.reshape(clip_shape),
        preferred_element_type=jnp.float32,
    )
    grad_values = jnp.einsum(
        "ghqk,gqhd->gkhd", weights, grad_parts, preferred_element_type=jnp.float32
    )
    inner_sum = jnp.sum(grad_weights * probabilities, axis=-1, keepdims=True)
    grad_scores = to_half(probabilities * (grad_weights - inner_sum))
    grad_query = jnp.einsum(
        "ghqk,gkhd->gqhd",
        grad_scores,
        key_rows.reshape(clip_shape),
        preferred_element_type=jnp.float32,
    ) * head_dim ** (-0.5)
    grad_keys = jnp.einsum(
        "ghqk,gqhd->gkhd",
        grad_scores,
        query_rows.reshape(clip_shape),
        preferred_element_type=jnp.float32,
    ) * head_dim ** (-0.5)
    flat_shape = query_rows.shape
    return (
        to_half(grad_query.reshape(flat_shape)),
        to_half(grad_keys.reshape(flat_shape)),
        to_half(grad_values.reshape(flat_shape)),
    )


def token_sum(tensor):
    return jnp.sum(tensor.astype(jnp.float32), axis=0)


def local(
    inputs,
    lengths,
    cotangent,
    ln1_gain,
    ln1_bias,
    w_query,
    b_query,
    w_key,
    w_value,
    b_value,
    w_attn_out,
    b_attn_out,
    ln2_gain,
    ln2_bias,
    w_in,
    b_in,
    w_out,
    b_out,
):
    token_rows = unpack_rows(inputs)
    token_grads = unpack_rows(cotangent)
    row_count, part_width = token_rows.shape
    full_width = part_width * lax.axis_size("col")
    local_heads = HEADS // lax.axis_size("col")
    head_dim = part_width // local_heads
    clip_count = lengths.shape[0]
    slot_len = row_count // clip_count
    group_size = 1
    turn_count = clip_count // group_size
    clip_shape = (group_size, slot_len, local_heads, head_dim)
    unit_width = w_in.shape[1]
    gathered_query, gathered_key, gathered_value, gathered_in = (
        lax.all_gather(to_half(w_query), "row", axis=0, tiled=True),
        lax.all_gather(to_half(w_key), "row", axis=0, tiled=True),
        lax.all_gather(to_half(w_value), "row", axis=0, tiled=True),
        lax.all_gather(to_half(w_in), "row", axis=0, tiled=True),
    )
    gathered_attn, gathered_out = (
        lax.all_gather(to_half(w_attn_out), "row", axis=1, tiled=True),
        lax.all_gather(to_half(w_out), "row", axis=1, tiled=True),
    )

    def one_turn(totals, scan_item):
        clip_rows, grad_rows, clip_lengths = scan_item
        normal_one, scale_one, shifted_one = norm_forward(clip_rows, ln1_gain, ln1_bias, full_width)
        normed = gather_rows(to_half(shifted_one))
        query_rows = to_half(dot_plain(normed, gathered_query) + b_query)
        key_rows = to_half(dot_plain(normed, gathered_key))
        value_rows = to_half(dot_plain(normed, gathered_value) + b_value)
        context, log_total = attend(
            query_rows, key_rows, value_rows, clip_lengths, clip_shape, head_dim
        )
        attn_part = reduce_rows(dot_plain(context, gathered_attn))
        middle = clip_rows + attn_part + b_attn_out
        normal_two, scale_two, shifted_two = norm_forward(middle, ln2_gain, ln2_bias, full_width)
        normed_two = gather_rows(to_half(shifted_two))
        hidden = dot_plain(normed_two, gathered_in) + b_in
        active = to_half(jax.nn.gelu(hidden, approximate=False))
        output = middle + reduce_rows(dot_plain(active, gathered_out)) + b_out
        valid_rows = (jnp.arange(slot_len)[None, :] < clip_lengths[:, None]).reshape(-1)
        grad_low = jnp.where(valid_rows[:, None], grad_rows, jnp.zeros_like(grad_rows))
        grad_output = grad_low.astype(jnp.float32)
        grad_full = gather_rows(grad_low)
        grad_w_out = dot_left(active, grad_full)
        grad_active = dot_right(grad_full, gathered_out)
        gelu_value, gelu_pull = jax.vjp(
            lambda tensor: jax.nn.gelu(tensor, approximate=False), hidden
        )
        grad_hidden = to_half(gelu_pull(grad_active)[0])
        grad_w_in = dot_left(normed_two, grad_hidden)
        grad_normed_two = reduce_rows(dot_right(grad_hidden, gathered_in))
        grad_middle = grad_output + norm_backward(
            grad_normed_two, normal_two, scale_two, ln2_gain, full_width
        )
        grad_mid_full = gather_rows(to_half(grad_middle))
        grad_w_attn = dot_left(context, grad_mid_full)
        grad_context = to_half(dot_right(grad_mid_full, gathered_attn))
        grad_query, grad_keys, grad_values = attend_back(
            query_rows,
            key_rows,
            value_rows,
            clip_lengths,
            log_total,
            grad_context,
            clip_shape,
            head_dim,
        )
        grad_w_query = dot_left(normed, grad_query)
        grad_w_key = dot_left(normed, grad_keys)
        grad_w_value = dot_left(normed, grad_values)
        grad_normed = reduce_rows(
            dot_right(grad_query, gathered_query)
            + dot_right(grad_keys, gathered_key)
            + dot_right(grad_values, gathered_value)
        )
        grad_inputs = grad_middle + norm_backward(
            grad_normed, normal_one, scale_one, ln1_gain, full_width
        )
        additions = (
            grad_w_query,
            grad_w_key,
            grad_w_value,
            grad_w_in,
            grad_w_attn,
            grad_w_out,
            token_sum(grad_normed * normal_one),
            token_sum(grad_normed),
            token_sum(grad_query),
            token_sum(grad_values),
            token_sum(grad_middle),
            token_sum(grad_normed_two * normal_two),
            token_sum(grad_normed_two),
            token_sum(grad_hidden),
            token_sum(grad_output),
        )
        totals = jax.tree.map(lambda first, second: first + second, totals, additions)
        return (totals, (output, grad_inputs))

    start_totals = (
        jnp.zeros(gathered_query.shape, jnp.float32),
        jnp.zeros(gathered_key.shape, jnp.float32),
        jnp.zeros(gathered_value.shape, jnp.float32),
        jnp.zeros(gathered_in.shape, jnp.float32),
        jnp.zeros(gathered_attn.shape, jnp.float32),
        jnp.zeros(gathered_out.shape, jnp.float32),
        jnp.zeros((part_width,), jnp.float32),
        jnp.zeros((part_width,), jnp.float32),
        jnp.zeros((part_width,), jnp.float32),
        jnp.zeros((part_width,), jnp.float32),
        jnp.zeros((part_width,), jnp.float32),
        jnp.zeros((part_width,), jnp.float32),
        jnp.zeros((part_width,), jnp.float32),
        jnp.zeros((unit_width,), jnp.float32),
        jnp.zeros((part_width,), jnp.float32),
    )
    scan_inputs = (
        token_rows.reshape(turn_count, group_size * slot_len, part_width),
        token_grads.reshape(turn_count, group_size * slot_len, part_width),
        lengths.reshape(turn_count, group_size),
    )
    totals, (outputs, grad_inputs) = lax.scan(one_turn, start_totals, scan_inputs)
    (
        sum_query,
        sum_key,
        sum_value,
        sum_in,
        sum_attn,
        sum_out,
        sum_ln1_gain,
        sum_ln1_bias,
        sum_bquery,
        sum_bvalue,
        sum_battn,
        sum_ln2_gain,
        sum_ln2_bias,
        sum_bin,
        sum_bout,
    ) = totals
    grad_query_w, grad_key_w, grad_value_w, grad_in_w = (
        lax.psum_scatter(
            sum_query.astype(jnp.bfloat16), "row", scatter_dimension=0, tiled=True
        ).astype(jnp.float32),
        lax.psum_scatter(
            sum_key.astype(jnp.bfloat16), "row", scatter_dimension=0, tiled=True
        ).astype(jnp.float32),
        lax.psum_scatter(
            sum_value.astype(jnp.bfloat16), "row", scatter_dimension=0, tiled=True
        ).astype(jnp.float32),
        lax.psum_scatter(
            sum_in.astype(jnp.bfloat16), "row", scatter_dimension=0, tiled=True
        ).astype(jnp.float32),
    )
    grad_attn_w, grad_out_w = (
        lax.psum_scatter(
            sum_attn.astype(jnp.bfloat16), "row", scatter_dimension=1, tiled=True
        ).astype(jnp.float32),
        lax.psum_scatter(
            sum_out.astype(jnp.bfloat16), "row", scatter_dimension=1, tiled=True
        ).astype(jnp.float32),
    )
    (
        vec_ln1_gain,
        vec_ln1_bias,
        vec_bquery,
        vec_bvalue,
        vec_battn,
        vec_ln2_gain,
        vec_ln2_bias,
        vec_bin,
        vec_bout,
    ) = lax.psum(
        (
            sum_ln1_gain,
            sum_ln1_bias,
            sum_bquery,
            sum_bvalue,
            sum_battn,
            sum_ln2_gain,
            sum_ln2_bias,
            sum_bin,
            sum_bout,
        ),
        "row",
    )
    return (
        pack_rows(outputs.reshape(row_count, part_width)),
        pack_rows(grad_inputs.reshape(row_count, part_width)),
        vec_ln1_gain,
        vec_ln1_bias,
        grad_query_w,
        vec_bquery,
        grad_key_w,
        grad_value_w,
        vec_bvalue,
        grad_attn_w,
        vec_battn,
        vec_ln2_gain,
        vec_ln2_bias,
        grad_in_w,
        vec_bin,
        grad_out_w,
        vec_bout,
    )


def solution(mesh):
    placed = (
        P("row", "col"),
        P("row"),
        P("row", "col"),
        P("col"),
        P("col"),
        P("row", "col"),
        P("col"),
        P("row", "col"),
        P("row", "col"),
        P("col"),
        P("col", "row"),
        P("col"),
        P("col"),
        P("col"),
        P("row", "col"),
        P("col"),
        P("col", "row"),
        P("col"),
    )
    return jax.shard_map(
        local,
        mesh=mesh,
        in_specs=placed,
        out_specs=(
            P("row", "col"),
            P("row", "col"),
            P("col"),
            P("col"),
            P("row", "col"),
            P("col"),
            P("row", "col"),
            P("row", "col"),
            P("col"),
            P("col", "row"),
            P("col"),
            P("col"),
            P("col"),
            P("row", "col"),
            P("col"),
            P("col", "row"),
            P("col"),
        ),
        check_vma=False,
    )
```

profile of v0, /device:TPU:0, one launch (start us, length us, event | category | flops | bytes accessed | tf_op | source)
XLA Modules:
  0.0 2354.0 jit_solution(7686544868051592714)
XLA Ops:
  70.9 2112.6 %while.43 = (s32[]{:T(128)}, f32[1280,160]{0,1:T(8,128)}, f32[1280,160]{0,1:T(8,128)}, f32[1280,160]{0,1:T(8,128)}, f32[1280,640]{1,0:T(8,128)}, /*index=5*/f32[...) while((s32[]{:T(128)}, f32[1280,160]{0,1:T(8,128)}, ...), condition=%wide.region_33.34_spmd.clone, body=%wide.region_0.33_spmd.clone.sunk | while | flops 26616791040 | bytes 708490176 | solution.py:289
  71.2 37.9 %all-reduce.9 = (f32[1500]{0:T(1024)S(1)}, f32[1500]{0:T(1024)S(1)}) all-reduce(f32[1500]{0:T(1024)S(1)} %fusion.181, f32[1500]{0:T(1024)S(1)} %dynamic-slice_reduce_fusion.2), channel_id=1, replica_groups=mesh['row'=4,'col'=8] {'col'}, use_global_device_ids=true, to_apply=%region_4.4 | all-reduce | flops 3000 | bytes 24000 | tf_op jit(solution)/shard_map/while/body/eval_jaxpr/psum | solution.py:52
  113.4 65.8 %all-gather.15.cloned.1.call-done = bf16[1500,1280]{0,1:T(8,128)(2,1)} async-done(((bf16[1500,160]{0,1:T(8,128)(2,1)}), bf16[1500,1280]{0,1:T(8,128)(2,1)}) %all-gather.15.cloned.1.call-update) | async-done | bytes 3840016 | tf_op jit(solution)/shard_map/while/body/eval_jaxpr/all_gather | solution.py:56
  218.4 138.4 %reduce-scatter.31.cloned.1.call-done = f32[1500,160]{0,1:T(8,128)} async-done(((f32[1500,1280]{0,1:T(8,128)}), f32[1500,160]{0,1:T(8,128)}) %reduce-scatter.31.cloned.1.call-update) | async-done | bytes 960016 | tf_op jit(solution)/shard_map/while/body/eval_jaxpr/reduce_scatter | solution.py:60
  358.3 35.2 %all-reduce.10 = (f32[1500]{0:T(1024)S(1)}, f32[1500]{0:T(1024)S(1)}) all-reduce(f32[1500]{0:T(1024)S(1)} %get-tuple-element.899, f32[1500]{0:T(1024)S(1)} %get-tuple-element.900), channel_id=1, replica_groups=mesh['row'=4,'col'=8] {'col'}, use_global_device_ids=true, to_apply=%region_11.11 | all-reduce | flops 3000 | bytes 24000 | tf_op jit(solution)/shard_map/while/body/eval_jaxpr/psum | solution.py:52
  398.3 64.5 %all-gather.17.cloned.1.call-done = bf16[1500,1280]{0,1:T(8,128)(2,1)} async-done(((bf16[1500,160]{0,1:T(8,128)(2,1)}), bf16[1500,1280]{0,1:T(8,128)(2,1)}) %all-gather.17.cloned.1.call-update) | async-done | bytes 3840016 | tf_op jit(solution)/shard_map/while/body/eval_jaxpr/all_gather | solution.py:56
  470.6 63.3 %all-gather.19.cloned.1.call-done = bf16[1500,1280]{0,1:T(8,128)(2,1)} async-done(((bf16[1500,160]{0,1:T(8,128)(2,1)}), bf16[1500,1280]{0,1:T(8,128)(2,1)}) %all-gather.19.cloned.1.call-update) | async-done | bytes 3840016 | tf_op jit(solution)/shard_map/while/body/eval_jaxpr/all_gather | solution.py:56
  533.9 15.7 convert_reduce_fusion.9
  556.3 138.4 %reduce-scatter.33.cloned.1.call-done = f32[1500,160]{0,1:T(8,128)} async-done(((f32[1500,1280]{0,1:T(8,128)}), f32[1500,160]{0,1:T(8,128)}) %reduce-scatter.33.cloned.1.call-update) | async-done | bytes 960016 | tf_op jit(solution)/shard_map/while/body/eval_jaxpr/reduce_scatter | solution.py:60
  696.9 35.2 %all-reduce.11 = (f32[1500]{0:T(1024)S(1)}, f32[1500]{0:T(1024)S(1)}) all-reduce(f32[1500]{0:T(1024)S(1)} %get-tuple-element.907, f32[1500]{0:T(1024)S(1)} %get-tuple-element.908), channel_id=1, replica_groups=mesh['row'=4,'col'=8] {'col'}, use_global_device_ids=true, to_apply=%region_16.16 | all-reduce | flops 3000 | bytes 24000 | tf_op jit(solution)/shard_map/while/body/eval_jaxpr/psum | solution.py:52
  746.4 56.8 %all-gather.21.cloned.1.call-done = bf16[1500,1280]{0,1:T(8,128)(2,1)} async-done(((bf16[1500,160]{0,1:T(8,128)(2,1)}), bf16[1500,1280]{0,1:T(8,128)(2,1)}) %all-gather.21.cloned.1.call-update) | async-done | bytes 3840016 | tf_op jit(solution)/shard_map/while/body/eval_jaxpr/all_gather | solution.py:56
  871.4 73.8 %reduce-scatter.37.cloned.1.call-done = f32[1500,160]{0,1:T(8,128)} async-done(((f32[1500,1280]{0,1:T(8,128)}), f32[1500,160]{0,1:T(8,128)}) %reduce-scatter.37.cloned.1.call-update) | async-done | bytes 960016 | tf_op jit(solution)/shard_map/while/body/eval_jaxpr/reduce_scatter | solution.py:60
  959.7 128.0 %reduce-scatter.35.cloned.1.call-done = f32[1500,160]{0,1:T(8,128)} async-done(((f32[1500,1280]{0,1:T(8,128)}), f32[1500,160]{0,1:T(8,128)}) %reduce-scatter.35.cloned.1.call-update) | async-done | bytes 960016 | tf_op jit(solution)/shard_map/while/body/eval_jaxpr/reduce_scatter | solution.py:60
  1089.4 35.2 %all-reduce.12 = (f32[1500]{0:T(1024)S(1)}, f32[1500]{0:T(1024)S(1)}) all-reduce(f32[1500]{0:T(1024)S(1)} %get-tuple-element.932, f32[1500]{0:T(1024)S(1)} %get-tuple-element.933), channel_id=1, replica_groups=mesh['row'=4,'col'=8] {'col'}, use_global_device_ids=true, to_apply=%region_32.32 | all-reduce | flops 3000 | bytes 24000 | tf_op jit(solution)/shard_map/while/body/eval_jaxpr/psum | solution.py:52
  1127.8 33.0 %all-reduce.9 = (f32[1500]{0:T(1024)S(1)}, f32[1500]{0:T(1024)S(1)}) all-reduce(f32[1500]{0:T(1024)S(1)} %fusion.181, f32[1500]{0:T(1024)S(1)} %dynamic-slice_reduce_fusion.2), channel_id=1, replica_groups=mesh['row'=4,'col'=8] {'col'}, use_global_device_ids=true, to_apply=%region_4.4 | all-reduce | flops 3000 | bytes 24000 | tf_op jit(solution)/shard_map/while/body/eval_jaxpr/psum | solution.py:52
  1165.1 65.6 %all-gather.15.cloned.1.call-done = bf16[1500,1280]{0,1:T(8,128)(2,1)} async-done(((bf16[1500,160]{0,1:T(8,128)(2,1)}), bf16[1500,1280]{0,1:T(8,128)(2,1)}) %all-gather.15.cloned.1.call-update) | async-done | bytes 3840016 | tf_op jit(solution)/shard_map/while/body/eval_jaxpr/all_gather | solution.py:56
  1269.9 138.4 %reduce-scatter.31.cloned.1.call-done = f32[1500,160]{0,1:T(8,128)} async-done(((f32[1500,1280]{0,1:T(8,128)}), f32[1500,160]{0,1:T(8,128)}) %reduce-scatter.31.cloned.1.call-update) | async-done | bytes 960016 | tf_op jit(solution)/shard_map/while/body/eval_jaxpr/reduce_scatter | solution.py:60
  1409.9 35.2 %all-reduce.10 = (f32[1500]{0:T(1024)S(1)}, f32[1500]{0:T(1024)S(1)}) all-reduce(f32[1500]{0:T(1024)S(1)} %get-tuple-element.899, f32[1500]{0:T(1024)S(1)} %get-tuple-element.900), channel_id=1, replica_groups=mesh['row'=4,'col'=8] {'col'}, use_global_device_ids=true, to_apply=%region_11.11 | all-reduce | flops 3000 | bytes 24000 | tf_op jit(solution)/shard_map/while/body/eval_jaxpr/psum | solution.py:52
  1449.6 64.7 %all-gather.17.cloned.1.call-done = bf16[1500,1280]{0,1:T(8,128)(2,1)} async-done(((bf16[1500,160]{0,1:T(8,128)(2,1)}), bf16[1500,1280]{0,1:T(8,128)(2,1)}) %all-gather.17.cloned.1.call-update) | async-done | bytes 3840016 | tf_op jit(solution)/shard_map/while/body/eval_jaxpr/all_gather | solution.py:56
  1522.1 63.3 %all-gather.19.cloned.1.call-done = bf16[1500,1280]{0,1:T(8,128)(2,1)} async-done(((bf16[1500,160]{0,1:T(8,128)(2,1)}), bf16[1500,1280]{0,1:T(8,128)(2,1)}) %all-gather.19.cloned.1.call-update) | async-done | bytes 3840016 | tf_op jit(solution)/shard_map/while/body/eval_jaxpr/all_gather | solution.py:56
  1585.4 15.7 convert_reduce_fusion.9
  1607.9 138.4 %reduce-scatter.33.cloned.1.call-done = f32[1500,160]{0,1:T(8,128)} async-done(((f32[1500,1280]{0,1:T(8,128)}), f32[1500,160]{0,1:T(8,128)}) %reduce-scatter.33.cloned.1.call-update) | async-done | bytes 960016 | tf_op jit(solution)/shard_map/while/body/eval_jaxpr/reduce_scatter | solution.py:60
  1748.5 35.2 %all-reduce.11 = (f32[1500]{0:T(1024)S(1)}, f32[1500]{0:T(1024)S(1)}) all-reduce(f32[1500]{0:T(1024)S(1)} %get-tuple-element.907, f32[1500]{0:T(1024)S(1)} %get-tuple-element.908), channel_id=1, replica_groups=mesh['row'=4,'col'=8] {'col'}, use_global_device_ids=true, to_apply=%region_16.16 | all-reduce | flops 3000 | bytes 24000 | tf_op jit(solution)/shard_map/while/body/eval_jaxpr/psum | solution.py:52
  1797.9 56.8 %all-gather.21.cloned.1.call-done = bf16[1500,1280]{0,1:T(8,128)(2,1)} async-done(((bf16[1500,160]{0,1:T(8,128)(2,1)}), bf16[1500,1280]{0,1:T(8,128)(2,1)}) %all-gather.21.cloned.1.call-update) | async-done | bytes 3840016 | tf_op jit(solution)/shard_map/while/body/eval_jaxpr/all_gather | solution.py:56
  1869.9 13.3 multiply_convert_fusion.4
  1924.4 72.2 %reduce-scatter.37.cloned.1.call-done = f32[1500,160]{0,1:T(8,128)} async-done(((f32[1500,1280]{0,1:T(8,128)}), f32[1500,160]{0,1:T(8,128)}) %reduce-scatter.37.cloned.1.call-update) | async-done | bytes 960016 | tf_op jit(solution)/shard_map/while/body/eval_jaxpr/reduce_scatter | solution.py:60
  2012.6 126.5 %reduce-scatter.35.cloned.1.call-done = f32[1500,160]{0,1:T(8,128)} async-done(((f32[1500,1280]{0,1:T(8,128)}), f32[1500,160]{0,1:T(8,128)}) %reduce-scatter.35.cloned.1.call-update) | async-done | bytes 960016 | tf_op jit(solution)/shard_map/while/body/eval_jaxpr/reduce_scatter | solution.py:60
  2140.8 35.2 %all-reduce.12 = (f32[1500]{0:T(1024)S(1)}, f32[1500]{0:T(1024)S(1)}) all-reduce(f32[1500]{0:T(1024)S(1)} %get-tuple-element.932, f32[1500]{0:T(1024)S(1)} %get-tuple-element.933), channel_id=1, replica_groups=mesh['row'=4,'col'=8] {'col'}, use_global_device_ids=true, to_apply=%region_32.32 | all-reduce | flops 3000 | bytes 24000 | tf_op jit(solution)/shard_map/while/body/eval_jaxpr/psum | solution.py:52
  2234.4 23.2 reduce-scatter.27.cloned.1.call-done
  2259.4 23.2 reduce-scatter.29.cloned.1.call-done
  2284.4 29.4 %reduce-scatter.19.cloned.1.call-done = bf16[320,640]{1,0:T(8,128)(2,1)} async-done(((bf16[1280,640]{1,0:T(8,128)(2,1)}), bf16[320,640]{1,0:T(8,128)(2,1)}) %reduce-scatter.19.cloned.1.call-update) | async-done | bytes 409616 | tf_op jit(solution)/shard_map/reduce_scatter | solution.py:317
  2315.7 29.2 %reduce-scatter.21.cloned.1.call-done = bf16[640,320]{0,1:T(8,128)(2,1)} async-done(((bf16[640,1280]{0,1:T(8,128)(2,1)}), bf16[640,320]{0,1:T(8,128)(2,1)}) %reduce-scatter.21.cloned.1.call-update) | async-done | bytes 409616 | tf_op jit(solution)/shard_map/reduce_scatter | solution.py:325
  (499 shorter events, 445.4 us)
Async XLA Ops:
  7.2 60.2 %all-gather.13.cloned.1.call-start = ((), (), s32[]{:S(2)}) async-start(), calls=%async_computation.11 | async-start | bytes 2048000 | tf_op jit(solution)/shard_map/all_gather | solution.py:188
  9.3 61.6 %all-gather.11.cloned.1.call-start = ((), (), s32[]{:S(2)}) async-start(), calls=%async_computation.10 | async-start | bytes 2048000 | tf_op jit(solution)/shard_map/all_gather | solution.py:184
  71.0 285.9 %copy-start.4 = (f32[2,1500,160]{1,2,0:T(8,128)}, f32[2,1500,160]{1,2,0:T(8,128)S(1)}, u32[]{:S(2)}) copy-start(f32[2,1500,160]{1,2,0:T(8,128)S(1)} %get-tuple-element.1032) | copy-start | bytes 5760004 | tf_op jit(solution)/shard_map/while
  71.0 732.2 %copy-start.25 = (bf16[160,1280]{1,0:T(8,128)(2,1)}, bf16[160,1280]{1,0:T(8,128)(2,1)S(1)}, u32[]{:S(2)}) copy-start(bf16[160,1280]{1,0:T(8,128)(2,1)S(1)} %get-tuple-element.1042) | copy-start | bytes 1228804 | tf_op jit(solution)/shard_map/while
  71.0 108.3 %all-gather.15.cloned.1.call-start = ((), (), s32[]{:S(2)}) async-start(), calls=%async_computation.18 | async-start | bytes 4423680 | tf_op jit(solution)/shard_map/while/body/eval_jaxpr/all_gather | solution.py:56
  111.5 245.3 %reduce-scatter.31.cloned.1.call-start = ((), (), s32[]{:S(2)}) async-start(), calls=%async_computation.19 | async-start | bytes 8847360 | tf_op jit(solution)/shard_map/while/body/eval_jaxpr/reduce_scatter | solution.py:60
  218.4 244.4 %all-gather.17.cloned.1.call-start = ((), (), s32[]{:S(2)}) async-start(), calls=%async_computation.20 | async-start | bytes 4423680 | tf_op jit(solution)/shard_map/while/body/eval_jaxpr/all_gather | solution.py:56
  358.3 373.8 %copy-start.2 = (f32[1500,160]{0,1:T(8,128)}, f32[1500,160]{0,1:T(8,128)S(1)}, u32[]{:S(2)}) copy-start(f32[1500,160]{0,1:T(8,128)S(1)} %get-tuple-element.898) | copy-start | bytes 2880004 | tf_op jit(solution)/shard_map/while
  395.3 138.6 %all-gather.19.cloned.1.call-start = ((), (), s32[]{:S(2)}) async-start(), calls=%async_computation.21 | async-start | bytes 4423680 | tf_op jit(solution)/shard_map/while/body/eval_jaxpr/all_gather | solution.py:56
  397.8 296.9 %reduce-scatter.33.cloned.1.call-start = ((), (), s32[]{:S(2)}) async-start(), calls=%async_computation.22 | async-start | bytes 8847360 | tf_op jit(solution)/shard_map/while/body/eval_jaxpr/reduce_scatter | solution.py:60
  556.2 175.9 %copy-start.11 = (bf16[1500,160]{0,1:T(8,128)(2,1)S(1)}, bf16[1500,160]{0,1:T(8,128)(2,1)}, u32[]{:S(2)}) copy-start(bf16[1500,160]{0,1:T(8,128)(2,1)} %get-tuple-element.905) | copy-start | bytes 1440004 | tf_op jit(solution)/shard_map/while
  556.3 246.9 %all-gather.21.cloned.1.call-start = ((), (), s32[]{:S(2)}) async-start(), calls=%async_computation.23 | async-start | bytes 4423680 | tf_op jit(solution)/shard_map/while/body/eval_jaxpr/all_gather | solution.py:56
  735.6 209.5 %reduce-scatter.37.cloned.1.call-start = ((), (), s32[]{:S(2)}) async-start(), calls=%async_computation.25 | async-start | bytes 8847360 | tf_op jit(solution)/shard_map/while/body/eval_jaxpr/reduce_scatter | solution.py:60
  746.3 341.5 %reduce-scatter.35.cloned.1.call-start = ((), (), s32[]{:S(2)}) async-start(), calls=%async_computation.24 | async-start | bytes 8847360 | tf_op jit(solution)/shard_map/while/body/eval_jaxpr/reduce_scatter | solution.py:60
  1127.6 280.8 %copy-start.4 = (f32[2,1500,160]{1,2,0:T(8,128)}, f32[2,1500,160]{1,2,0:T(8,128)S(1)}, u32[]{:S(2)}) copy-start(f32[2,1500,160]{1,2,0:T(8,128)S(1)} %get-tuple-element.1032) | copy-start | bytes 5760004 | tf_op jit(solution)/shard_map/while
  1127.6 727.1 %copy-start.25 = (bf16[160,1280]{1,0:T(8,128)(2,1)}, bf16[160,1280]{1,0:T(8,128)(2,1)S(1)}, u32[]{:S(2)}) copy-start(bf16[160,1280]{1,0:T(8,128)(2,1)S(1)} %get-tuple-element.1042) | copy-start | bytes 1228804 | tf_op jit(solution)/shard_map/while
  1127.6 103.1 %all-gather.15.cloned.1.call-start = ((), (), s32[]{:S(2)}) async-start(), calls=%async_computation.18 | async-start | bytes 4423680 | tf_op jit(solution)/shard_map/while/body/eval_jaxpr/all_gather | solution.py:56
  1163.2 245.2 %reduce-scatter.31.cloned.1.call-start = ((), (), s32[]{:S(2)}) async-start(), calls=%async_computation.19 | async-start | bytes 8847360 | tf_op jit(solution)/shard_map/while/body/eval_jaxpr/reduce_scatter | solution.py:60
  1269.9 244.4 %all-gather.17.cloned.1.call-start = ((), (), s32[]{:S(2)}) async-start(), calls=%async_computation.20 | async-start | bytes 4423680 | tf_op jit(solution)/shard_map/while/body/eval_jaxpr/all_gather | solution.py:56
  1409.8 373.8 %copy-start.2 = (f32[1500,160]{0,1:T(8,128)}, f32[1500,160]{0,1:T(8,128)S(1)}, u32[]{:S(2)}) copy-start(f32[1500,160]{0,1:T(8,128)S(1)} %get-tuple-element.898) | copy-start | bytes 2880004 | tf_op jit(solution)/shard_map/while
  1446.8 138.6 %all-gather.19.cloned.1.call-start = ((), (), s32[]{:S(2)}) async-start(), calls=%async_computation.21 | async-start | bytes 4423680 | tf_op jit(solution)/shard_map/while/body/eval_jaxpr/all_gather | solution.py:56
  1449.4 296.9 %reduce-scatter.33.cloned.1.call-start = ((), (), s32[]{:S(2)}) async-start(), calls=%async_computation.22 | async-start | bytes 8847360 | tf_op jit(solution)/shard_map/while/body/eval_jaxpr/reduce_scatter | solution.py:60
  1607.8 175.9 %copy-start.11 = (bf16[1500,160]{0,1:T(8,128)(2,1)S(1)}, bf16[1500,160]{0,1:T(8,128)(2,1)}, u32[]{:S(2)}) copy-start(bf16[1500,160]{0,1:T(8,128)(2,1)} %get-tuple-element.905) | copy-start | bytes 1440004 | tf_op jit(solution)/shard_map/while
  1607.8 246.9 %all-gather.21.cloned.1.call-start = ((), (), s32[]{:S(2)}) async-start(), calls=%async_computation.23 | async-start | bytes 4423680 | tf_op jit(solution)/shard_map/while/body/eval_jaxpr/all_gather | solution.py:56
  1787.2 209.4 %reduce-scatter.37.cloned.1.call-start = ((), (), s32[]{:S(2)}) async-start(), calls=%async_computation.25 | async-start | bytes 8847360 | tf_op jit(solution)/shard_map/while/body/eval_jaxpr/reduce_scatter | solution.py:60
  1797.8 341.3 %reduce-scatter.35.cloned.1.call-start = ((), (), s32[]{:S(2)}) async-start(), calls=%async_computation.24 | async-start | bytes 8847360 | tf_op jit(solution)/shard_map/while/body/eval_jaxpr/reduce_scatter | solution.py:60
  2183.5 41.4 %reduce-scatter.23.cloned.1.call-start = ((), (), s32[]{:S(2)}) async-start(), calls=%async_computation.14 | async-start | bytes 819200
  2186.0 46.7 %reduce-scatter.25.cloned.1.call-start = ((), (), s32[]{:S(2)}) async-start(), calls=%async_computation.15 | async-start | bytes 819200
  2188.3 69.3 %reduce-scatter.27.cloned.1.call-start = ((), (), s32[]{:S(2)}) async-start(), calls=%async_computation.16 | async-start | bytes 819200
  2189.5 93.1 %reduce-scatter.29.cloned.1.call-start = ((), (), s32[]{:S(2)}) async-start(), calls=%async_computation.17 | async-start | bytes 819200
  2190.8 123.0 %reduce-scatter.19.cloned.1.call-start = ((), (), s32[]{:S(2)}) async-start(), calls=%async_computation.12 | async-start | bytes 2048000 | tf_op jit(solution)/shard_map/reduce_scatter | solution.py:317
  2194.4 150.5 %reduce-scatter.21.cloned.1.call-start = ((), (), s32[]{:S(2)}) async-start(), calls=%async_computation.13 | async-start | bytes 2048000 | tf_op jit(solution)/shard_map/reduce_scatter | solution.py:325
  (127 other events, 4068.2 us)
Sparse Core Ops, SparseCore 0:
  9.6 25.3 all-gather.12
  37.1 20.5 all-gather.10
  111.6 67.5 all-gather.14
  218.5 138.2 reduce-scatter.30
  395.4 67.3 all-gather.16
  465.4 68.4 all-gather.18
  556.4 138.3 reduce-scatter.32
  735.8 67.3 all-gather.20
  806.8 138.3 reduce-scatter.36
  948.6 139.0 reduce-scatter.34
  1163.3 67.3 all-gather.14
  1270.0 138.3 reduce-scatter.30
  1446.9 67.3 all-gather.16
  1516.9 68.4 all-gather.18
  1607.9 138.3 reduce-scatter.32
  1787.3 67.3 all-gather.20
  1858.2 138.3 reduce-scatter.36
  2000.0 139.0 reduce-scatter.34
  2187.5 19.6 reduce-scatter.22
  2210.1 22.4 reduce-scatter.24
  2235.1 22.4 reduce-scatter.26
  2260.1 22.4 reduce-scatter.28
  2285.1 28.5 reduce-scatter.18
  2316.3 28.5 reduce-scatter.20
where the time goes:
time: 2360 us; the launch traced here: 2350 us
  waiting for transfers between devices  1570 us (67%)
  blocking collectives  326 us (14%)
  matrix products  255 us (11%)
  other arithmetic  109 us (5%)
  local copies, waits for them, and re-layouts  74.5 us (3%)
    reduce_scatter x8, waiting for transfers between devices, reduce_rows(): return lax.psum_scatter(tensor, 'col', scatter_dimension=1, tiled=True)  954 us
    all_gather x8, waiting for transfers between devices, gather_rows(): return lax.all_gather(tensor, 'col', axis=1, tiled=True)  501 us
    psum x8, blocking collectives, row_sums(): return lax.psum((jnp.sum(first, axis=1), jnp.sum(second, axis=1)), 'col')  282 us
    dot_general x12, matrix products, dot_right(): lax.dot_general(first, second, (((1,), (1,)), ((), ())), preferred_elemen...  68.5 us
    unnamed x12, waiting for transfers between devices  52.5 us
    dot_general x12, matrix products, dot_plain(): return jnp.dot(first, second, preferred_element_type=jnp.float32)  52.3 us
  transfers between devices with their start and end apart: 24, of which 21 were waited for; matrix products, arithmetic and copies ran while one was open for 11% of the time, Pallas kernels for 0%

commit v1 on v0

v1 whole, which is shorter than its diff:
```python
import functools

import jax
import jax.numpy as jnp
from jax import lax
from jax.experimental import pallas as pl
from jax.experimental.pallas import tpu as pltpu
from jax.sharding import Mesh
from jax.sharding import PartitionSpec as P

HEADS = 16
EPSILON = 1e-05
PAD = 128
LOG2E = 1.4426950408889634
LN2 = 0.6931471805599453
MASKED = -1e30
BF = jnp.bfloat16
F32 = jnp.float32


def dot(first, second, left, right):
    return lax.dot_general(
        first, second, (((left,), (right,)), ((), ())), preferred_element_type=F32
    )


def swap(tensor, axis, step=1):
    size = lax.axis_size(axis)
    return lax.ppermute(tensor, axis, [(i, i ^ step) for i in range(size)])


def pieces_of(tensor, axis):
    return [tensor] + [swap(tensor, axis, d) for d in range(1, lax.axis_size(axis))]


def in_order(pieces, axis):
    mine = lax.axis_index(axis)
    if len(pieces) == 2:
        return [lax.select_n((mine ^ j) == 1, *pieces) for j in range(2)]
    return [lax.select_n(mine ^ j, *pieces) for j in range(len(pieces))]


def pick(tensor, index, axis):
    return lax.dynamic_index_in_dim(tensor, index, axis, keepdims=False)


def gather_group(part):
    rows = []
    for own in pieces_of(part, "y"):
        rows.append(jnp.concatenate([own, swap(own, "k")], axis=0))
    return rows


def reduce_group(partials):
    quarter = partials[0].shape[0] // 2
    sums = [None] * len(partials)
    for d in reversed(range(len(partials))):
        part = partials[d]
        sums[d] = part[:quarter] + swap(part[quarter:].astype(BF), "k").astype(F32)
    total = sums[0]
    for d in range(1, len(partials)):
        total = total + swap(sums[d].astype(BF), "y", d).astype(F32)
    return total


def forward_body(query_ref, key_ref, value_ref, context_ref, weights_ref):
    scores = dot(key_ref[...], query_ref[...], 1, 1)
    top = jnp.max(scores, axis=0, keepdims=True)
    powers = jnp.exp2(scores - top)
    total = jnp.sum(powers, axis=0, keepdims=True)
    weights = (powers * (1.0 / total)).astype(BF)
    weights_ref[0] = weights
    context_ref[...] = dot(value_ref[...], weights, 0, 0).T.astype(BF)


def attend(packed, heads, block):
    slots = packed.shape[0]
    return pl.pallas_call(
        forward_body,
        grid=(heads, slots // block),
        in_specs=[
            pl.BlockSpec((block, PAD), lambda h, i: (i, h)),
            pl.BlockSpec((slots, PAD), lambda h, i: (0, heads + h)),
            pl.BlockSpec((slots, PAD), lambda h, i: (0, 2 * heads + h)),
        ],
        out_specs=[
            pl.BlockSpec((block, PAD), lambda h, i: (i, h)),
            pl.BlockSpec((1, slots, block), lambda h, i: (h, 0, i)),
        ],
        out_shape=[
            jax.ShapeDtypeStruct((slots, heads * PAD), BF),
            jax.ShapeDtypeStruct((heads, slots, slots), BF),
        ],
        compiler_params=pltpu.CompilerParams(vmem_limit_bytes=50 * 2**20),
        cost_estimate=pl.CostEstimate(
            flops=heads * slots * slots * PAD * 12,
            bytes_accessed=heads * slots * slots * 2,
            transcendentals=heads * slots * slots,
        ),
    )(packed, packed, packed)


def backward_body(
    head_dim,
    steps,
    query_ref,
    key_ref,
    value_ref,
    grad_ref,
    context_ref,
    weights_ref,
    out_ref,
    key_total,
    value_total,
):
    step = pl.program_id(1)
    block = query_ref.shape[0]
    grad = grad_ref[...]
    wide = grad.astype(F32)
    inner = jnp.sum(wide * context_ref[...].astype(F32), axis=1, keepdims=True)
    inner_high = inner.astype(BF).astype(F32)
    lane = lax.broadcasted_iota(jnp.int32, grad.shape, 1)
    extended = jnp.where(
        lane == head_dim,
        inner_high,
        jnp.where(lane == head_dim + 1, inner - inner_high, wide),
    ).astype(BF)
    centered = dot(value_ref[...], extended, 1, 1)
    weights = weights_ref[0]
    grad_scores = (weights.astype(F32) * centered).astype(BF)
    grad_value = dot(weights, grad, 1, 0)
    grad_key = dot(grad_scores, query_ref[...], 1, 0)
    grad_query = (dot(key_ref[...], grad_scores, 0, 0) * head_dim**-0.5).T
    out_ref[0, pl.ds(pl.multiple_of(step * block, block), block), :] = grad_query.astype(BF)

    @pl.when(step == 0)
    def _():
        key_total[...] = grad_key
        value_total[...] = grad_value

    @pl.when(step > 0)
    def _():
        key_total[...] += grad_key
        value_total[...] += grad_value

    @pl.when(step == steps - 1)
    def _():
        out_ref[1] = (key_total[...] * LN2).astype(BF)
        out_ref[2] = value_total[...].astype(BF)


def attend_back(packed, grad_context, context, weights, heads, head_dim, block):
    slots = packed.shape[0]
    steps = slots // block
    rows = pl.BlockSpec((block, PAD), lambda h, i: (i, h))
    return pl.pallas_call(
        functools.partial(backward_body, head_dim, steps),
        grid=(heads, steps),
        in_specs=[
            rows,
            pl.BlockSpec((slots, PAD), lambda h, i: (0, heads + h)),
            pl.BlockSpec((slots, PAD), lambda h, i: (0, 2 * heads + h)),
            rows,
            rows,
            pl.BlockSpec((1, slots, block), lambda h, i: (h, 0, i)),
        ],
        out_specs=pl.BlockSpec((3, slots, PAD), lambda h, i: (0, 0, h)),
        out_shape=jax.ShapeDtypeStruct((3, slots, heads * PAD), BF),
        scratch_shapes=[pltpu.VMEM((slots, PAD), F32)] * 2,
        compiler_params=pltpu.CompilerParams(vmem_limit_bytes=50 * 2**20),
        cost_estimate=pl.CostEstimate(
            flops=heads * slots * slots * PAD * 16,
            bytes_accessed=heads * slots * slots * 2,
            transcendentals=0,
        ),
    )(packed, packed, packed, grad_context, context, weights)


def norm_forward(tensor, gain, shift):
    centered = tensor - jnp.mean(tensor, axis=1, keepdims=True)
    scale = lax.rsqrt(jnp.mean(centered * centered, axis=1, keepdims=True) + EPSILON)
    normal = centered * scale
    return normal, scale, (normal * gain + shift).astype(BF)


def norm_backward(grad, normal, scale, gain):
    weighted = grad * gain
    return scale * (
        weighted
        - jnp.mean(weighted, axis=1, keepdims=True)
        - normal * jnp.mean(weighted * normal, axis=1, keepdims=True)
    )


def local(
    inputs,
    lengths,
    cotangent,
    ln1_gain,
    ln1_bias,
    w_query,
    b_query,
    w_key,
    w_value,
    b_value,
    w_attn_out,
    b_attn_out,
    ln2_gain,
    ln2_bias,
    w_in,
    b_in,
    w_out,
    b_out,
):
    x_size, z_size, y_size = (lax.axis_size(a) for a in ("x", "z", "y"))
    x, k, z, y = (lax.axis_index(a) for a in ("x", "k", "z", "y"))
    pack_count, packed_width = inputs.shape
    features = packed_width // 8
    columns = z_size * y_size
    width = features * columns
    clips = lengths.shape[0]
    slot = pack_count * 8 // clips
    group = 2 * y_size
    quarter = -(-slot // (128 * group)) * 128 if group <= 4 else -(-slot // (16 * group)) * 16
    while (quarter * group) % 128:
        quarter += 16
    slots = quarter * group
    rows = w_query.shape[0]
    block_heads = HEADS // columns
    head_dim = width // HEADS
    split = block_heads % 2 == 0
    part_heads = block_heads // 2 if split else block_heads
    heads = z_size * block_heads // 2
    units = w_in.shape[1]
    half_units = units // 2

    def to_tokens(tensor):
        tokens = (
            tensor.astype(BF)
            .reshape(pack_count, features, 8)
            .transpose(0, 2, 1)
            .reshape(clips, slot, features)
        )
        tokens = jnp.pad(tokens, ((0, 0), (0, slots - slot), (0, 0)))
        tokens = tokens.reshape(clips, y_size, 2, quarter, features)
        kept = pick(tokens, k, 2)
        other = swap(pick(tokens, 1 - k, 2), "k")
        ordered = jnp.concatenate(in_order([kept, other], "k"), axis=0)
        ordered = ordered.reshape(columns, quarter, features)
        moved = lax.all_to_all(ordered, ("z", "y"), 0, 0)
        return moved.transpose(1, 0, 2).reshape(quarter, width)

    def from_tokens(tensor):
        blocks = tensor.astype(BF).reshape(quarter, columns, features).transpose(1, 0, 2)
        moved = lax.all_to_all(blocks, ("z", "y"), 0, 0)
        moved = moved.reshape(2, clips, y_size, quarter, features)
        kept = pick(moved, k, 0)
        other = swap(pick(moved, 1 - k, 0), "k")
        ordered = jnp.stack(in_order([kept, other], "k"), axis=2)
        ordered = ordered.reshape(clips, slots, features)[:, :slot]
        return (
            ordered.reshape(pack_count, 8, features)
            .transpose(0, 2, 1)
            .reshape(pack_count, packed_width)
        )

    def by_core(tensor, parts):
        if not parts:
            return jnp.broadcast_to(tensor[None], (2,) + tensor.shape)
        return tensor.reshape((2, tensor.shape[0] // 2) + tensor.shape[1:])

    turned = [t.astype(BF).T for t in (w_query, w_key, w_value)] + [w_attn_out.astype(BF)]
    head_parts = jnp.stack([by_core(t, split) for t in turned], axis=1)
    head_parts = head_parts.reshape(2, 4 * part_heads * head_dim, rows)
    in_parts = by_core(w_in.astype(BF).T, True)
    out_parts = by_core(w_out.astype(BF), True)
    all_parts = jnp.concatenate([head_parts, in_parts, out_parts], axis=1)
    kept = pick(all_parts, k, 0)
    other = swap(pick(all_parts, 1 - k, 0), "k")
    shard = jnp.concatenate(in_order([kept, other], "k"), axis=1)
    head_rows = head_parts.shape[1]

    def gather_weights(part):
        stacked = jnp.concatenate(pieces_of(part, "z"), axis=0)
        return jnp.concatenate(in_order(pieces_of(stacked, "x"), "x"), axis=1)

    head_weights = gather_weights(shard[:head_rows])
    in_weights = gather_weights(shard[head_rows : head_rows + half_units])
    out_weights = gather_weights(shard[head_rows + half_units :])

    head_weights = head_weights.reshape(z_size, 4, part_heads, head_dim, width)
    if not split:
        head_weights = lax.dynamic_slice_in_dim(head_weights, k * (z_size // 2), z_size // 2, 0)
    head_weights = head_weights.transpose(1, 0, 2, 3, 4).reshape(4, heads, head_dim, width)
    head_weights = jnp.pad(head_weights, ((0, 0), (0, 0), (0, PAD - head_dim), (0, 0)))
    head_weights = head_weights.reshape(4, heads * PAD, width)
    qkv_weights = head_weights[:3].reshape(3 * heads * PAD, width)
    attn_weights = head_weights[3]

    full_vectors = jnp.stack([ln1_gain, ln1_bias, ln2_gain, ln2_bias, b_attn_out, b_out])
    full_count = full_vectors.shape[0]
    full_by_y = jnp.stack(in_order(pieces_of(full_vectors, "y"), "y"))
    part_vector = jnp.concatenate([b_query, b_value, b_in])
    vector_pieces = pieces_of(jnp.concatenate([full_by_y.reshape(-1), part_vector]), "z")
    full_size = full_by_y.size
    full_by_z = jnp.stack(in_order([p[:full_size] for p in vector_pieces], "z"))
    full_by_z = full_by_z.reshape(columns, full_count, features)
    gain_one, shift_one, gain_two, shift_two, attn_shift, out_shift = (
        full_by_z.transpose(1, 0, 2).reshape(full_count, 1, width)
    )
    part_by_z = jnp.stack([p[full_size:] for p in vector_pieces])

    def head_vector(tensor):
        tensor = tensor.reshape(z_size, block_heads, head_dim)
        if split:
            tensor = pick(tensor.reshape(z_size, 2, part_heads, head_dim), k, 1)
        else:
            tensor = lax.dynamic_slice_in_dim(tensor, k * (z_size // 2), z_size // 2, 0)
        tensor = tensor.reshape(heads, head_dim)
        return jnp.pad(tensor, ((0, 0), (0, PAD - head_dim)))

    query_shift = head_vector(part_by_z[:, :features])
    value_shift = head_vector(part_by_z[:, features : 2 * features])
    unit_shift = pick(part_by_z[:, 2 * features :].reshape(z_size, 2, half_units), k, 1).reshape(-1)

    all_lengths = jnp.concatenate(in_order(pieces_of(lengths, "k"), "k"))
    clip_length = pick(all_lengths, z, 0)

    quarter_slots = jnp.arange(quarter)
    own_valid = (y * 2 + k) * quarter + quarter_slots < clip_length
    slot_order = jnp.concatenate(
        [((y ^ dy) * 2 + (k ^ dk)) * quarter + quarter_slots for dy in range(y_size) for dk in range(2)]
    )
    key_mask = jnp.where(slot_order < clip_length, 0.0, MASKED)

    lane = jnp.arange(PAD)[None, :]
    none = jnp.zeros((heads, PAD), F32)
    is_first = jnp.broadcast_to(lane == head_dim, (heads, PAD)).astype(F32)
    is_extra = jnp.broadcast_to((lane >= head_dim) & (lane < head_dim + 2), (heads, PAD)).astype(F32)
    qkv_shift = jnp.concatenate([query_shift, none, value_shift]).reshape(1, -1)
    qkv_scale = jnp.concatenate([none + head_dim**-0.5 * LOG2E, none + 1, none + 1]).reshape(1, -1)
    qkv_extra = jnp.concatenate([is_first, none, -is_extra]).reshape(1, -1)
    mask_lane = jnp.concatenate([none, is_first, none]).reshape(1, -1)

    tokens = to_tokens(inputs).astype(F32)
    normal_one, scale_one, normed_part = norm_forward(tokens, gain_one, shift_one)
    normed_rows = gather_group(normed_part)
    grad_low = to_tokens(cotangent)
    grad_low = jnp.where(own_valid[:, None], grad_low, jnp.zeros_like(grad_low))
    grad_rows = gather_group(grad_low)
    grad_out = grad_low.astype(F32)

    packed = []
    for d, rows_d in enumerate(normed_rows):
        mask_d = key_mask[d * 2 * quarter : (d + 1) * 2 * quarter, None]
        product = (dot(rows_d, qkv_weights, 1, 1) + qkv_shift) * qkv_scale
        packed.append((product + qkv_extra + mask_d * mask_lane).astype(BF))
    packed = jnp.concatenate(packed, axis=0)
    block = slots // 2
    context, weights = attend(packed, heads, block)

    attn_part = reduce_group(
        [
            dot(context[d * 2 * quarter : (d + 1) * 2 * quarter], attn_weights, 1, 0)
            for d in range(y_size)
        ]
    )
    attn_part = attn_part + attn_shift
    middle = tokens + attn_part
    normal_two, scale_two, normed_two_part = norm_forward(middle, gain_two, shift_two)
    normed_two_rows = gather_group(normed_two_part)

    active_rows, grad_hidden_rows = [], []
    for rows_d, grad_d in zip(normed_two_rows, grad_rows):
        hidden = dot(rows_d, in_weights, 1, 1) + unit_shift
        below = 0.5 * (1.0 + lax.erf(hidden * 0.5**0.5))
        active_rows.append((hidden * below).astype(BF))
        slope = below + hidden * (jnp.exp(-0.5 * hidden * hidden) * (0.5 / jnp.pi) ** 0.5)
        grad_hidden_rows.append((dot(grad_d, out_weights, 1, 1) * slope).astype(BF))
    grad_normed_two = reduce_group([dot(g, in_weights, 1, 0) for g in grad_hidden_rows])
    grad_middle = grad_out + norm_backward(grad_normed_two, normal_two, scale_two, gain_two)
    grad_mid_part = grad_middle.astype(BF)
    grad_mid_rows = gather_group(grad_mid_part)

    normed = jnp.concatenate(normed_rows, axis=0)
    normed_two = jnp.concatenate(normed_two_rows, axis=0)
    active = jnp.concatenate(active_rows, axis=0)
    grad_hidden = jnp.concatenate(grad_hidden_rows, axis=0)
    grad_full = jnp.concatenate(grad_rows, axis=0)

    def reduce_weights(total):
        total = total.astype(BF)
        side = 2 * rows
        own = lax.dynamic_slice_in_dim(total, x * side, side, 1).astype(F32)
        for d in range(1, x_size):
            own = own + swap(lax.dynamic_slice_in_dim(total, (x ^ d) * side, side, 1), "x", d).astype(F32)
        own = own.reshape(z_size, -1, side)
        result = own[0]
        for d in range(1, z_size):
            result = result + swap(own[d].astype(BF), "z", d).astype(F32)
        return result

    def to_cores(total, parts):
        kept = lax.dynamic_slice_in_dim(total, k * rows, rows, 1)
        other = swap(lax.dynamic_slice_in_dim(total, (1 - k) * rows, rows, 1).astype(BF), "k").astype(F32)
        if not parts:
            return kept + other
        return jnp.stack(in_order([kept, other], "k"))

    out_total = reduce_weights(dot(active, grad_full, 0, 0))
    in_total = reduce_weights(dot(grad_hidden, normed_two, 0, 0))
    delta_part = reduce_group([dot(a, out_weights, 1, 0) for a in active_rows])
    delta = attn_part + delta_part + out_shift
    layer_out = inputs + from_tokens(delta).astype(F32)

    grad_mid_full = jnp.concatenate(grad_mid_rows, axis=0)
    grad_context = dot(grad_mid_full, attn_weights, 1, 1).astype(BF)
    grads = attend_back(packed, grad_context, context, weights, heads, head_dim, block)
    qkv_cube = qkv_weights.reshape(3, heads * PAD, width)
    grad_normed = reduce_group(
        [
            sum(dot(grads[j, d * 2 * quarter : (d + 1) * 2 * quarter], qkv_cube[j], 1, 0) for j in range(3))
            for d in range(y_size)
        ]
    )
    grad_tokens = norm_backward(grad_normed, normal_one, scale_one, gain_one)
    input_grad = from_tokens(grad_middle + grad_tokens).astype(F32)

    head_totals = [dot(grads[j], normed, 0, 0) for j in range(3)] + [dot(context, grad_mid_full, 0, 0)]
    head_totals = jnp.stack(head_totals).reshape(4, -1, part_heads, PAD, width)[:, :, :, :head_dim]
    head_totals = head_totals.transpose(1, 0, 2, 3, 4)
    if not split:
        blank = jnp.zeros((z_size,) + head_totals.shape[1:], F32)
        head_totals = lax.dynamic_update_slice_in_dim(blank, head_totals, k * (z_size // 2), 0)
    head_total = reduce_weights(head_totals.reshape(-1, width))
    head_blocks = to_cores(head_total, split).reshape(-1, 4, part_heads * head_dim, rows)
    grad_query_w, grad_key_w, grad_value_w, grad_attn_w = (
        head_blocks[:, j].reshape(features, rows) for j in range(4)
    )
    grad_in_w = to_cores(in_total, True).reshape(units, rows).T
    grad_out_w = to_cores(out_total, True).reshape(units, rows)

    full_sums = jnp.stack(
        [
            jnp.sum(v, axis=0)
            for v in (
                grad_normed * normal_one,
                grad_normed,
                grad_middle,
                grad_normed_two * normal_two,
                grad_normed_two,
                grad_out,
            )
        ]
    )

    def head_sums(tensor):
        total = jnp.sum(tensor.astype(F32), axis=0).reshape(-1, part_heads, PAD)[:, :, :head_dim]
        if not split:
            blank = jnp.zeros((z_size,) + total.shape[1:], F32)
            total = lax.dynamic_update_slice_in_dim(blank, total, k * (z_size // 2), 0)
        return total.reshape(z_size, -1)

    part_sums = jnp.concatenate(
        [
            head_sums(grads[0]),
            head_sums(grads[2]),
            jnp.sum(grad_hidden.astype(F32), axis=0).reshape(z_size, half_units),
        ],
        axis=1,
    )
    full_sums = full_sums.reshape(full_count, z_size, y_size, features).transpose(1, 2, 0, 3)
    flat = jnp.concatenate([full_sums.reshape(-1), part_sums.reshape(-1)])
    flat = sum(pieces_of(flat, "x"))
    full_cut = full_sums.size
    full_flat = flat[:full_cut].reshape(z_size, -1)
    part_flat = flat[full_cut:].reshape(z_size, -1)
    received = None
    for d in range(z_size):
        piece = jnp.concatenate([pick(full_flat, z ^ d, 0), part_flat[d]])
        received = piece if d == 0 else received + swap(piece, "z", d)
    cut = full_flat.shape[1]
    by_y = received[:cut].reshape(y_size, -1)
    mine = pick(by_y, y, 0)
    for d in range(1, y_size):
        mine = mine + swap(pick(by_y, y ^ d, 0), "y", d)
    last = jnp.concatenate([mine, received[cut:]])
    last_pair = [last, swap(last, "k")]
    own_size = mine.shape[0]
    vec_one_gain, vec_one_bias, vec_battn, vec_two_gain, vec_two_bias, vec_bout = (
        last_pair[0][:own_size] + last_pair[1][:own_size]
    ).reshape(full_count, features)
    head_size = part_heads * head_dim
    cores = in_order([p[own_size:] for p in last_pair], "k")
    if split:
        vec_bquery = jnp.concatenate([c[:head_size] for c in cores])
        vec_bvalue = jnp.concatenate([c[head_size : 2 * head_size] for c in cores])
    else:
        vec_bquery = cores[0][:head_size] + cores[1][:head_size]
        vec_bvalue = cores[0][head_size : 2 * head_size] + cores[1][head_size : 2 * head_size]
    vec_bin = jnp.concatenate([c[2 * head_size :] for c in cores])

    return (
        layer_out,
        input_grad,
        vec_one_gain,
        vec_one_bias,
        grad_query_w.T,
        vec_bquery,
        grad_key_w.T,
        grad_value_w.T,
        vec_bvalue,
        grad_attn_w,
        vec_battn,
        vec_two_gain,
        vec_two_bias,
        grad_in_w,
        vec_bin,
        grad_out_w,
        vec_bout,
    )


def solution(mesh):
    row_size, col_size = mesh.shape["row"], mesh.shape["col"]
    grid = Mesh(mesh.devices.reshape(row_size // 2, 2, 4, col_size // 4), ("x", "k", "z", "y"))
    row, col = ("x", "k"), ("z", "y")
    return jax.shard_map(
        local,
        mesh=grid,
        in_specs=(
            P(row, col),
            P(row),
            P(row, col),
            P(col),
            P(col),
            P(row, col),
            P(col),
            P(row, col),
            P(row, col),
            P(col),
            P(col, row),
            P(col),
            P(col),
            P(col),
            P(row, col),
            P(col),
            P(col, row),
            P(col),
        ),
        out_specs=(
            P(row, col),
            P(row, col),
            P(col),
            P(col),
            P(row, col),
            P(col),
            P(row, col),
            P(row, col),
            P(col),
            P(col, row),
            P(col),
            P(col),
            P(col),
            P(row, col),
            P(col),
            P(col, row),
            P(col),
        ),
        check_vma=False,
    )
```

time: 2360 us -> 827 us (0.35)
  waiting for transfers between devices: 1570 us -> 342 us
  blocking collectives: 326 us -> 0 us
  matrix products: 255 us -> 83.4 us
  starting transfers between devices: 1.61 us -> 130 us
  local copies, waits for them, and re-layouts: 74.5 us -> 129 us
  Pallas kernels: 0 us -> 45.6 us
  other arithmetic: 109 us -> 85 us
    reduce_scatter x10 -> x0, waiting for transfers between devices: 1010 us -> none  [the longest x8 954 us: reduce_rows(): return lax.psum_scatter(tensor, 'col', scatter_dimension=1, tiled=True)]
    all_gather x10 -> x0, waiting for transfers between devices: 501 us -> none  [the longest x8 501 us: gather_rows(): return lax.all_gather(tensor, 'col', axis=1, tiled=True)]
    ppermute x0 -> x67, waiting for transfers between devices: none -> 321 us  [swap(): return lax.ppermute(tensor, axis, [(i, i ^ step) for i in range(size)])]
    psum x9 -> x0, blocking collectives: 293 us -> none  [the longest x8 282 us: row_sums(): return lax.psum((jnp.sum(first, axis=1), jnp.sum(second, axis=1)), 'col')]
    dot_general x48 -> x25, matrix products: 255 us -> 83.4 us  [dot(): lax.dot_general(first, second, (((left,), (right,)), ((), ())), preferred...]
    ppermute x0 -> x67, starting transfers between devices: none -> 102 us  [swap(): return lax.ppermute(tensor, axis, [(i, i ^ step) for i in range(size)])]
    unnamed x12 -> x0, waiting for transfers between devices: 52.5 us -> none
    pallas_call x0 -> x2, Pallas kernels: none -> 45.6 us  [the longest x1 25.4 us: attend_back(): pl.pallas_call(functools.partial(backward_body, head_dim, steps), grid=(h...]
  transfers between devices with their start and end apart: 24 -> 71, of which waited for: 21 -> 18; matrix products, arithmetic and copies ran while one was open for 11% -> 32% of each run, Pallas kernels for 0% -> 6%
where the time goes in v1:
time: 827 us; the launch traced here: 818 us
  waiting for transfers between devices  342 us (41%)
  starting transfers between devices  130 us (16%)
  local copies, waits for them, and re-layouts  129 us (16%)
  other arithmetic  85 us (10%)
  matrix products  83.4 us (10%)
  Pallas kernels  45.6 us (6%)
    ppermute x67, waiting for transfers between devices, swap(): return lax.ppermute(tensor, axis, [(i, i ^ step) for i in range(size)])  321 us
    ppermute x67, starting transfers between devices, swap(): return lax.ppermute(tensor, axis, [(i, i ^ step) for i in range(size)])  102 us
    dot_general x25, matrix products, dot(): lax.dot_general(first, second, (((left,), (right,)), ((), ())), preferred...  83.4 us
    unnamed x160, local copies, waits for them, and re-layouts  26.3 us
    pallas_call x1, Pallas kernels, attend_back(): pl.pallas_call(functools.partial(backward_body, head_dim, steps), grid=(h...  25.4 us
    all_to_all x2, waiting for transfers between devices, from_tokens(): moved = lax.all_to_all(blocks, ('z', 'y'), 0, 0)  20.5 us
    pallas_call x1, Pallas kernels, attend(): pl.pallas_call(forward_body, grid=(heads, slots // block), in_specs=[pl.B...  20.2 us
    all_to_all x2, starting transfers between devices, to_tokens(): moved = lax.all_to_all(ordered, ('z', 'y'), 0, 0)  19.9 us
  transfers between devices with their start and end apart: 71, of which 18 were waited for; matrix products, arithmetic and copies ran while one was open for 32% of the time, Pallas kernels for 6%

profile of v1, /device:TPU:0, one launch (start us, length us, event | category | flops | bytes accessed | tf_op | source)
XLA Modules:
  0.0 818.3 jit_solution(17148365755753182256)
XLA Ops:
  35.2 5.1 all-to-all-start
  48.8 25.7 %collective-permute-done.7 = bf16[320,640]{0,1:T(8,128)(2,1)S(1)} collective-permute-done((bf16[320,640]{0,1:T(8,128)(2,1)S(1)}, bf16[320,640]{0,1:T(8,128)(2,1)S(1)}, u32[]{:S(2)}, u32[]{:S(2)}) %collective-permute-start.7) | collective-permute-done | bytes 409632 | tf_op jit(solution)/shard_map/ppermute | solution.py:29
  74.6 23.2 %collective-permute-done.8 = bf16[320,640]{0,1:T(8,128)(2,1)S(1)} collective-permute-done((bf16[320,640]{0,1:T(8,128)(2,1)S(1)}, bf16[320,640]{0,1:T(8,128)(2,1)S(1)}, u32[]{:S(2)}, u32[]{:S(2)}) %collective-permute-start.8) | collective-permute-done | bytes 409632 | tf_op jit(solution)/shard_map/ppermute | solution.py:29
  106.7 27.7 %collective-permute-done.10 = bf16[1280,640]{0,1:T(8,128)(2,1)} collective-permute-done((bf16[1280,640]{0,1:T(8,128)(2,1)}, bf16[1280,640]{0,1:T(8,128)(2,1)}, u32[]{:S(2)}, u32[]{:S(2)}) %collective-permute-start.10) | collective-permute-done | bytes 1638432 | tf_op jit(solution)/shard_map/ppermute | solution.py:29
  138.5 5.7 copy.85
  149.5 4.9 add_convert_fusion.1
  154.5 5.2 add_convert_fusion
  162.2 20.2 %shard_map.305 = (bf16[1536,512]{1,0:T(8,128)(2,1)S(1)}, bf16[4,1536,1536]{2,1,0:T(8,128)(2,1)}) custom-call(bf16[1536,1536]{1,0:T(8,128)(2,1)} %pad_maximum_fusion.query_ref.key_ref.value_ref, bf16[1536,1536]{1,0:T(8,128)(2,1)} %pad_maximum_fusion.query_ref.key_ref.value_ref, bf16[1536,1536]{1,0:T(8,128)(2,1)} %pad_maximum_fusion.query_ref.key_ref.value_ref), custom_call_target="tpu_custom_call" | custom-call | flops 14495514624 | bytes 18874368 | tf_op jit(solution)/shard_map/pallas_call | solution.py:78
  189.1 14.8 %all-to-all-start.2 = ((bf16[8,384,160]{1,2,0:T(8,128)(2,1)}), bf16[8,384,160]{1,2,0:T(8,128)(2,1)}, u32[]{:S(2)}, u32[]{:S(2)}) async-start(bf16[8,384,160]{1,2,0:T(8,128)(2,1)} %bitcast.248), calls=%async_computation.2 | async-start | bytes 1966080 | tf_op jit(solution)/shard_map/all_to_all | solution.py:250
  214.9 25.4 %collective-permute-done.18 = bf16[320,640]{0,1:T(8,128)(2,1)} collective-permute-done((bf16[320,640]{0,1:T(8,128)(2,1)}, bf16[320,640]{0,1:T(8,128)(2,1)}, u32[]{:S(2)}, u32[]{:S(2)}) %collective-permute-start.18) | collective-permute-done | bytes 409632 | tf_op jit(solution)/shard_map/ppermute | solution.py:29
  244.6 16.8 %collective-permute-done.19 = bf16[320,640]{0,1:T(8,128)(2,1)} collective-permute-done((bf16[320,640]{0,1:T(8,128)(2,1)}, bf16[320,640]{0,1:T(8,128)(2,1)}, u32[]{:S(2)}, u32[]{:S(2)}) %collective-permute-start.19) | collective-permute-done | bytes 409632 | tf_op jit(solution)/shard_map/ppermute | solution.py:29
  276.6 26.9 %collective-permute-done.23 = bf16[320,640]{0,1:T(8,128)(2,1)} collective-permute-done((bf16[320,640]{0,1:T(8,128)(2,1)}, bf16[320,640]{0,1:T(8,128)(2,1)}, u32[]{:S(2)}, u32[]{:S(2)}) %collective-permute-start.23) | collective-permute-done | bytes 409632 | tf_op jit(solution)/shard_map/ppermute | solution.py:29
  325.4 23.0 %collective-permute-done.25 = bf16[1280,640]{0,1:T(8,128)(2,1)} collective-permute-done((bf16[1280,640]{0,1:T(8,128)(2,1)}, bf16[1280,640]{0,1:T(8,128)(2,1)}, u32[]{:S(2)}, u32[]{:S(2)}) %collective-permute-start.25) | collective-permute-done | bytes 1638432 | tf_op jit(solution)/shard_map/ppermute | solution.py:29
  359.7 14.6 %collective-permute-done.27 = bf16[384,1280]{1,0:T(8,128)(2,1)S(1)} collective-permute-done((bf16[384,1280]{1,0:T(8,128)(2,1)S(1)}, bf16[384,1280]{1,0:T(8,128)(2,1)S(1)}, u32[]{:S(2)}, u32[]{:S(2)}) %collective-permute-start.27) | collective-permute-done | bytes 983072 | tf_op jit(solution)/shard_map/ppermute | solution.py:29
  374.4 4.6 fusion.25
  392.4 4.6 fusion.26
  402.4 5.9 convolution_convert_fusion.1
  411.1 8.7 %convolution_convert_fusion = bf16[1280,1280]{1,0:T(8,128)(2,1)} fusion(bf16[768,1280]{1,0:T(8,128)(2,1)S(1)} %copy-done.76, bf16[768,1280]{1,0:T(8,128)(2,1)S(1)} %copy-done.74, bf16[384,1280]{1,0:T(8,128)(2,1)S(1)} %collective-permute-done.36, bf16[384,1280]{1,0:T(8,128)(2,1)} %collective-permute-done.35, ...), kind=kOutput, calls=%fused_computation.1 | convolution fusion | flops 5058396160 | bytes 11141120 | tf_op jit(solution)/shard_map/dot_general | solution.py:22
  428.2 19.2 %collective-permute-done.57 = bf16[1280,640]{1,0:T(8,128)(2,1)} collective-permute-done((bf16[1280,640]{1,0:T(8,128)(2,1)S(1)}, bf16[1280,640]{1,0:T(8,128)(2,1)}, u32[]{:S(2)}, u32[]{:S(2)}) %collective-permute-start.57) | collective-permute-done | bytes 1638432 | tf_op jit(solution)/shard_map/ppermute | solution.py:29
  452.9 28.6 %collective-permute-done.62 = bf16[1280,640]{1,0:T(8,128)(2,1)S(1)} collective-permute-done((bf16[1280,640]{1,0:T(8,128)(2,1)S(1)}, bf16[1280,640]{1,0:T(8,128)(2,1)S(1)}, u32[]{:S(2)}, u32[]{:S(2)}) %collective-permute-start.62) | collective-permute-done | bytes 1638432 | tf_op jit(solution)/shard_map/ppermute | solution.py:29
  484.2 30.6 %collective-permute-start.59 = (bf16[320,640]{1,0:T(8,128)(2,1)}, bf16[320,640]{1,0:T(8,128)(2,1)}, u32[]{:S(2)}, u32[]{:S(2)}) collective-permute-start(bf16[320,640]{1,0:T(8,128)(2,1)} %get-tuple-element.122), channel_id=1, source_target_pairs={{0,4},{2,6},{4,0},{6,2},{1,5},{3,7},{5,1},{7,3},{8,12},{10,14},{12... | collective-permute-start | bytes 1228808 | tf_op jit(solution)/shard_map/ppermute | solution.py:29
  527.6 4.7 all-to-all-start.1
  537.6 29.1 %collective-permute-done.59 = bf16[320,640]{1,0:T(8,128)(2,1)} collective-permute-done((bf16[320,640]{1,0:T(8,128)(2,1)}, bf16[320,640]{1,0:T(8,128)(2,1)}, u32[]{:S(2)}, u32[]{:S(2)}) %collective-permute-start.59) | collective-permute-done | bytes 409632 | tf_op jit(solution)/shard_map/ppermute | solution.py:29
  570.7 24.5 %collective-permute-done.64 = bf16[320,640]{1,0:T(8,128)(2,1)S(1)} collective-permute-done((bf16[320,640]{1,0:T(8,128)(2,1)}, bf16[320,640]{1,0:T(8,128)(2,1)S(1)}, u32[]{:S(2)}, u32[]{:S(2)}) %collective-permute-start.64) | collective-permute-done | bytes 409632 | tf_op jit(solution)/shard_map/ppermute | solution.py:29
  606.2 4.3 convolution_convert_fusion.2.grad_ref
  610.5 25.4 %shard_map.306 = bf16[3,1536,512]{2,1,0:T(8,128)(2,1)} custom-call(bf16[1536,1536]{1,0:T(8,128)(2,1)} %pad_maximum_fusion.query_ref.key_ref.value_ref, bf16[1536,1536]{1,0:T(8,128)(2,1)} %pad_maximum_fusion.query_ref.key_ref.value_ref, bf16[1536,1536]{1,0:T(8,128)(2,1)} %pad_maximum_fusion.query_ref.key_ref.value_ref, ...), custom_call_target="tpu_custom_call" | custom-call | flops 19327352832 | bytes 18874368 | tf_op jit(solution)/shard_map/pallas_call | solution.py:156
  658.8 4.5 convolution_convert_fusion.3
  699.4 17.4 %collective-permute-done.52 = bf16[1280,640]{1,0:T(8,128)(2,1)} collective-permute-done((bf16[1280,640]{1,0:T(8,128)(2,1)}, bf16[1280,640]{1,0:T(8,128)(2,1)}, u32[]{:S(2)}, u32[]{:S(2)}) %collective-permute-start.52) | collective-permute-done | bytes 1638432 | tf_op jit(solution)/shard_map/ppermute | solution.py:29
  716.9 4.5 fusion.116
  736.4 15.0 %collective-permute-done.49 = f32[2400]{0:T(1024)S(1)} collective-permute-done((f32[2400]{0:T(1024)S(1)}, f32[2400]{0:T(1024)S(1)}, u32[]{:S(2)}, u32[]{:S(2)}) %collective-permute-start.49) | collective-permute-done | bytes 9632 | tf_op jit(solution)/shard_map/ppermute | solution.py:29
  751.4 15.8 %collective-permute-start.53 = (bf16[320,640]{1,0:T(8,128)(2,1)S(1)}, bf16[320,640]{1,0:T(8,128)(2,1)}, u32[]{:S(2)}, u32[]{:S(2)}) collective-permute-start(bf16[320,640]{1,0:T(8,128)(2,1)S(1)} %get-tuple-element.123), channel_id=1, source_target_pairs={{0,2},{2,0},{4,6},{6,4},{1,3},{3,1},{5,7},{7,5},{8,10},{10,8},{12,... | collective-permute-start | bytes 1228808 | tf_op jit(solution)/shard_map/ppermute | solution.py:29
  783.4 20.5 %all-to-all-done.3 = bf16[8,384,160]{1,2,0:T(8,128)(2,1)S(1)} async-done(((bf16[8,384,160]{1,2,0:T(8,128)(2,1)}), bf16[8,384,160]{1,2,0:T(8,128)(2,1)S(1)}, u32[]{:S(2)}, u32[]{:S(2)}) %all-to-all-start.3) | async-done | bytes 983072 | tf_op jit(solution)/shard_map/all_to_all | solution.py:255
  (513 shorter events, 307.8 us)
Async XLA Ops:
  24.1 162.7 %collective-permute-start.32 = (bf16[2,2,384,160]{2,3,1,0:T(8,128)(2,1)}, bf16[2,2,384,160]{2,3,1,0:T(8,128)(2,1)}, u32[]{:S(2)}, u32[]{:S(2)}) collective-permute-start(bf16[2,2,384,160]{2,3,1,0:T(8,128)(2,1)} %bitcast.263), channel_id=1, source_target_pairs={{0,8},{8,0},{1,9},{9,1},{2,10},{10,2},{3,11},{11,3},{4,12},{12,4},... | collective-permute-start | bytes 1474568 | tf_op jit(solution)/shard_map/ppermute | solution.py:29
  35.2 66.7 %all-to-all-start = ((bf16[8,384,160]{1,2,0:T(8,128)(2,1)}), bf16[8,384,160]{1,2,0:T(8,128)(2,1)S(1)}, u32[]{:S(2)}, u32[]{:S(2)}) async-start(bf16[8,384,160]{1,2,0:T(8,128)(2,1)} %bitcast.5), calls=%async_computation | async-start | bytes 1966080 | tf_op jit(solution)/shard_map/all_to_all | solution.py:250
  45.5 52.3 %collective-permute-start.8 = (bf16[320,640]{0,1:T(8,128)(2,1)S(1)}, bf16[320,640]{0,1:T(8,128)(2,1)S(1)}, u32[]{:S(2)}, u32[]{:S(2)}) collective-permute-start(bf16[320,640]{0,1:T(8,128)(2,1)S(1)} %get-tuple-element.137), channel_id=1, source_target_pairs={{0,4},{2,6},{4,0},{6,2},{1,5},{3,7},{5,1},{7,3},{8,12},{10,14},{12... | collective-permute-start | bytes 1228808 | tf_op jit(solution)/shard_map/ppermute | solution.py:29
  47.8 49.9 %collective-permute-start.9 = (bf16[320,640]{0,1:T(8,128)(2,1)S(1)}, bf16[320,640]{0,1:T(8,128)(2,1)S(1)}, u32[]{:S(2)}, u32[]{:S(2)}) collective-permute-start(bf16[320,640]{0,1:T(8,128)(2,1)S(1)} %get-tuple-element.137), channel_id=1, source_target_pairs={{0,6},{2,4},{4,2},{6,0},{1,7},{3,5},{5,3},{7,1},{8,14},{10,12},{12... | collective-permute-start | bytes 1228808 | tf_op jit(solution)/shard_map/ppermute | solution.py:29
  106.7 42.4 %collective-permute-start.5 = (bf16[384,1280]{1,0:T(8,128)(2,1)S(1)}, bf16[384,1280]{1,0:T(8,128)(2,1)}, u32[]{:S(2)}, u32[]{:S(2)}) collective-permute-start(bf16[384,1280]{1,0:T(8,128)(2,1)S(1)} %add_convert_fusion.4), channel_id=1, source_target_pairs={{0,8},{8,0},{1,9},{9,1},{2,10},{10,2},{3,11},{11,3},{4,12},{12,4},... | collective-permute-start | bytes 2949128 | tf_op jit(solution)/shard_map/ppermute | solution.py:29
  186.4 53.9 %collective-permute-start.15 = (bf16[384,1280]{1,0:T(8,128)(2,1)}, bf16[384,1280]{1,0:T(8,128)(2,1)}, u32[]{:S(2)}, u32[]{:S(2)}) collective-permute-start(bf16[384,1280]{1,0:T(8,128)(2,1)} %slice.611), channel_id=1, source_target_pairs={{0,8},{8,0},{1,9},{9,1},{2,10},{10,2},{3,11},{11,3},{4,12},{12,4},... | collective-permute-start | bytes 2949128 | tf_op jit(solution)/shard_map/ppermute | solution.py:29
  189.1 120.0 %all-to-all-start.2 = ((bf16[8,384,160]{1,2,0:T(8,128)(2,1)}), bf16[8,384,160]{1,2,0:T(8,128)(2,1)}, u32[]{:S(2)}, u32[]{:S(2)}) async-start(bf16[8,384,160]{1,2,0:T(8,128)(2,1)} %bitcast.248), calls=%async_computation.2 | async-start | bytes 1966080 | tf_op jit(solution)/shard_map/all_to_all | solution.py:250
  205.9 55.5 %collective-permute-start.19 = (bf16[320,640]{0,1:T(8,128)(2,1)}, bf16[320,640]{0,1:T(8,128)(2,1)}, u32[]{:S(2)}, u32[]{:S(2)}) collective-permute-start(bf16[320,640]{0,1:T(8,128)(2,1)} %get-tuple-element.138), channel_id=1, source_target_pairs={{0,4},{2,6},{4,0},{6,2},{1,5},{3,7},{5,1},{7,3},{8,12},{10,14},{12... | collective-permute-start | bytes 1228808 | tf_op jit(solution)/shard_map/ppermute | solution.py:29
  208.3 53.2 %collective-permute-start.20 = (bf16[320,640]{0,1:T(8,128)(2,1)}, bf16[320,640]{0,1:T(8,128)(2,1)}, u32[]{:S(2)}, u32[]{:S(2)}) collective-permute-start(bf16[320,640]{0,1:T(8,128)(2,1)} %get-tuple-element.138), channel_id=1, source_target_pairs={{0,6},{2,4},{4,2},{6,0},{1,7},{3,5},{5,3},{7,1},{8,14},{10,12},{12... | collective-permute-start | bytes 1228808 | tf_op jit(solution)/shard_map/ppermute | solution.py:29
  208.3 66.8 %collective-permute-start.22 = (bf16[320,640]{0,1:T(8,128)(2,1)}, bf16[320,640]{0,1:T(8,128)(2,1)}, u32[]{:S(2)}, u32[]{:S(2)}) collective-permute-start(bf16[320,640]{0,1:T(8,128)(2,1)} %get-tuple-element.136), channel_id=1, source_target_pairs={{0,2},{2,0},{4,6},{6,4},{1,3},{3,1},{5,7},{7,5},{8,10},{10,8},{12,... | collective-permute-start | bytes 1228808 | tf_op jit(solution)/shard_map/ppermute | solution.py:29
  240.3 63.2 %collective-permute-start.23 = (bf16[320,640]{0,1:T(8,128)(2,1)}, bf16[320,640]{0,1:T(8,128)(2,1)}, u32[]{:S(2)}, u32[]{:S(2)}) collective-permute-start(bf16[320,640]{0,1:T(8,128)(2,1)} %get-tuple-element.136), channel_id=1, source_target_pairs={{0,4},{2,6},{4,0},{6,2},{1,5},{3,7},{5,1},{7,3},{8,12},{10,14},{12... | collective-permute-start | bytes 1228808 | tf_op jit(solution)/shard_map/ppermute | solution.py:29
  240.3 63.2 %collective-permute-start.24 = (bf16[320,640]{0,1:T(8,128)(2,1)}, bf16[320,640]{0,1:T(8,128)(2,1)}, u32[]{:S(2)}, u32[]{:S(2)}) collective-permute-start(bf16[320,640]{0,1:T(8,128)(2,1)} %get-tuple-element.136), channel_id=1, source_target_pairs={{0,6},{2,4},{4,2},{6,0},{1,7},{3,5},{5,3},{7,1},{8,14},{10,12},{12... | collective-permute-start | bytes 1228808 | tf_op jit(solution)/shard_map/ppermute | solution.py:29
  261.4 57.5 %collective-permute-start.14 = (bf16[384,1280]{1,0:T(8,128)(2,1)}, bf16[384,1280]{1,0:T(8,128)(2,1)}, u32[]{:S(2)}, u32[]{:S(2)}) collective-permute-start(bf16[384,1280]{1,0:T(8,128)(2,1)} %slice.612), channel_id=1, source_target_pairs={{0,8},{8,0},{1,9},{9,1},{2,10},{10,2},{3,11},{11,3},{4,12},{12,4},... | collective-permute-start | bytes 2949128 | tf_op jit(solution)/shard_map/ppermute | solution.py:29
  261.4 57.5 %collective-permute-start.16 = (bf16[384,1280]{1,0:T(8,128)(2,1)}, bf16[384,1280]{1,0:T(8,128)(2,1)}, u32[]{:S(2)}, u32[]{:S(2)}) collective-permute-start(bf16[384,1280]{1,0:T(8,128)(2,1)} %fusion.40), channel_id=1, source_target_pairs={{0,1},{1,0},{2,3},{3,2},{4,5},{5,4},{6,7},{7,6},{8,9},{9,8},{10,11... | collective-permute-start | bytes 2949128 | tf_op jit(solution)/shard_map/ppermute | solution.py:29
  275.1 47.8 %collective-permute-start.21 = (bf16[1280,640]{0,1:T(8,128)(2,1)}, bf16[1280,640]{0,1:T(8,128)(2,1)}, u32[]{:S(2)}, u32[]{:S(2)}) collective-permute-start(bf16[1280,640]{0,1:T(8,128)(2,1)} %concatenate.144), channel_id=1, source_target_pairs={{0,16},{16,0},{1,17},{17,1},{2,18},{18,2},{3,19},{19,3},{4,20},{20... | collective-permute-start | bytes 4915208 | tf_op jit(solution)/shard_map/ppermute | solution.py:29
  318.9 55.5 %collective-permute-start.33 = (bf16[384,1280]{1,0:T(8,128)(2,1)}, bf16[384,1280]{1,0:T(8,128)(2,1)S(1)}, u32[]{:S(2)}, u32[]{:S(2)}) collective-permute-start(bf16[384,1280]{1,0:T(8,128)(2,1)} %broadcast_select_fusion.6), channel_id=1, source_target_pairs={{0,8},{8,0},{1,9},{9,1},{2,10},{10,2},{3,11},{11,3},{4,12},{12,4},... | collective-permute-start | bytes 2949128 | tf_op jit(solution)/shard_map/ppermute | solution.py:29
  359.6 161.2 %collective-permute-start.26 = (bf16[384,1280]{1,0:T(8,128)(2,1)}, bf16[384,1280]{1,0:T(8,128)(2,1)}, u32[]{:S(2)}, u32[]{:S(2)}) collective-permute-start(bf16[384,1280]{1,0:T(8,128)(2,1)} %slice.610), channel_id=1, source_target_pairs={{0,8},{8,0},{1,9},{9,1},{2,10},{10,2},{3,11},{11,3},{4,12},{12,4},... | collective-permute-start | bytes 2949128 | tf_op jit(solution)/shard_map/ppermute | solution.py:29
  383.0 101.2 %collective-permute-start.34 = (bf16[384,1280]{1,0:T(8,128)(2,1)}, bf16[384,1280]{1,0:T(8,128)(2,1)}, u32[]{:S(2)}, u32[]{:S(2)}) collective-permute-start(bf16[384,1280]{1,0:T(8,128)(2,1)} %slice.608), channel_id=1, source_target_pairs={{0,8},{8,0},{1,9},{9,1},{2,10},{10,2},{3,11},{11,3},{4,12},{12,4},... | collective-permute-start | bytes 2949128 | tf_op jit(solution)/shard_map/ppermute | solution.py:29
  422.4 59.1 %collective-permute-start.62 = (bf16[1280,640]{1,0:T(8,128)(2,1)S(1)}, bf16[1280,640]{1,0:T(8,128)(2,1)S(1)}, u32[]{:S(2)}, u32[]{:S(2)}) collective-permute-start(bf16[1280,640]{1,0:T(8,128)(2,1)S(1)} %constant_dynamic-slice_fusion), channel_id=1, source_target_pairs={{0,16},{16,0},{1,17},{17,1},{2,18},{18,2},{3,19},{19,3},{4,20},{20... | collective-permute-start | bytes 4915208 | tf_op jit(solution)/shard_map/ppermute | solution.py:29
  425.9 95.4 %collective-permute-start.30 = (bf16[384,1280]{1,0:T(8,128)(2,1)S(1)}, bf16[384,1280]{1,0:T(8,128)(2,1)S(1)}, u32[]{:S(2)}, u32[]{:S(2)}) collective-permute-start(bf16[384,1280]{1,0:T(8,128)(2,1)S(1)} %fusion.35), channel_id=1, source_target_pairs={{0,1},{1,0},{2,3},{3,2},{4,5},{5,4},{6,7},{7,6},{8,9},{9,8},{10,11... | collective-permute-start | bytes 2949128 | tf_op jit(solution)/shard_map/ppermute | solution.py:29
  447.4 67.4 %collective-permute-start.38 = (bf16[384,1280]{1,0:T(8,128)(2,1)S(1)}, bf16[384,1280]{1,0:T(8,128)(2,1)S(1)}, u32[]{:S(2)}, u32[]{:S(2)}) collective-permute-start(bf16[384,1280]{1,0:T(8,128)(2,1)S(1)} %fusion.33), channel_id=1, source_target_pairs={{0,1},{1,0},{2,3},{3,2},{4,5},{5,4},{6,7},{7,6},{8,9},{9,8},{10,11... | collective-permute-start | bytes 2949128 | tf_op jit(solution)/shard_map/ppermute | solution.py:29
  481.5 56.0 %collective-permute-start.60 = (bf16[320,640]{1,0:T(8,128)(2,1)}, bf16[320,640]{1,0:T(8,128)(2,1)}, u32[]{:S(2)}, u32[]{:S(2)}) collective-permute-start(bf16[320,640]{1,0:T(8,128)(2,1)} %get-tuple-element.121), channel_id=1, source_target_pairs={{0,6},{2,4},{4,2},{6,0},{1,7},{3,5},{5,3},{7,1},{8,14},{10,12},{12... | collective-permute-start | bytes 1228808 | tf_op jit(solution)/shard_map/ppermute | solution.py:29
  484.2 82.5 %collective-permute-start.59 = (bf16[320,640]{1,0:T(8,128)(2,1)}, bf16[320,640]{1,0:T(8,128)(2,1)}, u32[]{:S(2)}, u32[]{:S(2)}) collective-permute-start(bf16[320,640]{1,0:T(8,128)(2,1)} %get-tuple-element.122), channel_id=1, source_target_pairs={{0,4},{2,6},{4,0},{6,2},{1,5},{3,7},{5,1},{7,3},{8,12},{10,14},{12... | collective-permute-start | bytes 1228808 | tf_op jit(solution)/shard_map/ppermute | solution.py:29
  514.8 53.5 %collective-permute-start.58 = (bf16[320,640]{1,0:T(8,128)(2,1)}, bf16[320,640]{1,0:T(8,128)(2,1)}, u32[]{:S(2)}, u32[]{:S(2)}) collective-permute-start(bf16[320,640]{1,0:T(8,128)(2,1)} %get-tuple-element.120), channel_id=1, source_target_pairs={{0,2},{2,0},{4,6},{6,4},{1,3},{3,1},{5,7},{7,5},{8,10},{10,8},{12,... | collective-permute-start | bytes 1228808 | tf_op jit(solution)/shard_map/ppermute | solution.py:29
  520.8 75.8 %collective-permute-start.40 = (bf16[384,1280]{1,0:T(8,128)(2,1)}, bf16[384,1280]{1,0:T(8,128)(2,1)}, u32[]{:S(2)}, u32[]{:S(2)}) collective-permute-start(bf16[384,1280]{1,0:T(8,128)(2,1)} %convert_element_type.308), channel_id=1, source_target_pairs={{0,1},{1,0},{2,3},{3,2},{4,5},{5,4},{6,7},{7,6},{8,9},{9,8},{10,11... | collective-permute-start | bytes 2949128 | tf_op jit(solution)/shard_map/ppermute | solution.py:29
  527.6 76.6 %all-to-all-start.1 = ((bf16[8,384,160]{1,2,0:T(8,128)(2,1)}), bf16[8,384,160]{1,2,0:T(8,128)(2,1)}, u32[]{:S(2)}, u32[]{:S(2)}) async-start(bf16[8,384,160]{1,2,0:T(8,128)(2,1)} %bitcast.249), calls=%async_computation.1 | async-start | bytes 1966080 | tf_op jit(solution)/shard_map/all_to_all | solution.py:255
  537.5 57.7 %collective-permute-start.64 = (bf16[320,640]{1,0:T(8,128)(2,1)}, bf16[320,640]{1,0:T(8,128)(2,1)S(1)}, u32[]{:S(2)}, u32[]{:S(2)}) collective-permute-start(bf16[320,640]{1,0:T(8,128)(2,1)} %get-tuple-element.119), channel_id=1, source_target_pairs={{0,4},{2,6},{4,0},{6,2},{1,5},{3,7},{5,1},{7,3},{8,12},{10,14},{12... | collective-permute-start | bytes 1228808 | tf_op jit(solution)/shard_map/ppermute | solution.py:29
  606.1 73.8 %collective-permute-start.31 = (bf16[2,2,384,160]{2,3,1,0:T(8,128)(2,1)}, bf16[2,2,384,160]{2,3,1,0:T(8,128)(2,1)}, u32[]{:S(2)}, u32[]{:S(2)}) collective-permute-start(bf16[2,2,384,160]{2,3,1,0:T(8,128)(2,1)} %dynamic-slice_bitcast_fusion.1), channel_id=1, source_target_pairs={{0,8},{8,0},{1,9},{9,1},{2,10},{10,2},{3,11},{11,3},{4,12},{12,4},... | collective-permute-start | bytes 1474568 | tf_op jit(solution)/shard_map/ppermute | solution.py:29
  645.9 45.3 %collective-permute-start.43 = (bf16[384,1280]{1,0:T(8,128)(2,1)}, bf16[384,1280]{1,0:T(8,128)(2,1)}, u32[]{:S(2)}, u32[]{:S(2)}) collective-permute-start(bf16[384,1280]{1,0:T(8,128)(2,1)} %slice.605), channel_id=1, source_target_pairs={{0,8},{8,0},{1,9},{9,1},{2,10},{10,2},{3,11},{11,3},{4,12},{12,4},... | collective-permute-start | bytes 2949128 | tf_op jit(solution)/shard_map/ppermute | solution.py:29
  651.8 69.7 %collective-permute-start.42 = (bf16[384,1280]{1,0:T(8,128)(2,1)}, bf16[384,1280]{1,0:T(8,128)(2,1)}, u32[]{:S(2)}, u32[]{:S(2)}) collective-permute-start(bf16[384,1280]{1,0:T(8,128)(2,1)} %slice.606), channel_id=1, source_target_pairs={{0,8},{8,0},{1,9},{9,1},{2,10},{10,2},{3,11},{11,3},{4,12},{12,4},... | collective-permute-start | bytes 2949128 | tf_op jit(solution)/shard_map/ppermute | solution.py:29
  729.2 51.9 %collective-permute-start.55 = (bf16[320,640]{1,0:T(8,128)(2,1)}, bf16[320,640]{1,0:T(8,128)(2,1)}, u32[]{:S(2)}, u32[]{:S(2)}) collective-permute-start(bf16[320,640]{1,0:T(8,128)(2,1)} %get-tuple-element.124), channel_id=1, source_target_pairs={{0,6},{2,4},{4,2},{6,0},{1,7},{3,5},{5,3},{7,1},{8,14},{10,12},{12... | collective-permute-start | bytes 1228808 | tf_op jit(solution)/shard_map/ppermute | solution.py:29
  731.7 49.4 %collective-permute-start.54 = (bf16[320,640]{1,0:T(8,128)(2,1)}, bf16[320,640]{1,0:T(8,128)(2,1)}, u32[]{:S(2)}, u32[]{:S(2)}) collective-permute-start(bf16[320,640]{1,0:T(8,128)(2,1)} %get-tuple-element.125), channel_id=1, source_target_pairs={{0,4},{2,6},{4,0},{6,2},{1,5},{3,7},{5,1},{7,3},{8,12},{10,14},{12... | collective-permute-start | bytes 1228808 | tf_op jit(solution)/shard_map/ppermute | solution.py:29
  (116 other events, 1995.7 us)

commit v2 on v1

v2 whole, which is shorter than its diff:
```python
import functools

import jax
import jax.numpy as jnp
from jax import lax
from jax.experimental import pallas as pl
from jax.experimental.pallas import tpu as pltpu
from jax.sharding import Mesh
from jax.sharding import PartitionSpec as P

HEADS = 16
EPSILON = 1e-05
PAD = 128
LOG2E = 1.4426950408889634
LN2 = 0.6931471805599453
MASKED = -1e30
BF = jnp.bfloat16
F32 = jnp.float32


def dot(first, second, left, right):
    return lax.dot_general(
        first, second, (((left,), (right,)), ((), ())), preferred_element_type=F32
    )


GROUP = ("zl", "yl")


def size_of(axis):
    names = axis if isinstance(axis, tuple) else (axis,)
    total = 1
    for name in names:
        total *= lax.axis_size(name)
    return total


def swap(tensor, axis, step=1):
    return lax.ppermute(tensor, axis, [(i, i ^ step) for i in range(size_of(axis))])


def in_order(pieces, axis):
    mine = lax.axis_index(axis)
    if len(pieces) == 1:
        return pieces
    if len(pieces) == 2:
        return [lax.select_n((mine ^ j) == 1, *pieces) for j in range(2)]
    return [lax.select_n(mine ^ j, *pieces) for j in range(len(pieces))]


def pieces_of(tensor, axis):
    return [tensor] + [swap(tensor, axis, d) for d in range(1, size_of(axis))]


def pick(tensor, index, axis):
    return lax.dynamic_index_in_dim(tensor, index, axis, keepdims=False)


def sync(*values):
    return lax.optimization_barrier(values)


def far_pieces(part):
    return [swap(part, GROUP, d) for d in range(1, size_of(GROUP))]


def with_core(part):
    return jnp.concatenate([part, swap(part, "k")], axis=0)


def cores_sum(product, blocks):
    given = swap(product(blocks[1]).astype(BF), "k").astype(F32)
    return product(blocks[0]) + given


def send_far(sums):
    total = swap(sums[0].astype(BF), GROUP, 1).astype(F32)
    for d in range(2, len(sums) + 1):
        total = total + swap(sums[d - 1].astype(BF), GROUP, d).astype(F32)
    return total


def send_units(total, axis):
    return total[0], swap(total[1], axis)


def send_rows(total):
    x, count = lax.axis_index("x"), lax.axis_size("x")
    last = total.ndim - 1
    side = total.shape[last] // count
    parts = [lax.dynamic_slice_in_dim(total, (x ^ d) * side, side, last) for d in range(count)]
    return tuple(parts[:1] + [swap(parts[d], "x", d) for d in range(1, count)])


def summed(parts):
    return sum(p.astype(F32) for p in parts).astype(BF)


def join_body(pad_rows, x_ref, *refs):
    pieces, out_ref = refs[:-1], refs[-1]
    side = pieces[0].shape[-1]
    for d, piece in enumerate(pieces):
        for j in range(len(pieces)):

            @pl.when((x_ref[0] ^ d) == j)
            def _(piece=piece, j=j):
                columns = slice(j * side, (j + 1) * side)
                if not pad_rows:
                    out_ref[:, columns] = piece[...]
                    return
                count, head_dim = pad_rows
                for p in range(piece.shape[0]):
                    for h in range(count):
                        at = (p * count + h) * PAD
                        out_ref[at : at + head_dim, columns] = piece[p, 0, h * head_dim : (h + 1) * head_dim]
                        out_ref[at + head_dim : at + PAD, columns] = jnp.zeros((PAD - head_dim, side), BF)


def join_rows(pieces, in_spec, grid, out_block, pad_rows=None):
    width = pieces[0].shape[-1] * len(pieces)
    x = lax.axis_index("x").astype(jnp.int32).reshape(1)
    return pl.pallas_call(
        functools.partial(join_body, pad_rows),
        grid=(grid,),
        in_specs=[pl.BlockSpec(memory_space=pltpu.SMEM)] + [in_spec] * len(pieces),
        out_specs=pl.BlockSpec((out_block, width), lambda i: (i, 0)),
        out_shape=jax.ShapeDtypeStruct((grid * out_block, width), BF),
        compiler_params=pltpu.CompilerParams(vmem_limit_bytes=32 * 2**20),
        cost_estimate=pl.CostEstimate(flops=0, bytes_accessed=8 * pieces[0].size * len(pieces), transcendentals=0),
    )(x, *pieces)


def first_rows(slot, clips):
    return [[(slot * c - j + 7) // 8 for j in range(8)] for c in range(clips + 1)]


def take_body(starts, lanes, lines, packed_ref, out_ref, low):
    part = pl.program_id(0)
    count, packed_width = packed_ref.shape
    features = packed_width // 8
    choices = [(c, n) for c, row in enumerate(starts) for n in range(len(row))]

    @pl.when(part == 0)
    def _():
        packed = packed_ref[...].astype(F32)
        tail = max(row[-1][0] for row in starts) + lines - count
        packed = jnp.concatenate([packed, jnp.zeros((tail + -(tail + count) % 8, packed_width), F32)], axis=0)
        for at, (c, n) in enumerate(choices):
            start = starts[c][n][0]
            low[at] = packed[start : start + lines].astype(BF)

    source = lax.broadcasted_iota(jnp.int32, (packed_width, features), 0)
    target = lax.broadcasted_iota(jnp.int32, (packed_width, features), 1)
    for clip, row in enumerate(starts):
        taken = []
        for lane in range(lanes):
            position = part * lanes + lane
            choose = jnp.where(source == target * 8 + position, 1.0, 0.0).astype(BF)
            at = choices.index((clip, 0))
            for n in range(1, len(row)):
                at = jnp.where(position < row[n][1], choices.index((clip, n)), at)
            taken.append(dot(choose, low[at], 0, 1))
        out_ref[0, clip, 0] = jnp.concatenate(taken, axis=1).astype(BF)


def starts_by_clip(slot, clips):
    result = []
    for row in first_rows(slot, clips)[:-1]:
        result.append([(value, sum(v >= value for v in row)) for value in sorted(set(row))])
    return result


def take_positions(packed, slot, clips, lanes, lines):
    count, packed_width = packed.shape
    features = packed_width // 8
    starts = starts_by_clip(slot, clips)
    chips = 8 // (2 * lanes)
    return pl.pallas_call(
        functools.partial(take_body, starts, lanes, lines),
        grid=(8 // lanes,),
        in_specs=[pl.BlockSpec((count, packed_width), lambda j: (0, 0))],
        out_specs=pl.BlockSpec((1, clips, 1, features, lanes * lines), lambda j: (j % 2, 0, j // 2, 0, 0)),
        out_shape=jax.ShapeDtypeStruct((2, clips, chips, features, lanes * lines), BF),
        scratch_shapes=[pltpu.VMEM((sum(len(r) for r in starts), lines, packed_width), BF)],
        compiler_params=pltpu.CompilerParams(vmem_limit_bytes=32 * 2**20),
        cost_estimate=pl.CostEstimate(
            flops=4 * count * packed_width**2, bytes_accessed=8 * count * packed_width, transcendentals=0
        ),
    )(packed)


def put_body(rows, lanes, lines, added, *refs):
    base_ref, tokens_ref, out_ref, total = refs if added else (None,) + refs
    half = pl.program_id(0)
    count, packed_width = out_ref.shape
    features = packed_width // 8
    chips = tokens_ref.shape[2]
    source = lax.broadcasted_iota(jnp.int32, (4 * features, packed_width), 0)
    target = lax.broadcasted_iota(jnp.int32, (4 * features, packed_width), 1)
    position = source // features
    wanted = (source - position * features) * 8 + position + 4 * half
    choose = jnp.where(wanted == target, 1.0, 0.0).astype(BF)
    line = lax.broadcasted_iota(jnp.int32, (lines, 1), 0)

    @pl.when(half == 0)
    def _():
        total[...] = jnp.zeros_like(total)

    for clip in range(len(rows) - 1):
        blocks = [
            tokens_ref[core, clip, chip][:, lane * lines : (lane + 1) * lines]
            for chip in range(chips)
            for core in range(2)
            for lane in range(lanes)
        ]
        placed = dot(jnp.concatenate(blocks, axis=0), choose, 0, 0)
        for h in range(2):
            start, stop = rows[clip][4 * h], rows[clip + 1][4 * h]

            @pl.when(half == h)
            def _(start=start, stop=stop, placed=placed):
                total[start : start + lines] += jnp.where(line < stop - start, placed, 0.0)

    @pl.when(half == 1)
    def _():
        out_ref[...] = total[:count] + base_ref[...] if added else total[:count]


def put_positions(tokens, slot, count, lanes, lines, base=None):
    _, clips, chips, features, quarter = tokens.shape
    packed_width = features * 8
    rows = first_rows(slot, clips)
    assert all(len(set(row[:4])) == 1 and len(set(row[4:])) == 1 for row in rows)
    whole = pl.BlockSpec((count, packed_width), lambda h: (0, 0))
    in_specs = [pl.BlockSpec((2, clips, chips // 2, features, quarter), lambda h: (0, 0, h, 0, 0))]
    given = [tokens]
    if base is not None:
        in_specs, given = [whole] + in_specs, [base] + given
    last = max(max(row) for row in rows[:-1]) + lines
    return pl.pallas_call(
        functools.partial(put_body, rows, lanes, lines, base is not None),
        grid=(2,),
        in_specs=in_specs,
        out_specs=whole,
        out_shape=jax.ShapeDtypeStruct((count, packed_width), F32),
        scratch_shapes=[pltpu.VMEM((-(-last // 16) * 16, packed_width), F32)],
        compiler_params=pltpu.CompilerParams(vmem_limit_bytes=40 * 2**20),
        cost_estimate=pl.CostEstimate(
            flops=4 * count * packed_width**2, bytes_accessed=8 * count * packed_width, transcendentals=0
        ),
    )(*given)


def forward_body(query_ref, key_ref, value_ref, context_ref, wide_ref, weights_ref):
    scores = dot(key_ref[...], query_ref[...], 1, 1)
    top = jnp.max(scores, axis=0, keepdims=True)
    powers = jnp.exp2(scores - top)
    total = jnp.sum(powers, axis=0, keepdims=True)
    weights = (powers * (1.0 / total)).astype(BF)
    weights_ref[0] = weights
    context = dot(value_ref[...], weights, 0, 0).T
    context_ref[...] = context.astype(BF)
    wide_ref[...] = context


def attend(packed, heads, part):
    slots = packed.shape[0]
    block = slots // 2
    return pl.pallas_call(
        forward_body,
        grid=(heads,),
        in_specs=[
            pl.BlockSpec((block, PAD), lambda h: (part, h)),
            pl.BlockSpec((slots, PAD), lambda h: (0, heads + h)),
            pl.BlockSpec((slots, PAD), lambda h: (0, 2 * heads + h)),
        ],
        out_specs=[
            pl.BlockSpec((block, PAD), lambda h: (0, h)),
            pl.BlockSpec((block, PAD), lambda h: (0, h)),
            pl.BlockSpec((1, slots, block), lambda h: (h, 0, 0)),
        ],
        out_shape=[
            jax.ShapeDtypeStruct((block, heads * PAD), BF),
            jax.ShapeDtypeStruct((block, heads * PAD), F32),
            jax.ShapeDtypeStruct((heads, slots, block), BF),
        ],
        compiler_params=pltpu.CompilerParams(vmem_limit_bytes=50 * 2**20),
        cost_estimate=pl.CostEstimate(
            flops=heads * slots * slots * PAD * 6,
            bytes_accessed=heads * slots * slots,
            transcendentals=heads * slots * block,
        ),
    )(packed, packed, packed)


def backward_part(head_dim, query, key, value, grad, context, weights):
    wide = grad.astype(F32)
    inner = jnp.sum(wide * context, axis=1, keepdims=True)
    inner_high = inner.astype(BF).astype(F32)
    lane = lax.broadcasted_iota(jnp.int32, grad.shape, 1)
    extended = jnp.where(
        lane == head_dim,
        inner_high,
        jnp.where(lane == head_dim + 1, inner - inner_high, wide),
    ).astype(BF)
    centered = dot(value, extended, 1, 1)
    grad_scores = (weights.astype(F32) * centered).astype(BF)
    grad_value = dot(weights, grad, 1, 0)
    grad_key = dot(grad_scores, query, 1, 0)
    grad_query = (dot(key, grad_scores, 0, 0) * head_dim**-0.5).T
    return grad_query.astype(BF), grad_key, grad_value


def first_body(head_dim, query, key, value, grad, context, weights, query_out, key_out, value_out):
    query_out[...], key_out[...], value_out[...] = backward_part(
        head_dim, query[...], key[...], value[...], grad[...], context[...], weights[0]
    )


def second_body(
    head_dim, query, key, value, grad, context, weights, first_query, first_key, first_value, out_ref
):
    grad_query, grad_key, grad_value = backward_part(
        head_dim, query[...], key[...], value[...], grad[...], context[...], weights[0]
    )
    block = grad_query.shape[0]
    out_ref[0, :block] = first_query[...]
    out_ref[0, block:] = grad_query
    out_ref[1] = ((grad_key + first_key[...]) * LN2).astype(BF)
    out_ref[2] = (grad_value + first_value[...]).astype(BF)


def attend_back(packed, grad_context, context, weights, heads, head_dim, part, first=None):
    slots = packed.shape[0]
    block = slots // 2
    half = pl.BlockSpec((block, PAD), lambda h: (0, h))
    whole = pl.BlockSpec((slots, PAD), lambda h: (0, h))
    in_specs = [
        pl.BlockSpec((block, PAD), lambda h: (part, h)),
        pl.BlockSpec((slots, PAD), lambda h: (0, heads + h)),
        pl.BlockSpec((slots, PAD), lambda h: (0, 2 * heads + h)),
        half,
        half,
        pl.BlockSpec((1, slots, block), lambda h: (h, 0, 0)),
    ]
    given = [packed, packed, packed, grad_context, context, weights]
    if first is None:
        body = first_body
        out_specs = [half, whole, whole]
        out_shape = [
            jax.ShapeDtypeStruct((block, heads * PAD), BF),
            jax.ShapeDtypeStruct((slots, heads * PAD), F32),
            jax.ShapeDtypeStruct((slots, heads * PAD), F32),
        ]
    else:
        body = second_body
        in_specs += [half, whole, whole]
        given += first
        out_specs = pl.BlockSpec((3, slots, PAD), lambda h: (0, 0, h))
        out_shape = jax.ShapeDtypeStruct((3, slots, heads * PAD), BF)
    return pl.pallas_call(
        functools.partial(body, head_dim),
        grid=(heads,),
        in_specs=in_specs,
        out_specs=out_specs,
        out_shape=out_shape,
        compiler_params=pltpu.CompilerParams(vmem_limit_bytes=56 * 2**20),
        cost_estimate=pl.CostEstimate(
            flops=heads * slots * slots * PAD * 8,
            bytes_accessed=heads * slots * slots,
            transcendentals=0,
        ),
    )(*given)


def norm_forward(tensor, gain, shift):
    centered = tensor - jnp.mean(tensor, axis=1, keepdims=True)
    scale = lax.rsqrt(jnp.mean(centered * centered, axis=1, keepdims=True) + EPSILON)
    normal = centered * scale
    return normal, scale, (normal * gain + shift).astype(BF)


def norm_backward(grad, normal, scale, gain):
    weighted = grad * gain
    return scale * (
        weighted
        - jnp.mean(weighted, axis=1, keepdims=True)
        - normal * jnp.mean(weighted * normal, axis=1, keepdims=True)
    )


def local(
    inputs,
    lengths,
    cotangent,
    ln1_gain,
    ln1_bias,
    w_query,
    b_query,
    w_key,
    w_value,
    b_value,
    w_attn_out,
    b_attn_out,
    ln2_gain,
    ln2_bias,
    w_in,
    b_in,
    w_out,
    b_out,
):
    chips = size_of(GROUP)
    yl_size = lax.axis_size("yl")
    columns = 8 * yl_size
    k, zh, yh = (lax.axis_index(a) for a in ("k", "zh", "yh"))
    chip = lax.axis_index(GROUP)
    pack_count, packed_width = inputs.shape
    features = packed_width // 8
    width = features * columns
    clips = lengths.shape[0]
    slot = pack_count * 8 // clips
    group = 2 * chips
    lines = -(-(slot // 8 + 1) // 64) * 64
    lanes = 8 // group
    quarter = lanes * lines
    slots = 8 * lines
    half = slots // 2
    rows = w_query.shape[0]
    block_heads = HEADS // columns
    head_dim = width // HEADS
    split = block_heads % 2 == 0
    part_heads = block_heads // 2 if split else block_heads
    heads = 2 * block_heads
    units = w_in.shape[1]
    half_units = units // 2

    def start_of(clip, j):
        return (slot * clip - j + 7) // 8

    def order_tokens(own, other):
        ordered = jnp.stack(in_order([own, other], "k")).reshape(2, 2, 2, yl_size, features, quarter)
        return ordered.transpose(0, 2, 1, 3, 4, 5).reshape(columns, features, quarter)

    def exchange(blocks):
        return lax.all_to_all(blocks, ("zh", "zl", "yh", "yl"), 0, 0)

    def join(moved):
        return moved.reshape(width, quarter).T

    def cut(tensor):
        return tensor.T.reshape(columns, features, quarter)

    def by_core(tensor, parts):
        if not parts:
            return jnp.broadcast_to(tensor[None], (2,) + tensor.shape)
        return tensor.reshape((2, tensor.shape[0] // 2) + tensor.shape[1:])

    def double(part, axis):
        return part, swap(part, axis)

    def stacked(parts):
        return jnp.stack(parts)

    def arrange_heads(pieces):
        if not split:
            pieces = [lax.dynamic_slice_in_dim(p, k * (p.shape[0] // 2), p.shape[0] // 2, 0) for p in pieces]
        pieces = [p.reshape(-1, 4, part_heads * head_dim, 2 * rows) for p in pieces]
        block = (pieces[0].shape[0], 1) + pieces[0].shape[2:]
        return join_rows(
            pieces, pl.BlockSpec(block, lambda i: (0, i, 0, 0)), 4, heads * PAD, (part_heads, head_dim)
        )

    def arrange_units(pieces):
        return join_rows(pieces, pl.BlockSpec((half_units, 2 * rows), lambda i: (i, 0)), 4, half_units)

    full_vectors = jnp.stack([ln1_gain, ln1_bias, ln2_gain, ln2_bias, b_attn_out, b_out])
    part_vector = jnp.concatenate([b_query, b_value, b_in])
    full_count = full_vectors.shape[0]
    full_by = jnp.stack(in_order(pieces_of(full_vectors, GROUP), GROUP))
    all_lengths = jnp.concatenate(in_order(pieces_of(lengths, "k"), "k"))

    turned = [t.astype(BF).T for t in (w_query, w_key, w_value)] + [w_attn_out.astype(BF)]
    head_parts = jnp.stack([by_core(t, split) for t in turned], axis=1)
    head_parts = head_parts.reshape(2, 4 * part_heads * head_dim, rows)
    size = head_parts.shape[1]
    own_parts, other_parts = pick(head_parts, k, 0), swap(pick(head_parts, 1 - k, 0), "k")
    inputs_then, own_parts, full_by = sync(inputs, own_parts, full_by)
    full_size = full_by.size
    vector_pieces = pieces_of(jnp.concatenate([full_by.reshape(-1), part_vector]), "zh")
    taken = take_positions(inputs_then, slot, clips, lanes, lines)
    taken, vector_pieces = sync(taken, vector_pieces)
    full_by = jnp.stack(in_order([p[:full_size] for p in vector_pieces], "zh"))
    part_by = jnp.stack([p[full_size:] for p in vector_pieces])
    full_size = full_by.size
    vector_pieces = pieces_of(jnp.concatenate([full_by.reshape(-1), part_by.reshape(-1)]), "yh")
    own_tokens, other_tokens = pick(taken, k, 0), swap(pick(taken, 1 - k, 0), "k")
    head_shard = jnp.concatenate(in_order([own_parts, other_parts], "k"), axis=1)
    ordered, head_shard, vector_pieces = sync(order_tokens(own_tokens, other_tokens), head_shard, vector_pieces)
    head_pair = double(head_shard, "zh")
    moved = exchange(ordered)

    ordered, cotangent, w_in, w_out = sync(ordered, cotangent, w_in, w_out)
    unit_parts = jnp.stack([by_core(w_in.astype(BF).T, True), by_core(w_out.astype(BF), True)], axis=1)
    unit_parts = unit_parts.reshape(2, units, rows)
    own_parts, other_parts = pick(unit_parts, k, 0), swap(pick(unit_parts, 1 - k, 0), "k")
    own_parts, cotangent, head_pair = sync(own_parts, cotangent, head_pair)
    head_pair = double(stacked(head_pair), "yh")
    taken = take_positions(cotangent, slot, clips, lanes, lines)
    own_tokens, other_tokens = pick(taken, k, 0), swap(pick(taken, 1 - k, 0), "k")
    unit_shard = jnp.concatenate(in_order([own_parts, other_parts], "k"), axis=1)
    unit_shard = unit_shard.reshape(2, half_units, 2 * rows)
    ordered_grads = order_tokens(own_tokens, other_tokens)

    full_by = jnp.stack(in_order([p[:full_size] for p in vector_pieces], "yh"))
    part_by = jnp.stack([p[full_size:].reshape(part_by.shape) for p in vector_pieces]).reshape(4, -1)
    full_by = full_by.reshape(2, 2, 2, yl_size, full_count, features).transpose(4, 1, 2, 0, 3, 5)
    gain_one, shift_one, gain_two, shift_two, attn_shift, out_shift = full_by.reshape(full_count, 1, width)

    def head_vector(tensor):
        tensor = tensor.reshape(4, block_heads, head_dim)
        if split:
            tensor = pick(tensor.reshape(4, 2, part_heads, head_dim), k, 1)
        else:
            tensor = lax.dynamic_slice_in_dim(tensor, 2 * k, 2, 0)
        tensor = tensor.reshape(heads, head_dim)
        return jnp.pad(tensor, ((0, 0), (0, PAD - head_dim)))

    query_shift = head_vector(part_by[:, :features])
    value_shift = head_vector(part_by[:, features : 2 * features])
    unit_shift = pick(part_by[:, 2 * features :].reshape(4, 2, half_units), k, 1).reshape(-1)

    clip_length = pick(all_lengths, zh * 2 + yh, 0)

    def slots_of(part):
        j = part * lanes + jnp.repeat(jnp.arange(lanes), lines)
        return 8 * (start_of(yh, j) + jnp.tile(jnp.arange(lines), lanes)) + j - slot * yh

    own_valid = slots_of(chip * 2 + k) < clip_length
    slot_order = jnp.concatenate([slots_of((chip ^ d) * 2 + (k ^ c)) for d in range(chips) for c in range(2)])
    key_mask = jnp.where(slot_order < clip_length, 0.0, MASKED)

    lane = jnp.arange(PAD)[None, :]
    none = jnp.zeros((heads, PAD), F32)
    is_first = jnp.broadcast_to(lane == head_dim, (heads, PAD)).astype(F32)
    is_extra = jnp.broadcast_to((lane >= head_dim) & (lane < head_dim + 2), (heads, PAD)).astype(F32)
    qkv_shift = jnp.concatenate([query_shift, none, value_shift]).reshape(1, -1)
    qkv_scale = jnp.concatenate([none + head_dim**-0.5 * LOG2E, none + 1, none + 1]).reshape(1, -1)
    qkv_extra = jnp.concatenate([is_first, none, -is_extra]).reshape(1, -1)
    mask_lane = jnp.concatenate([none, is_first, none]).reshape(1, -1)

    def blocks_of(tensor):
        count = tensor.shape[0] // (2 * quarter)
        return [
            [tensor[(2 * d + c) * quarter : (2 * d + c + 1) * quarter] for c in range(2)]
            for d in range(count)
        ]

    moved, ordered_grads, unit_shard, gain_one, shift_one = sync(
        moved, ordered_grads, unit_shard, gain_one, shift_one
    )
    tokens = join(moved).astype(F32)
    normal_one, scale_one, normed_part = norm_forward(tokens, gain_one, shift_one)
    tokens, normal_one, scale_one, normed_part, head_pair = sync(
        tokens, normal_one, scale_one, normed_part, head_pair
    )
    normed_far = far_pieces(normed_part)
    head_pieces = pieces_of(stacked(head_pair).reshape(4 * size, 2 * rows), "x")
    in_pair = double(unit_shard[0], "zh")
    normed_near = with_core(normed_part)
    normed_near, in_pair = sync(normed_near, in_pair)
    in_pair = double(stacked(in_pair), "yh")
    out_pair = double(unit_shard[1], "zh")
    normed_near, normed_far, in_pair = sync(normed_near, normed_far, in_pair)
    in_pieces = pieces_of(stacked(in_pair).reshape(4 * half_units, 2 * rows), "x")
    head_pieces, normed_near, ordered_grads, out_pair = sync(head_pieces, normed_near, ordered_grads, out_pair)
    out_pair = double(stacked(out_pair), "yh")
    moved_grads = exchange(ordered_grads)
    head_weights = arrange_heads(head_pieces).reshape(4, heads * PAD, width)
    qkv_weights = head_weights[:3].reshape(3 * heads * PAD, width)
    attn_weights = head_weights[3]

    def qkv(rows_d, d):
        mask_d = key_mask[d * 2 * quarter : (d + 1) * 2 * quarter, None]
        product = (dot(rows_d, qkv_weights, 1, 1) + qkv_shift) * qkv_scale
        return (product + qkv_extra + mask_d * mask_lane).astype(BF)

    packed_near = qkv(normed_near, 0)
    normed_rows = [normed_near] + [with_core(v) for v in normed_far]
    packed = jnp.concatenate(
        [packed_near] + [qkv(v, d) for d, v in enumerate(normed_rows) if d], axis=0
    )
    far_context, far_wide, far_weights = attend(packed, heads, 1)

    def attn_product(v):
        return dot(v, attn_weights, 1, 0)

    near_chips = chips // 2
    far_sums = [cores_sum(attn_product, b).astype(BF) for b in blocks_of(far_context)]
    far_sums, packed, moved_grads = sync(far_sums, packed, moved_grads)
    far_total = send_far(far_sums) if near_chips == 1 else None
    near_context, near_wide, near_weights = attend(packed, heads, 0)
    grad_low = jnp.where(own_valid[:, None], join(moved_grads), jnp.zeros((quarter, width), BF))
    near_context, grad_low, far_total, out_pair = sync(near_context, grad_low, far_total, out_pair)
    out_pieces = pieces_of(stacked(out_pair).reshape(4 * half_units, 2 * rows), "x")
    near_sums = [cores_sum(attn_product, b) for b in blocks_of(near_context)]
    if near_chips > 1:
        far_total = send_far((near_sums + far_sums)[1:])
    near_sums, far_total, in_pieces = sync(near_sums, far_total, in_pieces)
    grad_far = far_pieces(grad_low)
    grad_near = with_core(grad_low)
    attn_part = near_sums[0] + far_total + attn_shift
    middle = tokens + attn_part
    normal_two, scale_two, normed_two_part = norm_forward(middle, gain_two, shift_two)
    normal_two, scale_two, normed_two_part, grad_near = sync(normal_two, scale_two, normed_two_part, grad_near)
    two_near = with_core(normed_two_part)
    two_far = far_pieces(normed_two_part)
    in_weights = arrange_units(in_pieces)

    def feed(rows_d):
        hidden = dot(rows_d, in_weights, 1, 1) + unit_shift
        below = 0.5 * (1.0 + lax.erf(hidden * 0.5**0.5))
        slope = below + hidden * (jnp.exp(-0.5 * hidden * hidden) * (0.5 / jnp.pi) ** 0.5)
        return (hidden * below).astype(BF), slope

    def feed_back(grad_d, slope):
        return (dot(grad_d, out_weights, 1, 1) * slope).astype(BF)

    near_active, near_slope = feed(two_near)
    near_active, near_slope, two_far = sync(near_active, near_slope, two_far)
    two_rows = [two_near] + [with_core(v) for v in two_far]
    far_feed = [feed(v) for v in two_rows[1:]]
    near_slope, far_feed, out_pieces, grad_far = sync(near_slope, far_feed, out_pieces, grad_far)
    out_weights = arrange_units(out_pieces)
    grad_rows = [grad_near] + [with_core(v) for v in grad_far]
    near_hidden = feed_back(grad_near, near_slope)
    grad_hidden = jnp.concatenate(
        [near_hidden] + [feed_back(g, f[1]) for g, f in zip(grad_rows[1:], far_feed)], axis=0
    )
    active = jnp.concatenate([near_active] + [f[0] for f in far_feed], axis=0)

    def in_product(v):
        return dot(v, in_weights, 1, 0)

    hidden_blocks = blocks_of(grad_hidden)
    far_two = [cores_sum(in_product, b).astype(BF) for b in hidden_blocks[1:]]
    grad_hidden, near_blocks, far_two, active = sync(grad_hidden, hidden_blocks[0], far_two, active)
    near_two = cores_sum(in_product, near_blocks)
    normed = jnp.concatenate(normed_rows, axis=0)
    normed_two = jnp.concatenate(two_rows, axis=0)
    grad_full = jnp.concatenate(grad_rows, axis=0)
    out_total = dot(active, grad_full, 0, 0).astype(BF)
    out_total, grad_hidden, near_two = sync(out_total, grad_hidden, near_two)
    out_half = send_units(out_total.reshape(2, -1, width), "yh")
    in_total = dot(grad_hidden, normed_two, 0, 0).astype(BF)
    in_total, near_two = sync(in_total, near_two)
    in_half = send_rows(in_total)
    grad_two = near_two + send_far(far_two)
    grad_out = grad_low.astype(F32)
    grad_middle = grad_out + norm_backward(grad_two, normal_two, scale_two, gain_two)
    grad_mid_part = grad_middle.astype(BF)
    grad_middle, grad_mid_part, active, grad_two = sync(grad_middle, grad_mid_part, active, grad_two)
    mid_far = far_pieces(grad_mid_part)
    mid_near = with_core(grad_mid_part)

    def context_grad(v):
        return dot(v, attn_weights, 1, 1).astype(BF)

    def out_product(v):
        return dot(v, out_weights, 1, 0)

    active_blocks = blocks_of(active)
    far_delta = [cores_sum(out_product, b).astype(BF) for b in active_blocks[1:]]
    near_delta = cores_sum(out_product, active_blocks[0])
    mid_half = jnp.concatenate([mid_near] + [with_core(v) for v in mid_far[: near_chips - 1]], axis=0)
    near_grad = context_grad(mid_half)
    near_grad, far_delta, near_delta = sync(near_grad, far_delta, near_delta)
    first = attend_back(packed, near_grad, near_wide, near_weights, heads, head_dim, 0)
    first, mid_far, out_half, in_half, far_delta = sync(first, mid_far, out_half, in_half, far_delta)
    delta_far = send_far(far_delta)
    out_half = send_rows(summed(out_half))
    in_half = send_units(summed(in_half).reshape(2, -1, 2 * rows), "yh")
    mid_rows = [mid_near] + [with_core(v) for v in mid_far]
    mid_full = jnp.concatenate(mid_rows, axis=0)
    far_grad = context_grad(mid_full[half:])
    grads = attend_back(packed, far_grad, far_wide, far_weights, heads, head_dim, 1, list(first))
    qkv_cube = qkv_weights.reshape(3, heads * PAD, width)

    def qkv_product(v):
        return sum(dot(v[j], qkv_cube[j], 1, 0) for j in range(3))

    grad_blocks = [
        [grads[:, (2 * d + c) * quarter : (2 * d + c + 1) * quarter] for c in range(2)] for d in range(chips)
    ]
    far_one = [cores_sum(qkv_product, b).astype(BF) for b in grad_blocks[1:]]
    grads, far_one, near_blocks, delta_far = sync(grads, far_one, grad_blocks[0], delta_far)
    far_arrived = send_far(far_one)
    near_one = cores_sum(qkv_product, near_blocks)
    delta = (attn_part + near_delta + delta_far + out_shift).astype(BF)
    moved_delta = exchange(cut(delta))

    def trim(total):
        return total.reshape(-1, part_heads, PAD, width)[:, :, :head_dim].reshape(-1, part_heads * head_dim, width)

    def head_chunk(totals):
        chunk = jnp.stack([trim(t) for t in totals], axis=1).reshape(-1, len(totals) * part_heads * head_dim, width)
        if not split:
            blank = jnp.zeros((4,) + chunk.shape[1:], BF)
            chunk = lax.dynamic_update_slice_in_dim(blank, chunk, 2 * k, 0)
        return chunk.reshape((2, 2) + chunk.shape[1:])

    context = jnp.concatenate([near_context, far_context], axis=0)
    query_key = head_chunk([dot(grads[j], normed, 0, 0).astype(BF) for j in range(2)])
    query_key, grads, near_one, far_arrived, out_half, in_half = sync(
        query_key, grads, near_one, far_arrived, out_half, in_half
    )
    grad_one = near_one + far_arrived
    grad_tokens = norm_backward(grad_one, normal_one, scale_one, gain_one)
    last_part = (grad_middle + grad_tokens).astype(BF)
    last_blocks, grad_one, moved_delta, query_key, grads, out_half, in_half = sync(
        cut(last_part), grad_one, moved_delta, query_key, grads, out_half, in_half
    )
    moved_last = exchange(last_blocks)
    query_key_half = send_rows(query_key)
    value_attn = head_chunk([dot(grads[2], normed, 0, 0).astype(BF), dot(context, mid_full, 0, 0).astype(BF)])
    value_attn, out_half, in_half, moved_delta = sync(value_attn, out_half, in_half, moved_delta)
    value_attn_half = send_units(value_attn, "yh")
    out_half = send_units(summed(out_half).reshape(2, -1, 2 * rows), "zh")
    in_half = send_units(summed(in_half).reshape(2, -1, 2 * rows), "zh")

    def two_cores(total, two):
        kept = lax.dynamic_slice_in_dim(total, k * rows, rows, 1)
        other = swap(lax.dynamic_slice_in_dim(total, (1 - k) * rows, rows, 1), "k")
        if not two:
            return kept.astype(F32) + other.astype(F32)
        return jnp.stack(in_order([kept, other], "k")).astype(F32)

    def kept_tokens(moved):
        moved = moved.reshape(2, 2, 2, yl_size, features, quarter).transpose(0, 2, 1, 3, 4, 5)
        kept = pick(moved, k, 0)
        other = swap(pick(moved, 1 - k, 0), "k")
        ordered = jnp.stack(in_order([kept, other], "k"))
        return ordered.reshape(2, clips, chips, features, quarter)

    def put(tokens, base=None):
        return put_positions(tokens, slot, pack_count, lanes, lines, base)

    layer_out = put(kept_tokens(moved_delta), inputs)
    layer_out, query_key_half, moved_last, grad_one = sync(layer_out, query_key_half, moved_last, grad_one)
    query_key_half = send_units(summed(query_key_half), "yh")
    input_grad = put(kept_tokens(moved_last))
    input_grad, value_attn_half, query_key_half, out_half, in_half = sync(
        input_grad, value_attn_half, query_key_half, out_half, in_half
    )
    value_attn_half = send_rows(summed(value_attn_half))
    query_key_half = send_units(summed(query_key_half), "zh")
    grad_out_w = two_cores(summed(out_half), True).reshape(units, rows)
    grad_in_w = two_cores(summed(in_half), True).reshape(units, rows).T
    grad_out_w, grad_in_w, value_attn_half = sync(grad_out_w, grad_in_w, value_attn_half)
    value_attn_half = send_units(summed(value_attn_half), "zh")
    head_parts = [
        two_cores(summed(t), split).reshape(-1, 2, part_heads * head_dim, rows)
        for t in (query_key_half, value_attn_half)
    ]
    grad_query_w, grad_key_w, grad_value_w, grad_attn_w = (
        t[:, j].reshape(features, rows) for t in head_parts for j in range(2)
    )

    full_sums = jnp.stack(
        [
            jnp.sum(v, axis=0)
            for v in (
                grad_one * normal_one,
                grad_one,
                grad_middle,
                grad_two * normal_two,
                grad_two,
                grad_out,
            )
        ]
    )

    def head_sums(tensor):
        total = jnp.sum(tensor.astype(F32), axis=0).reshape(-1, part_heads, PAD)[:, :, :head_dim]
        if not split:
            blank = jnp.zeros((4,) + total.shape[1:], F32)
            total = lax.dynamic_update_slice_in_dim(blank, total, 2 * k, 0)
        return total.reshape(4, -1)

    part_sums = jnp.concatenate(
        [
            head_sums(grads[0]),
            head_sums(grads[2]),
            jnp.sum(grad_hidden.astype(F32), axis=0).reshape(4, half_units),
        ],
        axis=1,
    )
    full_sums = full_sums.reshape(full_count, 2, 2, 2, yl_size, features).transpose(3, 1, 2, 4, 0, 5)
    full_size = full_sums.size
    flat = jnp.concatenate([full_sums.reshape(-1), part_sums.reshape(-1)])
    flat = sum(pieces_of(flat, "x"))
    full_flat, part_flat = flat[:full_size], flat[full_size:]
    for axis, index in (("yh", yh), ("zh", zh)):
        full_flat, part_flat = full_flat.reshape(2, -1), part_flat.reshape(2, -1)
        given = swap(jnp.concatenate([pick(full_flat, 1 - index, 0), part_flat[1]]), axis)
        cut_at = full_flat.shape[1]
        full_flat = pick(full_flat, index, 0) + given[:cut_at]
        part_flat = part_flat[0] + given[cut_at:]
    by_chip = full_flat.reshape(chips, -1)
    mine = pick(by_chip, chip, 0)
    for d in range(1, chips):
        mine = mine + swap(pick(by_chip, chip ^ d, 0), GROUP, d)
    own_size = mine.shape[0]
    last_pair = pieces_of(jnp.concatenate([mine, part_flat]), "k")
    vec_one_gain, vec_one_bias, vec_battn, vec_two_gain, vec_two_bias, vec_bout = (
        last_pair[0][:own_size] + last_pair[1][:own_size]
    ).reshape(full_count, features)
    head_size = part_heads * head_dim
    cores = in_order([p[own_size:] for p in last_pair], "k")
    if split:
        vec_bquery = jnp.concatenate([c[:head_size] for c in cores])
        vec_bvalue = jnp.concatenate([c[head_size : 2 * head_size] for c in cores])
    else:
        vec_bquery = cores[0][:head_size] + cores[1][:head_size]
        vec_bvalue = cores[0][head_size : 2 * head_size] + cores[1][head_size : 2 * head_size]
    vec_bin = jnp.concatenate([c[2 * head_size :] for c in cores])

    return (
        layer_out,
        input_grad,
        vec_one_gain,
        vec_one_bias,
        grad_query_w.T,
        vec_bquery,
        grad_key_w.T,
        grad_value_w.T,
        vec_bvalue,
        grad_attn_w,
        vec_battn,
        vec_two_gain,
        vec_two_bias,
        grad_in_w,
        vec_bin,
        grad_out_w,
        vec_bout,
    )


def solution(mesh):
    row_size, col_size = mesh.shape["row"], mesh.shape["col"]
    shape = (row_size // 2, 2, 2, 2, 2, col_size // 8)
    row, col = ("x", "k"), ("zh", "zl", "yh", "yl")
    grid = Mesh(mesh.devices.reshape(shape), row + col)
    return jax.shard_map(
        local,
        mesh=grid,
        in_specs=(
            P(row, col),
            P(row),
            P(row, col),
            P(col),
            P(col),
            P(row, col),
            P(col),
            P(row, col),
            P(row, col),
            P(col),
            P(col, row),
            P(col),
            P(col),
            P(col),
            P(row, col),
            P(col),
            P(col, row),
            P(col),
        ),
        out_specs=(
            P(row, col),
            P(row, col),
            P(col),
            P(col),
            P(row, col),
            P(col),
            P(row, col),
            P(row, col),
            P(col),
            P(col, row),
            P(col),
            P(col),
            P(col),
            P(row, col),
            P(col),
            P(col, row),
            P(col),
        ),
        check_vma=False,
    )
```

time: 827 us -> 609 us (0.74)
  waiting for transfers between devices: 342 us -> 205 us
  local copies, waits for them, and re-layouts: 129 us -> 68.3 us
  starting transfers between devices: 130 us -> 70.4 us
  Pallas kernels: 45.6 us -> 73.4 us
  matrix products: 83.4 us -> 111 us
  other arithmetic: 85 us -> 73.7 us
    ppermute x67 -> x64, waiting for transfers between devices: 321 us -> 178 us  [swap(): lax.ppermute(tensor, axis, [(i, i ^ step) for i in range(size_of(axis))])]
    ppermute x67 -> x64, starting transfers between devices: 102 us -> 54 us  [swap(): lax.ppermute(tensor, axis, [(i, i ^ step) for i in range(size_of(axis))])]
    pallas_call x2 -> x11, Pallas kernels: 45.6 us -> 73.4 us  [the longest x2 28.1 us: attend_back(): pl.pallas_call(functools.partial(body, head_dim), grid=(heads,), in_specs...]
    dot_general x25 -> x38, matrix products: 83.4 us -> 111 us  [dot(): lax.dot_general(first, second, (((left,), (right,)), ((), ())), preferred...]
    convert_element_type x14 -> x1, local copies, waits for them, and re-layouts: 19.9 us -> 0.56 us  [local(): tokens = join(moved).astype(F32)]
    concatenate x5 -> x4, local copies, waits for them, and re-layouts: 16.1 us -> 3.66 us  [the longest x1 2.27 us: local(): normed = jnp.concatenate(normed_rows, axis=0)]
    all_to_all x4, starting transfers between devices: 28.2 us -> 16.4 us  [exchange(): return lax.all_to_all(blocks, ('zh', 'zl', 'yh', 'yl'), 0, 0)]
    unnamed x160 -> x136, local copies, waits for them, and re-layouts: 26.3 us -> 18.2 us
  transfers between devices with their start and end apart: 71 -> 68, of which waited for: 18 -> 31; matrix products, arithmetic and copies ran while one was open for 32% -> 35% of each run, Pallas kernels for 6% -> 12%
where the time goes in v2:
time: 609 us; the launch traced here: 604 us
  waiting for transfers between devices  205 us (34%)
  matrix products  111 us (18%)
  other arithmetic  73.7 us (12%)
  Pallas kernels  73.4 us (12%)
  starting transfers between devices  70.4 us (12%)
  local copies, waits for them, and re-layouts  68.3 us (11%)
    ppermute x64, waiting for transfers between devices, swap(): lax.ppermute(tensor, axis, [(i, i ^ step) for i in range(size_of(axis))])  178 us
    dot_general x38, matrix products, dot(): lax.dot_general(first, second, (((left,), (right,)), ((), ())), preferred...  111 us
    ppermute x64, starting transfers between devices, swap(): lax.ppermute(tensor, axis, [(i, i ^ step) for i in range(size_of(axis))])  54 us
    pallas_call x2, Pallas kernels, attend_back(): pl.pallas_call(functools.partial(body, head_dim), grid=(heads,), in_specs...  28.1 us
    all_to_all x4, waiting for transfers between devices, exchange(): return lax.all_to_all(blocks, ('zh', 'zl', 'yh', 'yl'), 0, 0)  27 us
    pallas_call x2, Pallas kernels, attend(): pl.pallas_call(forward_body, grid=(heads,), in_specs=[pl.BlockSpec((block...  22.9 us
    unnamed x136, local copies, waits for them, and re-layouts  18.2 us
    all_to_all x4, starting transfers between devices, exchange(): return lax.all_to_all(blocks, ('zh', 'zl', 'yh', 'yl'), 0, 0)  16.4 us
  transfers between devices with their start and end apart: 68, of which 31 were waited for; matrix products, arithmetic and copies ran while one was open for 35% of the time, Pallas kernels for 12%

profile of v2, /device:TPU:0, one launch (start us, length us, event | category | flops | bytes accessed | tf_op | source)
XLA Modules:
  0.0 604.4 jit_solution(14626457228816039283)
XLA Ops:
  37.9 28.6 %collective-permute-done.5 = bf16[320,640]{1,0:T(8,128)(2,1)S(1)} collective-permute-done((bf16[320,640]{1,0:T(8,128)(2,1)S(1)}, bf16[320,640]{1,0:T(8,128)(2,1)S(1)}, u32[]{:S(2)}, u32[]{:S(2)}) %collective-permute-start.5) | collective-permute-done | bytes 409632 | tf_op jit(solution)/shard_map/ppermute | solution.py:39
  83.1 14.1 %collective-permute-done.8 = bf16[2,320,640]{2,1,0:T(8,128)(2,1)} collective-permute-done((bf16[2,320,640]{2,1,0:T(8,128)(2,1)}, bf16[2,320,640]{2,1,0:T(8,128)(2,1)}, u32[]{:S(2)}, u32[]{:S(2)}) %collective-permute-start.8) | collective-permute-done | bytes 819232 | tf_op jit(solution)/shard_map/ppermute | solution.py:39
  107.9 14.6 %collective-permute-done.11 = bf16[320,640]{1,0:T(8,128)(2,1)S(1)} collective-permute-done((bf16[320,640]{1,0:T(8,128)(2,1)S(1)}, bf16[320,640]{1,0:T(8,128)(2,1)S(1)}, u32[]{:S(2)}, u32[]{:S(2)}) %collective-permute-start.11) | collective-permute-done | bytes 409632 | tf_op jit(solution)/shard_map/ppermute | solution.py:39
  127.1 13.9 %collective-permute-done.12 = bf16[384,1280]{1,0:T(8,128)(2,1)} collective-permute-done((bf16[384,1280]{1,0:T(8,128)(2,1)}, bf16[384,1280]{1,0:T(8,128)(2,1)}, u32[]{:S(2)}, u32[]{:S(2)}) %collective-permute-start.12) | collective-permute-done | bytes 983072 | tf_op jit(solution)/shard_map/ppermute | solution.py:39
  148.0 4.5 all-to-all-start.1
  157.7 4.9 add_convert_fusion
  165.1 11.5 %shard_map.308 = (bf16[768,512]{1,0:T(8,128)(2,1)S(1)}, f32[768,512]{1,0:T(8,128)S(1)}, bf16[4,1536,768]{2,1,0:T(8,128)(2,1)}) custom-call(bf16[1536,1536]{1,0:T(8,128)(2,1)} %pad_maximum_fusion.query_ref.key_ref.value_ref.query.key.value, bf16[1536,1536]{1,0:T(8,128)(2,1)} %pad_maximum_fusion.query_ref.key_ref.value_ref.query.key.value, ...), custom_call_target="tpu_custom_call" | custom-call | flops 7247757312 | bytes 9437184 | tf_op jit(solution)/shard_map/pallas_call | solution.py:269
  187.1 11.4 %shard_map.309 = (bf16[768,512]{1,0:T(8,128)(2,1)S(1)}, f32[768,512]{1,0:T(8,128)S(1)}, bf16[4,1536,768]{2,1,0:T(8,128)(2,1)}) custom-call(bf16[1536,1536]{1,0:T(8,128)(2,1)} %pad_maximum_fusion.query_ref.key_ref.value_ref.query.key.value, bf16[1536,1536]{1,0:T(8,128)(2,1)} %pad_maximum_fusion.query_ref.key_ref.value_ref.query.key.value, ...), custom_call_target="tpu_custom_call" | custom-call | flops 7247757312 | bytes 9437184 | tf_op jit(solution)/shard_map/pallas_call | solution.py:269
  229.2 7.0 %fusion.3 = (f32[768,1280]{1,0:T(8,128)}, bf16[768,1280]{1,0:T(8,128)(2,1)}) fusion(f32[1280]{0:T(1024)S(1)} %add.520, bf16[1280,1280]{1,0:T(8,128)(2,1)S(1)} %shard_map.310, bf16[384,1280]{1,0:T(8,128)(2,1)} %collective-permute-done.23, bf16[384,1280]{1,0:T(8,128)(2,1)} %get-tuple-element.215), kind=kOutput, calls=%fused_computation.13 | convolution fusion | flops 2531328000 | bytes 11146240 | tf_op jit(solution)/shard_map/dot_general | solution.py:22
  236.2 14.6 %collective-permute-done.24 = bf16[384,1280]{1,0:T(8,128)(2,1)} collective-permute-done((bf16[384,1280]{1,0:T(8,128)(2,1)}, bf16[384,1280]{1,0:T(8,128)(2,1)}, u32[]{:S(2)}, u32[]{:S(2)}) %collective-permute-start.24) | collective-permute-done | bytes 983072 | tf_op jit(solution)/shard_map/ppermute | solution.py:39
  263.4 6.4 %fusion.7 = (f32[768,1280]{1,0:T(8,128)S(1)}, bf16[768,1280]{1,0:T(8,128)(2,1)S(1)}) fusion(f32[1280]{0:T(1024)S(1)} %add.520, bf16[1280,1280]{1,0:T(8,128)(2,1)} %copy-done.1, bf16[384,1280]{1,0:T(8,128)(2,1)} %collective-permute-done.25, bf16[384,1280]{1,0:T(8,128)(2,1)} %collective-permute-done.24), kind=kOutput, calls=%fused_computation.17 | convolution fusion | flops 2531328000 | bytes 11146240 | tf_op jit(solution)/shard_map/dot_general | solution.py:22
  269.8 14.0 %collective-permute-done.27 = bf16[384,1280]{1,0:T(8,128)(2,1)} collective-permute-done((bf16[384,1280]{1,0:T(8,128)(2,1)}, bf16[384,1280]{1,0:T(8,128)(2,1)}, u32[]{:S(2)}, u32[]{:S(2)}) %collective-permute-start.27) | collective-permute-done | bytes 983072 | tf_op jit(solution)/shard_map/ppermute | solution.py:39
  283.8 6.8 %collective-permute-done.26.refs_1_ = bf16[1280,640]{1,0:T(8,128)(2,1)S(1)} collective-permute-done((bf16[1280,640]{1,0:T(8,128)(2,1)S(1)}, bf16[1280,640]{1,0:T(8,128)(2,1)S(1)}, u32[]{:S(2)}, u32[]{:S(2)}) %collective-permute-start.26) | collective-permute-done | bytes 1638432 | tf_op jit(solution)/shard_map/ppermute | solution.py:39
  310.9 7.1 %convolution_convert_fusion.1 = bf16[1280,1280]{1,0:T(8,128)(2,1)S(1)} fusion(bf16[1536,1280]{1,0:T(8,128)(2,1)S(1)} %pad_maximum_fusion.2, bf16[384,1280]{1,0:T(8,128)(2,1)S(1)} %collective-permute-done.28, bf16[384,1280]{1,0:T(8,128)(2,1)} %collective-permute-done.27, bf16[768,1280]{1,0:T(8,128)(2,1)S(1)} %copy-done.40), kind=kOutput, calls=%fused_computation.2 | convolution fusion | flops 5046599680 | bytes 11141120 | tf_op jit(solution)/shard_map/dot_general | solution.py:22
  319.5 7.6 %convolution_convert_fusion = bf16[1280,1280]{1,0:T(8,128)(2,1)S(1)} fusion(bf16[1536,1280]{1,0:T(8,128)(2,1)S(1)} %pad_maximum_fusion.1, bf16[384,1280]{1,0:T(8,128)(2,1)} %collective-permute-done.25, bf16[384,1280]{1,0:T(8,128)(2,1)} %collective-permute-done.24, bf16[384,1280]{1,0:T(8,128)(2,1)} %collective-permute-done.23, ...), kind=kOutput, calls=%fused_computation.1 | convolution fusion | flops 5050531840 | bytes 11141120 | tf_op jit(solution)/shard_map/dot_general | solution.py:22
  327.1 6.1 %collective-permute-done.31 = bf16[384,1280]{1,0:T(8,128)(2,1)S(1)} collective-permute-done((bf16[384,1280]{1,0:T(8,128)(2,1)S(1)}, bf16[384,1280]{1,0:T(8,128)(2,1)S(1)}, u32[]{:S(2)}, u32[]{:S(2)}) %collective-permute-start.31) | collective-permute-done | bytes 983072 | tf_op jit(solution)/shard_map/ppermute | solution.py:39
  351.3 4.5 fusion.36
  355.8 4.3 convolution_add_fusion.11
  363.7 13.6 %shard_map.312 = (bf16[768,512]{1,0:T(8,128)(2,1)}, f32[1536,512]{1,0:T(8,128)}, f32[1536,512]{1,0:T(8,128)}) custom-call(bf16[1536,1536]{1,0:T(8,128)(2,1)} %pad_maximum_fusion.query_ref.key_ref.value_ref.query.key.value, bf16[1536,1536]{1,0:T(8,128)(2,1)} %pad_maximum_fusion.query_ref.key_ref.value_ref.query.key.value, ...), custom_call_target="tpu_custom_call" | custom-call | flops 9663676416 | bytes 9437184 | tf_op jit(solution)/shard_map/pallas_call | solution.py:361
  377.3 7.0 %collective-permute-done.36 = bf16[640,1280]{1,0:T(8,128)(2,1)} collective-permute-done((bf16[640,1280]{1,0:T(8,128)(2,1)}, bf16[640,1280]{1,0:T(8,128)(2,1)}, u32[]{:S(2)}, u32[]{:S(2)}) %collective-permute-start.36) | collective-permute-done | bytes 1638432 | tf_op jit(solution)/shard_map/ppermute | solution.py:39
  406.1 14.5 %shard_map.313 = bf16[3,1536,512]{2,1,0:T(8,128)(2,1)} custom-call(bf16[1536,1536]{1,0:T(8,128)(2,1)} %pad_maximum_fusion.query_ref.key_ref.value_ref.query.key.value, bf16[1536,1536]{1,0:T(8,128)(2,1)} %pad_maximum_fusion.query_ref.key_ref.value_ref.query.key.value, bf16[1536,1536]{1,0:T(8,128)(2,1)} %pad_maximum_fusion.query_ref.key_ref.value_ref.query.key.value, ...), custom_call_target="tpu_custom_call" | custom-call | flops 9663676416 | bytes 9437184 | tf_op jit(solution)/shard_map/pallas_call | solution.py:361
  434.5 4.5 convolution_convert_fusion.3
  439.6 4.4 convolution_convert_fusion.4
  449.8 4.6 all-to-all-start.2
  464.9 14.4 %all-to-all-done.2 = bf16[8,160,384]{2,1,0:T(8,128)(2,1)} async-done(((bf16[8,160,384]{2,1,0:T(8,128)(2,1)}), bf16[8,160,384]{2,1,0:T(8,128)(2,1)}, u32[]{:S(2)}, u32[]{:S(2)}) %all-to-all-start.2) | async-done | bytes 983072 | tf_op jit(solution)/shard_map/all_to_all | solution.py:445
  479.3 4.8 convolution_convert_fusion.2
  510.9 6.4 %shard_map.314 = f32[375,1280]{1,0:T(8,128)} custom-call(f32[375,1280]{1,0:T(8,128)S(1)} %copy-done.11, bf16[2,2,2,160,384]{4,3,2,1,0:T(8,128)(2,1)S(1)} %maximum_bitcast_fusion.2.refs_1_), custom_call_target="tpu_custom_call" | custom-call | flops 2457600000 | bytes 3840000 | tf_op jit(solution)/shard_map/pallas_call | solution.py:240
  517.3 12.6 %all-to-all-done.3 = bf16[8,160,384]{2,1,0:T(8,128)(2,1)S(1)} async-done(((bf16[8,160,384]{2,1,0:T(8,128)(2,1)}), bf16[8,160,384]{2,1,0:T(8,128)(2,1)S(1)}, u32[]{:S(2)}, u32[]{:S(2)}) %all-to-all-start.3) | async-done | bytes 983072 | tf_op jit(solution)/shard_map/all_to_all | solution.py:445
  544.2 11.7 %collective-permute-done.54 = f32[2400]{0:T(1024)S(1)} collective-permute-done((f32[2400]{0:T(1024)S(1)}, f32[2400]{0:T(1024)S(1)}, u32[]{:S(2)}, u32[]{:S(2)}) %collective-permute-start.54) | collective-permute-done | bytes 9632 | tf_op jit(solution)/shard_map/ppermute | solution.py:39
  565.6 6.6 %shard_map.315 = f32[375,1280]{1,0:T(8,128)} custom-call(bf16[2,2,2,160,384]{4,3,2,1,0:T(8,128)(2,1)S(1)} %maximum_bitcast_fusion.3.refs_0_), custom_call_target="tpu_custom_call" | custom-call | flops 2457600000 | bytes 3840000 | tf_op jit(solution)/shard_map/pallas_call | solution.py:240
  579.0 5.0 collective-permute-done.57
  592.2 8.7 %collective-permute-done.62 = bf16[160,640]{1,0:T(8,128)(2,1)S(1)} collective-permute-done((bf16[160,640]{1,0:T(8,128)(2,1)S(1)}, bf16[160,640]{1,0:T(8,128)(2,1)S(1)}, u32[]{:S(2)}, u32[]{:S(2)}) %collective-permute-start.62) | collective-permute-done | bytes 204832 | tf_op jit(solution)/shard_map/ppermute | solution.py:39
  (541 shorter events, 301.1 us)
Async XLA Ops:
  9.5 88.1 %collective-permute-start.15 = (s32[2]{0:T(128)S(1)}, s32[2]{0:T(128)S(1)}, u32[]{:S(2)}, u32[]{:S(2)}) collective-permute-start(s32[2]{0:T(128)S(1)} %copy-done.57), channel_id=1, source_target_pairs={{0,8},{8,0},{1,9},{9,1},{2,10},{10,2},{3,11},{11,3},{4,12},{12,4},... | collective-permute-start | bytes 32 | tf_op jit(solution)/shard_map/ppermute | solution.py:39
  20.9 58.9 %all-to-all-start = ((bf16[8,160,384]{2,1,0:T(8,128)(2,1)}), bf16[8,160,384]{2,1,0:T(8,128)(2,1)S(1)}, u32[]{:S(2)}, u32[]{:S(2)}) async-start(bf16[8,160,384]{2,1,0:T(8,128)(2,1)} %bitcast.23), calls=%async_computation | async-start | bytes 1966080 | tf_op jit(solution)/shard_map/all_to_all | solution.py:445
  34.6 31.9 %collective-permute-start.5 = (bf16[320,640]{1,0:T(8,128)(2,1)S(1)}, bf16[320,640]{1,0:T(8,128)(2,1)S(1)}, u32[]{:S(2)}, u32[]{:S(2)}) collective-permute-start(bf16[320,640]{1,0:T(8,128)(2,1)S(1)} %pad_maximum_fusion.18), channel_id=1, source_target_pairs={{0,4},{4,0},{1,5},{5,1},{2,6},{6,2},{3,7},{7,3},{8,12},{12,8},{9,1... | collective-permute-start | bytes 1228808 | tf_op jit(solution)/shard_map/ppermute | solution.py:39
  37.4 34.3 %collective-permute-start.7 = (bf16[640,320]{0,1:T(8,128)(2,1)}, bf16[640,320]{0,1:T(8,128)(2,1)}, u32[]{:S(2)}, u32[]{:S(2)}) collective-permute-start(bf16[640,320]{0,1:T(8,128)(2,1)} %get-tuple-element.450), channel_id=1, source_target_pairs={{0,8},{8,0},{1,9},{9,1},{2,10},{10,2},{3,11},{11,3},{4,12},{12,4},... | collective-permute-start | bytes 1228808 | tf_op jit(solution)/shard_map/ppermute | solution.py:39
  76.2 21.0 %collective-permute-start.8 = (bf16[2,320,640]{2,1,0:T(8,128)(2,1)}, bf16[2,320,640]{2,1,0:T(8,128)(2,1)}, u32[]{:S(2)}, u32[]{:S(2)}) collective-permute-start(bf16[2,320,640]{2,1,0:T(8,128)(2,1)} %pad_maximum_fusion.12), channel_id=1, source_target_pairs={{0,1},{1,0},{2,3},{3,2},{4,5},{5,4},{6,7},{7,6},{8,9},{9,8},{10,11... | collective-permute-start | bytes 2457608 | tf_op jit(solution)/shard_map/ppermute | solution.py:39
  99.2 48.7 %collective-permute-start.9 = (bf16[1280,640]{1,0:T(8,128)(2,1)S(1)}, bf16[1280,640]{1,0:T(8,128)(2,1)S(1)}, u32[]{:S(2)}, u32[]{:S(2)}) collective-permute-start(bf16[1280,640]{1,0:T(8,128)(2,1)S(1)} %bitcast.325), channel_id=1, source_target_pairs={{0,16},{16,0},{1,17},{17,1},{2,18},{18,2},{3,19},{19,3},{4,20},{20... | collective-permute-start | bytes 4915208 | tf_op jit(solution)/shard_map/ppermute | solution.py:39
  103.4 37.6 %collective-permute-start.12 = (bf16[384,1280]{1,0:T(8,128)(2,1)}, bf16[384,1280]{1,0:T(8,128)(2,1)}, u32[]{:S(2)}, u32[]{:S(2)}) collective-permute-start(bf16[384,1280]{1,0:T(8,128)(2,1)} %get-tuple-element.186), channel_id=1, source_target_pairs={{0,2},{2,0},{1,3},{3,1},{4,6},{6,4},{5,7},{7,5},{8,10},{10,8},{9,1... | collective-permute-start | bytes 2949128 | tf_op jit(solution)/shard_map/ppermute | solution.py:39
  123.5 20.4 %collective-permute-start.13 = (bf16[2,320,640]{2,1,0:T(8,128)(2,1)}, bf16[2,320,640]{2,1,0:T(8,128)(2,1)}, u32[]{:S(2)}, u32[]{:S(2)}) collective-permute-start(bf16[2,320,640]{2,1,0:T(8,128)(2,1)} %pad_maximum_fusion.13), channel_id=1, source_target_pairs={{0,1},{1,0},{2,3},{3,2},{4,5},{5,4},{6,7},{7,6},{8,9},{9,8},{10,11... | collective-permute-start | bytes 2457608 | tf_op jit(solution)/shard_map/ppermute | solution.py:39
  126.8 21.2 %collective-permute-start.14 = (bf16[320,640]{1,0:T(8,128)(2,1)}, bf16[320,640]{1,0:T(8,128)(2,1)}, u32[]{:S(2)}, u32[]{:S(2)}) collective-permute-start(bf16[320,640]{1,0:T(8,128)(2,1)} %get-tuple-element.203), channel_id=1, source_target_pairs={{0,4},{4,0},{1,5},{5,1},{2,6},{6,2},{3,7},{7,3},{8,12},{12,8},{9,1... | collective-permute-start | bytes 1228808 | tf_op jit(solution)/shard_map/ppermute | solution.py:39
  148.0 37.7 %all-to-all-start.1 = ((bf16[8,160,384]{2,1,0:T(8,128)(2,1)}), bf16[8,160,384]{2,1,0:T(8,128)(2,1)}, u32[]{:S(2)}, u32[]{:S(2)}) async-start(bf16[8,160,384]{2,1,0:T(8,128)(2,1)} %bitcast.335), calls=%async_computation.1 | async-start | bytes 1966080 | tf_op jit(solution)/shard_map/all_to_all | solution.py:445
  179.9 31.7 %collective-permute-start.19 = (bf16[2,320,640]{2,1,0:T(8,128)(2,1)}, bf16[2,320,640]{2,1,0:T(8,128)(2,1)}, u32[]{:S(2)}, u32[]{:S(2)}) collective-permute-start(bf16[2,320,640]{2,1,0:T(8,128)(2,1)} %pad_maximum_fusion.14), channel_id=1, source_target_pairs={{0,1},{1,0},{2,3},{3,2},{4,5},{5,4},{6,7},{7,6},{8,9},{9,8},{10,11... | collective-permute-start | bytes 2457608 | tf_op jit(solution)/shard_map/ppermute | solution.py:39
  183.4 37.5 %collective-permute-start.21 = (bf16[1280,640]{1,0:T(8,128)(2,1)S(1)}, bf16[1280,640]{1,0:T(8,128)(2,1)S(1)}, u32[]{:S(2)}, u32[]{:S(2)}) collective-permute-start(bf16[1280,640]{1,0:T(8,128)(2,1)S(1)} %bitcast.327), channel_id=1, source_target_pairs={{0,16},{16,0},{1,17},{17,1},{2,18},{18,2},{3,19},{19,3},{4,20},{20... | collective-permute-start | bytes 4915208 | tf_op jit(solution)/shard_map/ppermute | solution.py:39
  185.6 23.4 %collective-permute-start.18 = (bf16[384,1280]{1,0:T(8,128)(2,1)}, bf16[384,1280]{1,0:T(8,128)(2,1)}, u32[]{:S(2)}, u32[]{:S(2)}) collective-permute-start(bf16[384,1280]{1,0:T(8,128)(2,1)} %add_convert_fusion.8), channel_id=1, source_target_pairs={{0,2},{2,0},{1,3},{3,1},{4,6},{6,4},{5,7},{7,5},{8,10},{10,8},{9,1... | collective-permute-start | bytes 2949128 | tf_op jit(solution)/shard_map/ppermute | solution.py:39
  226.3 24.5 %collective-permute-start.24 = (bf16[384,1280]{1,0:T(8,128)(2,1)}, bf16[384,1280]{1,0:T(8,128)(2,1)}, u32[]{:S(2)}, u32[]{:S(2)}) collective-permute-start(bf16[384,1280]{1,0:T(8,128)(2,1)} %get-tuple-element.215), channel_id=1, source_target_pairs={{0,2},{2,0},{1,3},{3,1},{4,6},{6,4},{5,7},{7,5},{8,10},{10,8},{9,1... | collective-permute-start | bytes 2949128 | tf_op jit(solution)/shard_map/ppermute | solution.py:39
  252.3 38.3 %collective-permute-start.26 = (bf16[1280,640]{1,0:T(8,128)(2,1)S(1)}, bf16[1280,640]{1,0:T(8,128)(2,1)S(1)}, u32[]{:S(2)}, u32[]{:S(2)}) collective-permute-start(bf16[1280,640]{1,0:T(8,128)(2,1)S(1)} %bitcast.323), channel_id=1, source_target_pairs={{0,16},{16,0},{1,17},{17,1},{2,18},{18,2},{3,19},{19,3},{4,20},{20... | collective-permute-start | bytes 4915208 | tf_op jit(solution)/shard_map/ppermute | solution.py:39
  259.6 24.2 %collective-permute-start.27 = (bf16[384,1280]{1,0:T(8,128)(2,1)}, bf16[384,1280]{1,0:T(8,128)(2,1)}, u32[]{:S(2)}, u32[]{:S(2)}) collective-permute-start(bf16[384,1280]{1,0:T(8,128)(2,1)} %select_bitcast_fusion), channel_id=1, source_target_pairs={{0,2},{2,0},{1,3},{3,1},{4,6},{6,4},{5,7},{7,5},{8,10},{10,8},{9,1... | collective-permute-start | bytes 2949128 | tf_op jit(solution)/shard_map/ppermute | solution.py:39
  309.4 23.8 %collective-permute-start.31 = (bf16[384,1280]{1,0:T(8,128)(2,1)S(1)}, bf16[384,1280]{1,0:T(8,128)(2,1)S(1)}, u32[]{:S(2)}, u32[]{:S(2)}) collective-permute-start(bf16[384,1280]{1,0:T(8,128)(2,1)S(1)} %fusion.35), channel_id=1, source_target_pairs={{0,2},{2,0},{1,3},{3,1},{4,6},{6,4},{5,7},{7,5},{8,10},{10,8},{9,1... | collective-permute-start | bytes 2949128 | tf_op jit(solution)/shard_map/ppermute | solution.py:39
  342.2 35.1 %collective-permute-start.35 = (bf16[384,1280]{1,0:T(8,128)(2,1)}, bf16[384,1280]{1,0:T(8,128)(2,1)}, u32[]{:S(2)}, u32[]{:S(2)}) collective-permute-start(bf16[384,1280]{1,0:T(8,128)(2,1)} %get-tuple-element.240), channel_id=1, source_target_pairs={{0,2},{2,0},{1,3},{3,1},{4,6},{6,4},{5,7},{7,5},{8,10},{10,8},{9,1... | collective-permute-start | bytes 2949128 | tf_op jit(solution)/shard_map/ppermute | solution.py:39
  346.1 38.2 %collective-permute-start.36 = (bf16[640,1280]{1,0:T(8,128)(2,1)}, bf16[640,1280]{1,0:T(8,128)(2,1)}, u32[]{:S(2)}, u32[]{:S(2)}) collective-permute-start(bf16[640,1280]{1,0:T(8,128)(2,1)} %get-tuple-element.411), channel_id=1, source_target_pairs={{0,1},{1,0},{2,3},{3,2},{4,5},{5,4},{6,7},{7,6},{8,9},{9,8},{10,11... | collective-permute-start | bytes 4915208 | tf_op jit(solution)/shard_map/ppermute | solution.py:39
  350.0 38.0 %collective-permute-start.37 = (bf16[1280,640]{1,0:T(8,128)(2,1)}, bf16[1280,640]{1,0:T(8,128)(2,1)}, u32[]{:S(2)}, u32[]{:S(2)}) collective-permute-start(bf16[1280,640]{1,0:T(8,128)(2,1)} %get-tuple-element.409), channel_id=1, source_target_pairs={{0,16},{16,0},{1,17},{17,1},{2,18},{18,2},{3,19},{19,3},{4,20},{20... | collective-permute-start | bytes 4915208 | tf_op jit(solution)/shard_map/ppermute | solution.py:39
  388.1 37.5 %collective-permute-start.40 = (bf16[384,1280]{1,0:T(8,128)(2,1)}, bf16[384,1280]{1,0:T(8,128)(2,1)S(1)}, u32[]{:S(2)}, u32[]{:S(2)}) collective-permute-start(bf16[384,1280]{1,0:T(8,128)(2,1)} %fusion.36), channel_id=1, source_target_pairs={{0,2},{2,0},{1,3},{3,1},{4,6},{6,4},{5,7},{7,5},{8,10},{10,8},{9,1... | collective-permute-start | bytes 2949128 | tf_op jit(solution)/shard_map/ppermute | solution.py:39
  391.6 69.6 %collective-permute-start.43 = (bf16[640,640]{1,0:T(8,128)(2,1)}, bf16[640,640]{1,0:T(8,128)(2,1)}, u32[]{:S(2)}, u32[]{:S(2)}) collective-permute-start(bf16[640,640]{1,0:T(8,128)(2,1)} %get-tuple-element.423), channel_id=1, source_target_pairs={{0,16},{16,0},{1,17},{17,1},{2,18},{18,2},{3,19},{19,3},{4,20},{20... | collective-permute-start | bytes 2457608 | tf_op jit(solution)/shard_map/ppermute | solution.py:39
  396.0 65.2 %collective-permute-start.44 = (bf16[640,640]{1,0:T(8,128)(2,1)}, bf16[640,640]{1,0:T(8,128)(2,1)}, u32[]{:S(2)}, u32[]{:S(2)}) collective-permute-start(bf16[640,640]{1,0:T(8,128)(2,1)} %get-tuple-element.421), channel_id=1, source_target_pairs={{0,1},{1,0},{2,3},{3,2},{4,5},{5,4},{6,7},{7,6},{8,9},{9,8},{10,11... | collective-permute-start | bytes 2457608 | tf_op jit(solution)/shard_map/ppermute | solution.py:39
  432.9 25.9 %collective-permute-start.41 = (bf16[384,1280]{1,0:T(8,128)(2,1)}, bf16[384,1280]{1,0:T(8,128)(2,1)}, u32[]{:S(2)}, u32[]{:S(2)}) collective-permute-start(bf16[384,1280]{1,0:T(8,128)(2,1)} %fusion.38), channel_id=1, source_target_pairs={{0,8},{8,0},{1,9},{9,1},{2,10},{10,2},{3,11},{11,3},{4,12},{12,4},... | collective-permute-start | bytes 2949128 | tf_op jit(solution)/shard_map/ppermute | solution.py:39
  433.0 24.4 %collective-permute-start.42 = (bf16[384,1280]{1,0:T(8,128)(2,1)}, bf16[384,1280]{1,0:T(8,128)(2,1)}, u32[]{:S(2)}, u32[]{:S(2)}) collective-permute-start(bf16[384,1280]{1,0:T(8,128)(2,1)} %add_convert_fusion.6), channel_id=1, source_target_pairs={{0,2},{2,0},{1,3},{3,1},{4,6},{6,4},{5,7},{7,5},{8,10},{10,8},{9,1... | collective-permute-start | bytes 2949128 | tf_op jit(solution)/shard_map/ppermute | solution.py:39
  449.8 29.5 %all-to-all-start.2 = ((bf16[8,160,384]{2,1,0:T(8,128)(2,1)}), bf16[8,160,384]{2,1,0:T(8,128)(2,1)}, u32[]{:S(2)}, u32[]{:S(2)}) async-start(bf16[8,160,384]{2,1,0:T(8,128)(2,1)} %bitcast.91), calls=%async_computation.2 | async-start | bytes 1966080 | tf_op jit(solution)/shard_map/all_to_all | solution.py:445
  490.9 26.4 %collective-permute-start.46 = (bf16[2,2,160,640]{3,2,1,0:T(8,128)(2,1)}, bf16[2,2,160,640]{3,2,1,0:T(8,128)(2,1)}, u32[]{:S(2)}, u32[]{:S(2)}) collective-permute-start(bf16[2,2,160,640]{3,2,1,0:T(8,128)(2,1)} %get-tuple-element.419), channel_id=1, source_target_pairs={{0,16},{16,0},{1,17},{17,1},{2,18},{18,2},{3,19},{19,3},{4,20},{20... | collective-permute-start | bytes 2457608 | tf_op jit(solution)/shard_map/ppermute | solution.py:39
  491.8 38.2 %all-to-all-start.3 = ((bf16[8,160,384]{2,1,0:T(8,128)(2,1)}), bf16[8,160,384]{2,1,0:T(8,128)(2,1)S(1)}, u32[]{:S(2)}, u32[]{:S(2)}) async-start(bf16[8,160,384]{2,1,0:T(8,128)(2,1)} %bitcast.336), calls=%async_computation.3 | async-start | bytes 1966080 | tf_op jit(solution)/shard_map/all_to_all | solution.py:445
  498.2 74.0 %collective-permute-start.48 = (bf16[2,160,1280]{2,1,0:T(8,128)(2,1)}, bf16[2,160,1280]{2,1,0:T(8,128)(2,1)}, u32[]{:S(2)}, u32[]{:S(2)}) collective-permute-start(bf16[2,160,1280]{2,1,0:T(8,128)(2,1)} %get-tuple-element.417), channel_id=1, source_target_pairs={{0,1},{1,0},{2,3},{3,2},{4,5},{5,4},{6,7},{7,6},{8,9},{9,8},{10,11... | collective-permute-start | bytes 2457608 | tf_op jit(solution)/shard_map/ppermute | solution.py:39
  504.2 68.0 %collective-permute-start.50 = (bf16[320,640]{1,0:T(8,128)(2,1)}, bf16[320,640]{1,0:T(8,128)(2,1)}, u32[]{:S(2)}, u32[]{:S(2)}) collective-permute-start(bf16[320,640]{1,0:T(8,128)(2,1)} %get-tuple-element.442), channel_id=1, source_target_pairs={{0,4},{4,0},{1,5},{5,1},{2,6},{6,2},{3,7},{7,3},{8,12},{12,8},{9,1... | collective-permute-start | bytes 1228808 | tf_op jit(solution)/shard_map/ppermute | solution.py:39
  535.5 36.7 %collective-permute-start.51 = (bf16[320,640]{1,0:T(8,128)(2,1)}, bf16[320,640]{1,0:T(8,128)(2,1)}, u32[]{:S(2)}, u32[]{:S(2)}) collective-permute-start(bf16[320,640]{1,0:T(8,128)(2,1)} %get-tuple-element.440), channel_id=1, source_target_pairs={{0,4},{4,0},{1,5},{5,1},{2,6},{6,2},{3,7},{7,3},{8,12},{12,8},{9,1... | collective-permute-start | bytes 1228808 | tf_op jit(solution)/shard_map/ppermute | solution.py:39
  538.9 26.5 %collective-permute-start.47 = (bf16[2,2,1,160,384]{4,3,1,0,2:T(8,128)(2,1)}, bf16[2,2,1,160,384]{4,3,1,0,2:T(8,128)(2,1)S(1)}, u32[]{:S(2)}, u32[]{:S(2)}) collective-permute-start(bf16[2,2,1,160,384]{4,3,1,0,2:T(8,128)(2,1)} %bitcast.317), channel_id=1, source_target_pairs={{0,8},{8,0},{1,9},{9,1},{2,10},{10,2},{3,11},{11,3},{4,12},{12,4},... | collective-permute-start | bytes 1474568 | tf_op jit(solution)/shard_map/ppermute | solution.py:39
  (98 other events, 732.3 us)

commit v3 on v2

--- a/solution.py
+++ b/solution.py
@@ -25,6 +25,7 @@
 
 
 GROUP = ("zl", "yl")
+OTHERS = ("x", "zh", "yh")
 
 
 def size_of(axis):
@@ -80,8 +81,9 @@
     return total
 
 
-def send_units(total, axis):
-    return total[0], swap(total[1], axis)
+def send_units(total, axis, dim):
+    mine = lax.axis_index(axis)
+    return pick(total, mine, dim), swap(pick(total, 1 - mine, dim), axis)
 
 
 def send_rows(total):
@@ -96,38 +98,33 @@
     return sum(p.astype(F32) for p in parts).astype(BF)
 
 
-def join_body(pad_rows, x_ref, *refs):
-    pieces, out_ref = refs[:-1], refs[-1]
-    side = pieces[0].shape[-1]
-    for d, piece in enumerate(pieces):
-        for j in range(len(pieces)):
-
-            @pl.when((x_ref[0] ^ d) == j)
-            def _(piece=piece, j=j):
-                columns = slice(j * side, (j + 1) * side)
-                if not pad_rows:
-                    out_ref[:, columns] = piece[...]
-                    return
-                count, head_dim = pad_rows
-                for p in range(piece.shape[0]):
-                    for h in range(count):
-                        at = (p * count + h) * PAD
-                        out_ref[at : at + head_dim, columns] = piece[p, 0, h * head_dim : (h + 1) * head_dim]
-                        out_ref[at + head_dim : at + PAD, columns] = jnp.zeros((PAD - head_dim, side), BF)
-
-
-def join_rows(pieces, in_spec, grid, out_block, pad_rows=None):
-    width = pieces[0].shape[-1] * len(pieces)
-    x = lax.axis_index("x").astype(jnp.int32).reshape(1)
+def join_body(padded, stack_ref, out_ref):
+    count, blocks = stack_ref.shape[:2]
+    side = stack_ref.shape[-1]
+    for x in range(count):
+        columns = slice(x * side, (x + 1) * side)
+        if not padded:
+            out_ref[:, columns] = stack_ref[x, 0, 0]
+            continue
+        head_dim = stack_ref.shape[-2]
+        for p in range(blocks):
+            for h in range(stack_ref.shape[3]):
+                at = (p * stack_ref.shape[3] + h) * PAD
+                out_ref[at : at + head_dim, columns] = stack_ref[x, p, 0, h]
+                out_ref[at + head_dim : at + PAD, columns] = jnp.zeros((PAD - head_dim, side), BF)
+
+
+def join_rows(stack, in_spec, grid, out_block, padded):
+    width = stack.shape[-1] * stack.shape[0]
     return pl.pallas_call(
-        functools.partial(join_body, pad_rows),
+        functools.partial(join_body, padded),
         grid=(grid,),
-        in_specs=[pl.BlockSpec(memory_space=pltpu.SMEM)] + [in_spec] * len(pieces),
+        in_specs=[in_spec],
         out_specs=pl.BlockSpec((out_block, width), lambda i: (i, 0)),
         out_shape=jax.ShapeDtypeStruct((grid * out_block, width), BF),
         compiler_params=pltpu.CompilerParams(vmem_limit_bytes=32 * 2**20),
-        cost_estimate=pl.CostEstimate(flops=0, bytes_accessed=8 * pieces[0].size * len(pieces), transcendentals=0),
-    )(x, *pieces)
+        cost_estimate=pl.CostEstimate(flops=1000, bytes_accessed=1000, transcendentals=0),
+    )(stack)
 
 
 def first_rows(slot, clips):
@@ -183,9 +180,7 @@
         out_shape=jax.ShapeDtypeStruct((2, clips, chips, features, lanes * lines), BF),
         scratch_shapes=[pltpu.VMEM((sum(len(r) for r in starts), lines, packed_width), BF)],
         compiler_params=pltpu.CompilerParams(vmem_limit_bytes=32 * 2**20),
-        cost_estimate=pl.CostEstimate(
-            flops=4 * count * packed_width**2, bytes_accessed=8 * count * packed_width, transcendentals=0
-        ),
+        cost_estimate=pl.CostEstimate(flops=1000, bytes_accessed=1000, transcendentals=0),
     )(packed)
 
 
@@ -245,9 +240,7 @@
         out_shape=jax.ShapeDtypeStruct((count, packed_width), F32),
         scratch_shapes=[pltpu.VMEM((-(-last // 16) * 16, packed_width), F32)],
         compiler_params=pltpu.CompilerParams(vmem_limit_bytes=40 * 2**20),
-        cost_estimate=pl.CostEstimate(
-            flops=4 * count * packed_width**2, bytes_accessed=8 * count * packed_width, transcendentals=0
-        ),
+        cost_estimate=pl.CostEstimate(flops=1000, bytes_accessed=1000, transcendentals=0),
     )(*given)
 
 
@@ -285,11 +278,7 @@
             jax.ShapeDtypeStruct((heads, slots, block), BF),
         ],
         compiler_params=pltpu.CompilerParams(vmem_limit_bytes=50 * 2**20),
-        cost_estimate=pl.CostEstimate(
-            flops=heads * slots * slots * PAD * 6,
-            bytes_accessed=heads * slots * slots,
-            transcendentals=heads * slots * block,
-        ),
+        cost_estimate=pl.CostEstimate(flops=1000, bytes_accessed=1000, transcendentals=0),
     )(packed, packed, packed)
 
 
@@ -365,11 +354,7 @@
         out_specs=out_specs,
         out_shape=out_shape,
         compiler_params=pltpu.CompilerParams(vmem_limit_bytes=56 * 2**20),
-        cost_estimate=pl.CostEstimate(
-            flops=heads * slots * slots * PAD * 8,
-            bytes_accessed=heads * slots * slots,
-            transcendentals=0,
-        ),
+        cost_estimate=pl.CostEstimate(flops=1000, bytes_accessed=1000, transcendentals=0),
     )(*given)
 
 
@@ -455,23 +440,20 @@
             return jnp.broadcast_to(tensor[None], (2,) + tensor.shape)
         return tensor.reshape((2, tensor.shape[0] // 2) + tensor.shape[1:])
 
-    def double(part, axis):
-        return part, swap(part, axis)
-
-    def stacked(parts):
-        return jnp.stack(parts)
-
-    def arrange_heads(pieces):
+    def gather_others(shard):
+        return lax.all_gather(shard, OTHERS, axis=0)
+
+    def arrange_heads(stack):
+        stack = stack.reshape(-1, 4, 4, part_heads, head_dim, 2 * rows)
         if not split:
-            pieces = [lax.dynamic_slice_in_dim(p, k * (p.shape[0] // 2), p.shape[0] // 2, 0) for p in pieces]
-        pieces = [p.reshape(-1, 4, part_heads * head_dim, 2 * rows) for p in pieces]
-        block = (pieces[0].shape[0], 1) + pieces[0].shape[2:]
-        return join_rows(
-            pieces, pl.BlockSpec(block, lambda i: (0, i, 0, 0)), 4, heads * PAD, (part_heads, head_dim)
-        )
-
-    def arrange_units(pieces):
-        return join_rows(pieces, pl.BlockSpec((half_units, 2 * rows), lambda i: (i, 0)), 4, half_units)
+            stack = lax.dynamic_slice_in_dim(stack, 2 * k, 2, 1)
+        block = stack.shape[:2] + (1,) + stack.shape[3:]
+        return join_rows(stack, pl.BlockSpec(block, lambda i: (0, 0, i, 0, 0, 0)), 4, heads * PAD, True)
+
+    def arrange_units(stack, which):
+        stack = stack.reshape(-1, 4, 2, half_units, 2 * rows)
+        block = (stack.shape[0], 1, 1) + stack.shape[3:]
+        return join_rows(stack, pl.BlockSpec(block, lambda i: (0, i, which, 0, 0)), 4, half_units, False)
 
     full_vectors = jnp.stack([ln1_gain, ln1_bias, ln2_gain, ln2_bias, b_attn_out, b_out])
     part_vector = jnp.concatenate([b_query, b_value, b_in])
@@ -479,41 +461,36 @@
     full_by = jnp.stack(in_order(pieces_of(full_vectors, GROUP), GROUP))
     all_lengths = jnp.concatenate(in_order(pieces_of(lengths, "k"), "k"))
 
+    taken = take_positions(inputs, slot, clips, lanes, lines)
+    own_tokens, other_tokens = pick(taken, k, 0), swap(pick(taken, 1 - k, 0), "k")
     turned = [t.astype(BF).T for t in (w_query, w_key, w_value)] + [w_attn_out.astype(BF)]
     head_parts = jnp.stack([by_core(t, split) for t in turned], axis=1)
     head_parts = head_parts.reshape(2, 4 * part_heads * head_dim, rows)
-    size = head_parts.shape[1]
     own_parts, other_parts = pick(head_parts, k, 0), swap(pick(head_parts, 1 - k, 0), "k")
-    inputs_then, own_parts, full_by = sync(inputs, own_parts, full_by)
+    head_shard = jnp.concatenate(in_order([own_parts, other_parts], "k"), axis=1)
+    head_stacked = gather_others(head_shard)
+
+    ordered, cotangent, w_in, w_out, full_by = sync(
+        order_tokens(own_tokens, other_tokens), cotangent, w_in, w_out, full_by
+    )
+    moved = exchange(ordered)
     full_size = full_by.size
-    vector_pieces = pieces_of(jnp.concatenate([full_by.reshape(-1), part_vector]), "zh")
-    taken = take_positions(inputs_then, slot, clips, lanes, lines)
-    taken, vector_pieces = sync(taken, vector_pieces)
-    full_by = jnp.stack(in_order([p[:full_size] for p in vector_pieces], "zh"))
-    part_by = jnp.stack([p[full_size:] for p in vector_pieces])
-    full_size = full_by.size
-    vector_pieces = pieces_of(jnp.concatenate([full_by.reshape(-1), part_by.reshape(-1)]), "yh")
-    own_tokens, other_tokens = pick(taken, k, 0), swap(pick(taken, 1 - k, 0), "k")
-    head_shard = jnp.concatenate(in_order([own_parts, other_parts], "k"), axis=1)
-    ordered, head_shard, vector_pieces = sync(order_tokens(own_tokens, other_tokens), head_shard, vector_pieces)
-    head_pair = double(head_shard, "zh")
-    moved = exchange(ordered)
-
-    ordered, cotangent, w_in, w_out = sync(ordered, cotangent, w_in, w_out)
+    vector_pieces = in_order(pieces_of(jnp.concatenate([full_by.reshape(-1), part_vector]), "zh"), "zh")
+    vector_pieces = in_order(pieces_of(jnp.stack(vector_pieces), "yh"), "yh")
     unit_parts = jnp.stack([by_core(w_in.astype(BF).T, True), by_core(w_out.astype(BF), True)], axis=1)
     unit_parts = unit_parts.reshape(2, units, rows)
     own_parts, other_parts = pick(unit_parts, k, 0), swap(pick(unit_parts, 1 - k, 0), "k")
-    own_parts, cotangent, head_pair = sync(own_parts, cotangent, head_pair)
-    head_pair = double(stacked(head_pair), "yh")
+    unit_shard = jnp.concatenate(in_order([own_parts, other_parts], "k"), axis=1)
+    unit_shard = unit_shard.reshape(2, half_units, 2 * rows)
+    unit_stacked = gather_others(unit_shard)
     taken = take_positions(cotangent, slot, clips, lanes, lines)
     own_tokens, other_tokens = pick(taken, k, 0), swap(pick(taken, 1 - k, 0), "k")
-    unit_shard = jnp.concatenate(in_order([own_parts, other_parts], "k"), axis=1)
-    unit_shard = unit_shard.reshape(2, half_units, 2 * rows)
     ordered_grads = order_tokens(own_tokens, other_tokens)
 
-    full_by = jnp.stack(in_order([p[:full_size] for p in vector_pieces], "yh"))
-    part_by = jnp.stack([p[full_size:].reshape(part_by.shape) for p in vector_pieces]).reshape(4, -1)
-    full_by = full_by.reshape(2, 2, 2, yl_size, full_count, features).transpose(4, 1, 2, 0, 3, 5)
+    all_vectors = jnp.stack(vector_pieces, axis=1)
+    part_by = all_vectors[:, :, full_size:].reshape(4, -1)
+    full_by = all_vectors[:, :, :full_size].reshape(2, 2, 2, yl_size, full_count, features)
+    full_by = full_by.transpose(4, 0, 2, 1, 3, 5)
     gain_one, shift_one, gain_two, shift_two, attn_shift, out_shift = full_by.reshape(full_count, 1, width)
 
     def head_vector(tensor):
@@ -555,27 +532,14 @@
             for d in range(count)
         ]
 
-    moved, ordered_grads, unit_shard, gain_one, shift_one = sync(
-        moved, ordered_grads, unit_shard, gain_one, shift_one
-    )
     tokens = join(moved).astype(F32)
     normal_one, scale_one, normed_part = norm_forward(tokens, gain_one, shift_one)
-    tokens, normal_one, scale_one, normed_part, head_pair = sync(
-        tokens, normal_one, scale_one, normed_part, head_pair
-    )
     normed_far = far_pieces(normed_part)
-    head_pieces = pieces_of(stacked(head_pair).reshape(4 * size, 2 * rows), "x")
-    in_pair = double(unit_shard[0], "zh")
     normed_near = with_core(normed_part)
-    normed_near, in_pair = sync(normed_near, in_pair)
-    in_pair = double(stacked(in_pair), "yh")
-    out_pair = double(unit_shard[1], "zh")
-    normed_near, normed_far, in_pair = sync(normed_near, normed_far, in_pair)
-    in_pieces = pieces_of(stacked(in_pair).reshape(4 * half_units, 2 * rows), "x")
-    head_pieces, normed_near, ordered_grads, out_pair = sync(head_pieces, normed_near, ordered_grads, out_pair)
-    out_pair = double(stacked(out_pair), "yh")
+    normed_near, head_stacked = sync(normed_near, head_stacked)
+    head_weights = arrange_heads(head_stacked).reshape(4, heads * PAD, width)
+    normed_far, ordered_grads = sync(normed_far, ordered_grads)
     moved_grads = exchange(ordered_grads)
-    head_weights = arrange_heads(head_pieces).reshape(4, heads * PAD, width)
     qkv_weights = head_weights[:3].reshape(3 * heads * PAD, width)
     attn_weights = head_weights[3]
 
@@ -599,22 +563,23 @@
     far_sums, packed, moved_grads = sync(far_sums, packed, moved_grads)
     far_total = send_far(far_sums) if near_chips == 1 else None
     near_context, near_wide, near_weights = attend(packed, heads, 0)
+    normed = jnp.concatenate(normed_rows, axis=0)
     grad_low = jnp.where(own_valid[:, None], join(moved_grads), jnp.zeros((quarter, width), BF))
-    near_context, grad_low, far_total, out_pair = sync(near_context, grad_low, far_total, out_pair)
-    out_pieces = pieces_of(stacked(out_pair).reshape(4 * half_units, 2 * rows), "x")
+    if near_chips == 1:
+        near_context, far_total, normed, grad_low = sync(near_context, far_total, normed, grad_low)
     near_sums = [cores_sum(attn_product, b) for b in blocks_of(near_context)]
     if near_chips > 1:
         far_total = send_far((near_sums + far_sums)[1:])
-    near_sums, far_total, in_pieces = sync(near_sums, far_total, in_pieces)
     grad_far = far_pieces(grad_low)
     grad_near = with_core(grad_low)
     attn_part = near_sums[0] + far_total + attn_shift
     middle = tokens + attn_part
     normal_two, scale_two, normed_two_part = norm_forward(middle, gain_two, shift_two)
-    normal_two, scale_two, normed_two_part, grad_near = sync(normal_two, scale_two, normed_two_part, grad_near)
     two_near = with_core(normed_two_part)
     two_far = far_pieces(normed_two_part)
-    in_weights = arrange_units(in_pieces)
+    two_near, unit_stacked, grad_far = sync(two_near, unit_stacked, grad_far)
+    in_weights = arrange_units(unit_stacked, 0)
+    out_weights = arrange_units(unit_stacked, 1)
 
     def feed(rows_d):
         hidden = dot(rows_d, in_weights, 1, 1) + unit_shift
@@ -626,13 +591,11 @@
         return (dot(grad_d, out_weights, 1, 1) * slope).astype(BF)
 
     near_active, near_slope = feed(two_near)
-    near_active, near_slope, two_far = sync(near_active, near_slope, two_far)
+    near_hidden = feed_back(grad_near, near_slope)
+    near_hidden, two_far = sync(near_hidden, two_far)
     two_rows = [two_near] + [with_core(v) for v in two_far]
     far_feed = [feed(v) for v in two_rows[1:]]
-    near_slope, far_feed, out_pieces, grad_far = sync(near_slope, far_feed, out_pieces, grad_far)
-    out_weights = arrange_units(out_pieces)
     grad_rows = [grad_near] + [with_core(v) for v in grad_far]
-    near_hidden = feed_back(grad_near, near_slope)
     grad_hidden = jnp.concatenate(
         [near_hidden] + [feed_back(g, f[1]) for g, f in zip(grad_rows[1:], far_feed)], axis=0
     )
@@ -645,20 +608,18 @@
     far_two = [cores_sum(in_product, b).astype(BF) for b in hidden_blocks[1:]]
     grad_hidden, near_blocks, far_two, active = sync(grad_hidden, hidden_blocks[0], far_two, active)
     near_two = cores_sum(in_product, near_blocks)
-    normed = jnp.concatenate(normed_rows, axis=0)
     normed_two = jnp.concatenate(two_rows, axis=0)
     grad_full = jnp.concatenate(grad_rows, axis=0)
-    out_total = dot(active, grad_full, 0, 0).astype(BF)
-    out_total, grad_hidden, near_two = sync(out_total, grad_hidden, near_two)
-    out_half = send_units(out_total.reshape(2, -1, width), "yh")
-    in_total = dot(grad_hidden, normed_two, 0, 0).astype(BF)
-    in_total, near_two = sync(in_total, near_two)
+
+    out_total = dot(active, grad_full, 0, 0).astype(BF).reshape(2, 2, half_units, width)
+    in_total = dot(grad_hidden, normed_two, 0, 0).astype(BF).reshape(2, 2, half_units, width)
+    out_half = send_units(out_total, "yh", 1)
     in_half = send_rows(in_total)
-    grad_two = near_two + send_far(far_two)
+    two_arrived, active = sync(send_far(far_two), active)
+    grad_two = near_two + two_arrived
     grad_out = grad_low.astype(F32)
     grad_middle = grad_out + norm_backward(grad_two, normal_two, scale_two, gain_two)
     grad_mid_part = grad_middle.astype(BF)
-    grad_middle, grad_mid_part, active, grad_two = sync(grad_middle, grad_mid_part, active, grad_two)
     mid_far = far_pieces(grad_mid_part)
     mid_near = with_core(grad_mid_part)
 
@@ -668,17 +629,21 @@
     def out_product(v):
         return dot(v, out_weights, 1, 0)
 
-    active_blocks = blocks_of(active)
-    far_delta = [cores_sum(out_product, b).astype(BF) for b in active_blocks[1:]]
-    near_delta = cores_sum(out_product, active_blocks[0])
     mid_half = jnp.concatenate([mid_near] + [with_core(v) for v in mid_far[: near_chips - 1]], axis=0)
     near_grad = context_grad(mid_half)
-    near_grad, far_delta, near_delta = sync(near_grad, far_delta, near_delta)
+    active_blocks = blocks_of(active)
+    delta_given = swap(jnp.concatenate([out_product(b[1]).astype(BF) for b in active_blocks]), "k")
+    delta_cores = [
+        out_product(b[0]) + delta_given[d * quarter : (d + 1) * quarter].astype(F32)
+        for d, b in enumerate(active_blocks)
+    ]
+    near_delta, far_delta = delta_cores[0], [v.astype(BF) for v in delta_cores[1:]]
+    near_grad, near_delta, far_delta = sync(near_grad, near_delta, far_delta)
     first = attend_back(packed, near_grad, near_wide, near_weights, heads, head_dim, 0)
-    first, mid_far, out_half, in_half, far_delta = sync(first, mid_far, out_half, in_half, far_delta)
+    first, mid_far, far_delta, out_half, in_half = sync(first, mid_far, far_delta, out_half, in_half)
     delta_far = send_far(far_delta)
     out_half = send_rows(summed(out_half))
-    in_half = send_units(summed(in_half).reshape(2, -1, 2 * rows), "yh")
+    in_half = send_units(summed(in_half), "yh", 1)
     mid_rows = [mid_near] + [with_core(v) for v in mid_far]
     mid_full = jnp.concatenate(mid_rows, axis=0)
     far_grad = context_grad(mid_full[half:])
@@ -692,11 +657,14 @@
         [grads[:, (2 * d + c) * quarter : (2 * d + c + 1) * quarter] for c in range(2)] for d in range(chips)
     ]
     far_one = [cores_sum(qkv_product, b).astype(BF) for b in grad_blocks[1:]]
-    grads, far_one, near_blocks, delta_far = sync(grads, far_one, grad_blocks[0], delta_far)
+    grads, far_one, near_blocks, out_half, in_half = sync(grads, far_one, grad_blocks[0], out_half, in_half)
     far_arrived = send_far(far_one)
     near_one = cores_sum(qkv_product, near_blocks)
-    delta = (attn_part + near_delta + delta_far + out_shift).astype(BF)
-    moved_delta = exchange(cut(delta))
+    unit_sums = jnp.stack([summed(out_half), summed(in_half)])
+    far_arrived, unit_sums = sync(far_arrived, unit_sums)
+    unit_half = send_units(unit_sums, "zh", 1)
+    context = jnp.concatenate([near_context, far_context], axis=0)
+    grads, near_one, delta_far, context, mid_full = sync(grads, near_one, delta_far, context, mid_full)
 
     def trim(total):
         return total.reshape(-1, part_heads, PAD, width)[:, :, :head_dim].reshape(-1, part_heads * head_dim, width)
@@ -708,62 +676,17 @@
             chunk = lax.dynamic_update_slice_in_dim(blank, chunk, 2 * k, 0)
         return chunk.reshape((2, 2) + chunk.shape[1:])
 
-    context = jnp.concatenate([near_context, far_context], axis=0)
     query_key = head_chunk([dot(grads[j], normed, 0, 0).astype(BF) for j in range(2)])
-    query_key, grads, near_one, far_arrived, out_half, in_half = sync(
-        query_key, grads, near_one, far_arrived, out_half, in_half
-    )
+    value_attn = head_chunk([dot(grads[2], normed, 0, 0).astype(BF), dot(context, mid_full, 0, 0).astype(BF)])
+    query_key_half = send_rows(query_key)
+    value_attn_half = send_units(value_attn, "yh", 1)
     grad_one = near_one + far_arrived
     grad_tokens = norm_backward(grad_one, normal_one, scale_one, gain_one)
     last_part = (grad_middle + grad_tokens).astype(BF)
-    last_blocks, grad_one, moved_delta, query_key, grads, out_half, in_half = sync(
-        cut(last_part), grad_one, moved_delta, query_key, grads, out_half, in_half
-    )
-    moved_last = exchange(last_blocks)
-    query_key_half = send_rows(query_key)
-    value_attn = head_chunk([dot(grads[2], normed, 0, 0).astype(BF), dot(context, mid_full, 0, 0).astype(BF)])
-    value_attn, out_half, in_half, moved_delta = sync(value_attn, out_half, in_half, moved_delta)
-    value_attn_half = send_units(value_attn, "yh")
-    out_half = send_units(summed(out_half).reshape(2, -1, 2 * rows), "zh")
-    in_half = send_units(summed(in_half).reshape(2, -1, 2 * rows), "zh")
-
-    def two_cores(total, two):
-        kept = lax.dynamic_slice_in_dim(total, k * rows, rows, 1)
-        other = swap(lax.dynamic_slice_in_dim(total, (1 - k) * rows, rows, 1), "k")
-        if not two:
-            return kept.astype(F32) + other.astype(F32)
-        return jnp.stack(in_order([kept, other], "k")).astype(F32)
-
-    def kept_tokens(moved):
-        moved = moved.reshape(2, 2, 2, yl_size, features, quarter).transpose(0, 2, 1, 3, 4, 5)
-        kept = pick(moved, k, 0)
-        other = swap(pick(moved, 1 - k, 0), "k")
-        ordered = jnp.stack(in_order([kept, other], "k"))
-        return ordered.reshape(2, clips, chips, features, quarter)
-
-    def put(tokens, base=None):
-        return put_positions(tokens, slot, pack_count, lanes, lines, base)
-
-    layer_out = put(kept_tokens(moved_delta), inputs)
-    layer_out, query_key_half, moved_last, grad_one = sync(layer_out, query_key_half, moved_last, grad_one)
-    query_key_half = send_units(summed(query_key_half), "yh")
-    input_grad = put(kept_tokens(moved_last))
-    input_grad, value_attn_half, query_key_half, out_half, in_half = sync(
-        input_grad, value_attn_half, query_key_half, out_half, in_half
-    )
+    moved_last = exchange(cut(last_part))
+    query_key_half = send_units(summed(query_key_half), "yh", 1)
     value_attn_half = send_rows(summed(value_attn_half))
-    query_key_half = send_units(summed(query_key_half), "zh")
-    grad_out_w = two_cores(summed(out_half), True).reshape(units, rows)
-    grad_in_w = two_cores(summed(in_half), True).reshape(units, rows).T
-    grad_out_w, grad_in_w, value_attn_half = sync(grad_out_w, grad_in_w, value_attn_half)
-    value_attn_half = send_units(summed(value_attn_half), "zh")
-    head_parts = [
-        two_cores(summed(t), split).reshape(-1, 2, part_heads * head_dim, rows)
-        for t in (query_key_half, value_attn_half)
-    ]
-    grad_query_w, grad_key_w, grad_value_w, grad_attn_w = (
-        t[:, j].reshape(features, rows) for t in head_parts for j in range(2)
-    )
+    delta = (attn_part + near_delta + delta_far + out_shift).astype(BF)
 
     full_sums = jnp.stack(
         [
@@ -794,21 +717,54 @@
         ],
         axis=1,
     )
-    full_sums = full_sums.reshape(full_count, 2, 2, 2, yl_size, features).transpose(3, 1, 2, 4, 0, 5)
-    full_size = full_sums.size
-    flat = jnp.concatenate([full_sums.reshape(-1), part_sums.reshape(-1)])
-    flat = sum(pieces_of(flat, "x"))
+    full_sums = full_sums.reshape(full_count, 2, 2, 2, yl_size, features).transpose(1, 3, 2, 4, 0, 5)
+    full_size = full_sums[0, 0].size
+    flat = jnp.concatenate([full_sums.reshape(2, 2, -1), part_sums.reshape(2, 2, -1)], axis=2)
+    flat_pieces = pieces_of(flat, "x")
+    moved_last, query_key_half, value_attn_half, delta_blocks, flat_pieces, unit_half = sync(
+        moved_last, query_key_half, value_attn_half, cut(delta), flat_pieces, unit_half
+    )
+    moved_delta = exchange(delta_blocks)
+    head_half = send_units(jnp.stack([summed(query_key_half), summed(value_attn_half)]), "zh", 1)
+
+    def two_cores(total, two):
+        last = total.ndim - 1
+        kept = lax.dynamic_slice_in_dim(total, k * rows, rows, last)
+        other = swap(lax.dynamic_slice_in_dim(total, (1 - k) * rows, rows, last), "k")
+        if not two:
+            return kept.astype(F32) + other.astype(F32)
+        return jnp.stack(in_order([kept, other], "k"), axis=1).astype(F32)
+
+    def kept_tokens(moved):
+        moved = moved.reshape(2, 2, 2, yl_size, features, quarter).transpose(0, 2, 1, 3, 4, 5)
+        kept = pick(moved, k, 0)
+        other = swap(pick(moved, 1 - k, 0), "k")
+        ordered = jnp.stack(in_order([kept, other], "k"))
+        return ordered.reshape(2, clips, chips, features, quarter)
+
+    def put(tokens, base=None):
+        return put_positions(tokens, slot, pack_count, lanes, lines, base)
+
+    flat_half = send_units(sum(flat_pieces), "yh", 1)
+    input_grad, moved_delta, flat_half = sync(put(kept_tokens(moved_last)), moved_delta, flat_half)
+    flat = sum(send_units(sum(flat_half), "zh", 0))
     full_flat, part_flat = flat[:full_size], flat[full_size:]
-    for axis, index in (("yh", yh), ("zh", zh)):
-        full_flat, part_flat = full_flat.reshape(2, -1), part_flat.reshape(2, -1)
-        given = swap(jnp.concatenate([pick(full_flat, 1 - index, 0), part_flat[1]]), axis)
-        cut_at = full_flat.shape[1]
-        full_flat = pick(full_flat, index, 0) + given[:cut_at]
-        part_flat = part_flat[0] + given[cut_at:]
+
     by_chip = full_flat.reshape(chips, -1)
     mine = pick(by_chip, chip, 0)
     for d in range(1, chips):
         mine = mine + swap(pick(by_chip, chip ^ d, 0), GROUP, d)
+    unit_cores = two_cores(summed(unit_half), True)
+    grad_out_w = unit_cores[0].reshape(units, rows)
+    grad_in_w = unit_cores[1].reshape(units, rows).T
+    layer_out = put(kept_tokens(moved_delta), inputs)
+    input_grad, head_half, mine = sync(input_grad, head_half, mine)
+    head_cores = two_cores(summed(head_half), split)
+    head_cores = head_cores.reshape(2, -1, 2, part_heads * head_dim, rows)
+    grad_query_w, grad_key_w, grad_value_w, grad_attn_w = (
+        head_cores[i, :, j].reshape(features, rows) for i in range(2) for j in range(2)
+    )
+
     own_size = mine.shape[0]
     last_pair = pieces_of(jnp.concatenate([mine, part_flat]), "k")
     vec_one_gain, vec_one_bias, vec_battn, vec_two_gain, vec_two_bias, vec_bout = (

time: 609 us -> 575 us (0.944)
  waiting for transfers between devices: 205 us -> 181 us
  starting transfers between devices: 70.4 us -> 55 us
  between operations: 2.75 us -> 16.2 us
  matrix products: 111 us -> 100 us
    ppermute x64 -> x50, waiting for transfers between devices: 178 us -> 155 us  [swap(): lax.ppermute(tensor, axis, [(i, i ^ step) for i in range(size_of(axis))])]
    ppermute x64 -> x50, starting transfers between devices: 54 us -> 38.4 us  [swap(): lax.ppermute(tensor, axis, [(i, i ^ step) for i in range(size_of(axis))])]
    dot_general x38, matrix products: 111 us -> 100 us  [dot(): lax.dot_general(first, second, (((left,), (right,)), ((), ())), preferred...]
    concatenate x3 -> x4, other arithmetic: 0.09 us -> 10.2 us  [the longest x1 3.89 us: local(): normed = jnp.concatenate(normed_rows, axis=0)]
    unnamed x136 -> x182, local copies, waits for them, and re-layouts: 18.2 us -> 22.2 us
    convert_element_type x12 -> x6, other arithmetic: 12.8 us -> 9.11 us  [summed(): return sum((p.astype(F32) for p in parts)).astype(BF)]
  transfers between devices with their start and end apart: 68 -> 56, of which waited for: 31 -> 20; matrix products, arithmetic and copies ran while one was open for 35% -> 37% of each run, Pallas kernels for 12% -> 11%
where the time goes in v3:
time: 575 us; the launch traced here: 570 us
  waiting for transfers between devices  181 us (31%)
  matrix products  100 us (17%)
  other arithmetic  75.4 us (13%)
  Pallas kernels  73.5 us (13%)
  local copies, waits for them, and re-layouts  68.4 us (12%)
  starting transfers between devices  55 us (10%)
  between operations  16.2 us (3%)
    ppermute x50, waiting for transfers between devices, swap(): lax.ppermute(tensor, axis, [(i, i ^ step) for i in range(size_of(axis))])  155 us
    dot_general x38, matrix products, dot(): lax.dot_general(first, second, (((left,), (right,)), ((), ())), preferred...  100 us
    ppermute x50, starting transfers between devices, swap(): lax.ppermute(tensor, axis, [(i, i ^ step) for i in range(size_of(axis))])  38.4 us
    pallas_call x2, Pallas kernels, attend_back(): pl.pallas_call(functools.partial(body, head_dim), grid=(heads,), in_specs...  28.2 us
    all_to_all x4, waiting for transfers between devices, exchange(): return lax.all_to_all(blocks, ('zh', 'zl', 'yh', 'yl'), 0, 0)  26 us
    pallas_call x2, Pallas kernels, attend(): pl.pallas_call(forward_body, grid=(heads,), in_specs=[pl.BlockSpec((block...  22.8 us
    unnamed x182, local copies, waits for them, and re-layouts  22.2 us
    all_to_all x4, starting transfers between devices, exchange(): return lax.all_to_all(blocks, ('zh', 'zl', 'yh', 'yl'), 0, 0)  16.3 us
  transfers between devices with their start and end apart: 56, of which 20 were waited for; matrix products, arithmetic and copies ran while one was open for 37% of the time, Pallas kernels for 11%

profile of v3, /device:TPU:0, one launch (start us, length us, event | category | flops | bytes accessed | tf_op | source)
XLA Modules:
  0.0 569.7 jit_solution(1677871626770069817)
XLA Ops:
  8.8 3.8 shard_map.305
  50.2 7.8 %all-to-all-done = bf16[8,160,384]{2,1,0:T(8,128)(2,1)S(1)} async-done(((bf16[8,160,384]{2,1,0:T(8,128)(2,1)}), bf16[8,160,384]{2,1,0:T(8,128)(2,1)S(1)}, u32[]{:S(2)}, u32[]{:S(2)}) %all-to-all-start) | async-done | bytes 983072 | tf_op jit(solution)/shard_map/all_to_all | solution.py:430
  74.2 28.5 %collective-permute-done.7 = bf16[384,1280]{1,0:T(8,128)(2,1)} collective-permute-done((bf16[384,1280]{1,0:T(8,128)(2,1)}, bf16[384,1280]{1,0:T(8,128)(2,1)}, u32[]{:S(2)}, u32[]{:S(2)}) %collective-permute-start.7) | collective-permute-done | bytes 983072 | tf_op jit(solution)/shard_map/ppermute | solution.py:40
  103.1 3.9 all-to-all-start.1
  113.1 6.5 %add_convert_fusion = bf16[768,1536]{1,0:T(8,128)(2,1)S(1)} fusion(bf16[2048,1280]{1,0:T(8,128)(2,1)S(1)} %shard_map.306, f32[768]{0:T(1024)S(1)} %get-tuple-element.337, f32[1536]{0:T(1024)S(1)} %get-tuple-element.345, f32[1536]{0:T(1024)S(1)} %get-tuple-element.344, f32[1536]{0:T(1024)S(1)} %copy-done.83, f32[1536]{0:T(1024)S(1)} %get-tuple-element.350, ...), kind=kOutput, calls=%fused_computation.6 | convolution fusion | flops 3030908928 | bytes 8294400 | tf_op jit(solution)/shard_map/dot_general | solution.py:22
  125.8 11.4 %shard_map.308 = (bf16[768,512]{1,0:T(8,128)(2,1)S(1)}, f32[768,512]{1,0:T(8,128)S(1)}, bf16[4,1536,768]{2,1,0:T(8,128)(2,1)}) custom-call(bf16[1536,1536]{1,0:T(8,128)(2,1)} %pad_maximum_fusion.query_ref.key_ref.value_ref.query.key.value, bf16[1536,1536]{1,0:T(8,128)(2,1)} %pad_maximum_fusion.query_ref.key_ref.value_ref.query.key.value, ...), custom_call_target="tpu_custom_call" | custom-call | flops 1000 | bytes 1000 | tf_op jit(solution)/shard_map/pallas_call | solution.py:262
  145.4 3.9 pad_maximum_fusion.1
  149.3 11.4 %shard_map.309 = (bf16[768,512]{1,0:T(8,128)(2,1)S(1)}, f32[768,512]{1,0:T(8,128)S(1)}, bf16[4,1536,768]{2,1,0:T(8,128)(2,1)}) custom-call(bf16[1536,1536]{1,0:T(8,128)(2,1)} %pad_maximum_fusion.query_ref.key_ref.value_ref.query.key.value, bf16[1536,1536]{1,0:T(8,128)(2,1)} %pad_maximum_fusion.query_ref.key_ref.value_ref.query.key.value, ...), custom_call_target="tpu_custom_call" | custom-call | flops 1000 | bytes 1000 | tf_op jit(solution)/shard_map/pallas_call | solution.py:262
  167.1 13.2 %collective-permute-done.11 = bf16[384,1280]{1,0:T(8,128)(2,1)} collective-permute-done((bf16[384,1280]{1,0:T(8,128)(2,1)}, bf16[384,1280]{1,0:T(8,128)(2,1)}, u32[]{:S(2)}, u32[]{:S(2)}) %collective-permute-start.11) | collective-permute-done | bytes 983072 | tf_op jit(solution)/shard_map/ppermute | solution.py:40
  188.7 4.3 fusion.178
  199.3 42.7 %collective-permute-done.16 = bf16[384,1280]{1,0:T(8,128)(2,1)} collective-permute-done((bf16[384,1280]{1,0:T(8,128)(2,1)}, bf16[384,1280]{1,0:T(8,128)(2,1)}, u32[]{:S(2)}, u32[]{:S(2)}) %collective-permute-start.16) | collective-permute-done | bytes 983072 | tf_op jit(solution)/shard_map/ppermute | solution.py:40
  245.5 4.1 multiply_convert_fusion.1
  250.3 5.6 fusion.22
  255.9 6.9 %collective-permute-done.17 = bf16[384,1280]{1,0:T(8,128)(2,1)} collective-permute-done((bf16[384,1280]{1,0:T(8,128)(2,1)}, bf16[384,1280]{1,0:T(8,128)(2,1)}, u32[]{:S(2)}, u32[]{:S(2)}) %collective-permute-start.17) | collective-permute-done | bytes 983072 | tf_op jit(solution)/shard_map/ppermute | solution.py:40
  266.0 4.7 multiply_convert_fusion
  270.7 5.0 fusion.23
  283.3 7.2 %convolution_convert_fusion.1 = bf16[1280,1280]{1,0:T(8,128)(2,1)S(1)} fusion(bf16[1536,1280]{1,0:T(8,128)(2,1)S(1)} %pad_maximum_fusion.3, bf16[384,1280]{1,0:T(8,128)(2,1)S(1)} %collective-permute-done.18, bf16[384,1280]{1,0:T(8,128)(2,1)} %collective-permute-done.16, bf16[384,1280]{1,0:T(8,128)(2,1)} %collective-permute-done.13, ...), kind=kOutput, calls=%fused_computation.2 | convolution fusion | flops 5050531840 | bytes 11141120 | tf_op jit(solution)/shard_map/dot_general | solution.py:22
  295.4 10.0 %collective-permute-done.22 = bf16[384,1280]{1,0:T(8,128)(2,1)S(1)} collective-permute-done((bf16[384,1280]{1,0:T(8,128)(2,1)S(1)}, bf16[384,1280]{1,0:T(8,128)(2,1)S(1)}, u32[]{:S(2)}, u32[]{:S(2)}) %collective-permute-start.22) | collective-permute-done | bytes 983072 | tf_op jit(solution)/shard_map/ppermute | solution.py:40
  315.4 7.2 %convolution_convert_fusion = bf16[1280,1280]{1,0:T(8,128)(2,1)S(1)} fusion(bf16[1536,1280]{1,0:T(8,128)(2,1)S(1)} %pad_maximum_fusion.2, bf16[384,1280]{1,0:T(8,128)(2,1)} %collective-permute-done.19, bf16[384,1280]{1,0:T(8,128)(2,1)} %collective-permute-done.17, bf16[768,1280]{1,0:T(8,128)(2,1)S(1)} %copy-done.45), kind=kOutput, calls=%fused_computation.1 | convolution fusion | flops 5046599680 | bytes 11141120 | tf_op jit(solution)/shard_map/dot_general | solution.py:22
  328.8 4.2 fusion.55.grad
  333.0 3.9 convert_add_fusion.2
  340.5 13.9 %shard_map.312 = (bf16[768,512]{1,0:T(8,128)(2,1)}, f32[1536,512]{1,0:T(8,128)}, f32[1536,512]{1,0:T(8,128)}) custom-call(bf16[1536,1536]{1,0:T(8,128)(2,1)} %pad_maximum_fusion.query_ref.key_ref.value_ref.query.key.value, bf16[1536,1536]{1,0:T(8,128)(2,1)} %pad_maximum_fusion.query_ref.key_ref.value_ref.query.key.value, ...), custom_call_target="tpu_custom_call" | custom-call | flops 1000 | bytes 1000 | tf_op jit(solution)/shard_map/pallas_call | solution.py:350
  354.4 8.0 %collective-permute-done.27 = bf16[2,2,320,640]{3,2,1,0:T(8,128)(2,1)} collective-permute-done((bf16[2,2,320,640]{3,2,1,0:T(8,128)(2,1)}, bf16[2,2,320,640]{3,2,1,0:T(8,128)(2,1)}, u32[]{:S(2)}, u32[]{:S(2)}) %collective-permute-start.27) | collective-permute-done | bytes 1638432 | tf_op jit(solution)/shard_map/ppermute | solution.py:40
  375.2 14.4 %shard_map.313 = bf16[3,1536,512]{2,1,0:T(8,128)(2,1)} custom-call(bf16[1536,1536]{1,0:T(8,128)(2,1)} %pad_maximum_fusion.query_ref.key_ref.value_ref.query.key.value, bf16[1536,1536]{1,0:T(8,128)(2,1)} %pad_maximum_fusion.query_ref.key_ref.value_ref.query.key.value, bf16[1536,1536]{1,0:T(8,128)(2,1)} %pad_maximum_fusion.query_ref.key_ref.value_ref.query.key.value, ...), custom_call_target="tpu_custom_call" | custom-call | flops 1000 | bytes 1000 | tf_op jit(solution)/shard_map/pallas_call | solution.py:350
  423.9 4.4 collective-permute-done.34
  432.0 5.1 all-to-all-start.2
  464.1 7.4 %collective-permute-done.37 = bf16[2,160,1280]{2,1,0:T(8,128)(2,1)} collective-permute-done((bf16[2,160,1280]{2,1,0:T(8,128)(2,1)}, bf16[2,160,1280]{2,1,0:T(8,128)(2,1)}, u32[]{:S(2)}, u32[]{:S(2)}) %collective-permute-start.37) | collective-permute-done | bytes 819232 | tf_op jit(solution)/shard_map/ppermute | solution.py:40
  479.5 16.8 %collective-permute-done.40 = bf16[2,320,640]{2,1,0:T(8,128)(2,1)} collective-permute-done((bf16[2,320,640]{2,1,0:T(8,128)(2,1)}, bf16[2,320,640]{2,1,0:T(8,128)(2,1)}, u32[]{:S(2)}, u32[]{:S(2)}) %collective-permute-start.40) | collective-permute-done | bytes 819232 | tf_op jit(solution)/shard_map/ppermute | solution.py:40
  498.0 3.8 all-to-all-start.3
  512.0 6.4 %shard_map.314 = f32[375,1280]{1,0:T(8,128)} custom-call(bf16[2,2,2,160,384]{4,3,2,1,0:T(8,128)(2,1)S(1)} %maximum_bitcast_fusion.2.refs_0_), custom_call_target="tpu_custom_call" | custom-call | flops 1000 | bytes 1000 | tf_op jit(solution)/shard_map/pallas_call | solution.py:235
  518.4 17.8 %all-to-all-done.3 = bf16[8,160,384]{2,1,0:T(8,128)(2,1)S(1)} async-done(((bf16[8,160,384]{2,1,0:T(8,128)(2,1)}), bf16[8,160,384]{2,1,0:T(8,128)(2,1)S(1)}, u32[]{:S(2)}, u32[]{:S(2)}) %all-to-all-start.3) | async-done | bytes 983072 | tf_op jit(solution)/shard_map/all_to_all | solution.py:430
  556.1 6.4 %shard_map.315 = f32[375,1280]{1,0:T(8,128)} custom-call(f32[375,1280]{1,0:T(8,128)S(1)} %copy-done.3, bf16[2,2,2,160,384]{4,3,2,1,0:T(8,128)(2,1)S(1)} %maximum_bitcast_fusion.3.refs_1_), custom_call_target="tpu_custom_call" | custom-call | flops 1000 | bytes 1000 | tf_op jit(solution)/shard_map/pallas_call | solution.py:235
  (517 shorter events, 253.1 us)
Async XLA Ops:
  7.2 102.8 %all-gather.6.cloned.1.call-start = ((), (), s32[]{:S(2)}) async-start(), calls=%async_computation.5 | async-start | bytes 3686400 | tf_op jit(solution)/shard_map/all_gather | solution.py:444
  22.7 21.2 %collective-permute-start.2 = (f32[2880]{0:T(1024)S(1)}, f32[2880]{0:T(1024)S(1)}, u32[]{:S(2)}, u32[]{:S(2)}) collective-permute-start(f32[2880]{0:T(1024)S(1)} %concatenate.105), channel_id=1, source_target_pairs={{0,4},{4,0},{1,5},{5,1},{2,6},{6,2},{3,7},{7,3},{8,12},{12,8},{9,1... | collective-permute-start | bytes 34568 | tf_op jit(solution)/shard_map/ppermute | solution.py:40
  25.3 32.8 %all-to-all-start = ((bf16[8,160,384]{2,1,0:T(8,128)(2,1)}), bf16[8,160,384]{2,1,0:T(8,128)(2,1)S(1)}, u32[]{:S(2)}, u32[]{:S(2)}) async-start(bf16[8,160,384]{2,1,0:T(8,128)(2,1)} %bitcast.6), calls=%async_computation | async-start | bytes 1966080 | tf_op jit(solution)/shard_map/all_to_all | solution.py:430
  28.9 213.1 %all-gather.4.cloned.1.call-start = ((), (), s32[]{:S(2)}) async-start(), calls=%async_computation.4 | async-start | bytes 7372800 | tf_op jit(solution)/shard_map/all_gather | solution.py:444
  32.9 39.0 %collective-permute-start.8 = (bf16[2,2,160,384]{3,2,1,0:T(8,128)(2,1)S(1)}, bf16[2,2,160,384]{3,2,1,0:T(8,128)(2,1)}, u32[]{:S(2)}, u32[]{:S(2)}) collective-permute-start(bf16[2,2,160,384]{3,2,1,0:T(8,128)(2,1)S(1)} %dynamic-slice_bitcast_fusion.7), channel_id=1, source_target_pairs={{0,8},{8,0},{1,9},{9,1},{2,10},{10,2},{3,11},{11,3},{4,12},{12,4},... | collective-permute-start | bytes 1474568 | tf_op jit(solution)/shard_map/ppermute | solution.py:40
  46.7 17.6 %collective-permute-start.15 = (bf16[640,320]{0,1:T(8,128)(2,1)}, bf16[640,320]{0,1:T(8,128)(2,1)}, u32[]{:S(2)}, u32[]{:S(2)}) collective-permute-start(bf16[640,320]{0,1:T(8,128)(2,1)} %dynamic-slice_bitcast_fusion.11), channel_id=1, source_target_pairs={{0,8},{8,0},{1,9},{9,1},{2,10},{10,2},{3,11},{11,3},{4,12},{12,4},... | collective-permute-start | bytes 1228808 | tf_op jit(solution)/shard_map/ppermute | solution.py:40
  64.3 38.4 %collective-permute-start.7 = (bf16[384,1280]{1,0:T(8,128)(2,1)}, bf16[384,1280]{1,0:T(8,128)(2,1)}, u32[]{:S(2)}, u32[]{:S(2)}) collective-permute-start(bf16[384,1280]{1,0:T(8,128)(2,1)} %add_convert_fusion.11), channel_id=1, source_target_pairs={{0,2},{2,0},{1,3},{3,1},{4,6},{6,4},{5,7},{7,5},{8,10},{10,8},{9,1... | collective-permute-start | bytes 2949128 | tf_op jit(solution)/shard_map/ppermute | solution.py:40
  71.8 35.2 %collective-permute-start.4 = (bf16[384,1280]{1,0:T(8,128)(2,1)}, bf16[384,1280]{1,0:T(8,128)(2,1)}, u32[]{:S(2)}, u32[]{:S(2)}) collective-permute-start(bf16[384,1280]{1,0:T(8,128)(2,1)} %add_convert_fusion.11), channel_id=1, source_target_pairs={{0,8},{8,0},{1,9},{9,1},{2,10},{10,2},{3,11},{11,3},{4,12},{12,4},... | collective-permute-start | bytes 2949128 | tf_op jit(solution)/shard_map/ppermute | solution.py:40
  103.1 40.7 %all-to-all-start.1 = ((bf16[8,160,384]{2,1,0:T(8,128)(2,1)}), bf16[8,160,384]{2,1,0:T(8,128)(2,1)S(1)}, u32[]{:S(2)}, u32[]{:S(2)}) async-start(bf16[8,160,384]{2,1,0:T(8,128)(2,1)} %bitcast.43), calls=%async_computation.1 | async-start | bytes 1966080 | tf_op jit(solution)/shard_map/all_to_all | solution.py:430
  143.8 36.5 %collective-permute-start.11 = (bf16[384,1280]{1,0:T(8,128)(2,1)}, bf16[384,1280]{1,0:T(8,128)(2,1)}, u32[]{:S(2)}, u32[]{:S(2)}) collective-permute-start(bf16[384,1280]{1,0:T(8,128)(2,1)} %add_convert_fusion.10), channel_id=1, source_target_pairs={{0,2},{2,0},{1,3},{3,1},{4,6},{6,4},{5,7},{7,5},{8,10},{10,8},{9,1... | collective-permute-start | bytes 2949128 | tf_op jit(solution)/shard_map/ppermute | solution.py:40
  194.8 47.2 %collective-permute-start.16 = (bf16[384,1280]{1,0:T(8,128)(2,1)}, bf16[384,1280]{1,0:T(8,128)(2,1)}, u32[]{:S(2)}, u32[]{:S(2)}) collective-permute-start(bf16[384,1280]{1,0:T(8,128)(2,1)} %select_bitcast_fusion), channel_id=1, source_target_pairs={{0,2},{2,0},{1,3},{3,1},{4,6},{6,4},{5,7},{7,5},{8,10},{10,8},{9,1... | collective-permute-start | bytes 2949128 | tf_op jit(solution)/shard_map/ppermute | solution.py:40
  197.6 52.7 %collective-permute-start.13 = (bf16[384,1280]{1,0:T(8,128)(2,1)}, bf16[384,1280]{1,0:T(8,128)(2,1)}, u32[]{:S(2)}, u32[]{:S(2)}) collective-permute-start(bf16[384,1280]{1,0:T(8,128)(2,1)} %select_bitcast_fusion), channel_id=1, source_target_pairs={{0,8},{8,0},{1,9},{9,1},{2,10},{10,2},{3,11},{11,3},{4,12},{12,4},... | collective-permute-start | bytes 2949128 | tf_op jit(solution)/shard_map/ppermute | solution.py:40
  197.7 65.1 %collective-permute-start.17 = (bf16[384,1280]{1,0:T(8,128)(2,1)}, bf16[384,1280]{1,0:T(8,128)(2,1)}, u32[]{:S(2)}, u32[]{:S(2)}) collective-permute-start(bf16[384,1280]{1,0:T(8,128)(2,1)} %add_convert_fusion.9), channel_id=1, source_target_pairs={{0,2},{2,0},{1,3},{3,1},{4,6},{6,4},{5,7},{7,5},{8,10},{10,8},{9,1... | collective-permute-start | bytes 2949128 | tf_op jit(solution)/shard_map/ppermute | solution.py:40
  281.3 24.1 %collective-permute-start.22 = (bf16[384,1280]{1,0:T(8,128)(2,1)S(1)}, bf16[384,1280]{1,0:T(8,128)(2,1)S(1)}, u32[]{:S(2)}, u32[]{:S(2)}) collective-permute-start(bf16[384,1280]{1,0:T(8,128)(2,1)S(1)} %add_convert_fusion.8), channel_id=1, source_target_pairs={{0,2},{2,0},{1,3},{3,1},{4,6},{6,4},{5,7},{7,5},{8,10},{10,8},{9,1... | collective-permute-start | bytes 2949128 | tf_op jit(solution)/shard_map/ppermute | solution.py:40
  282.8 25.9 %collective-permute-start.21 = (bf16[384,1280]{1,0:T(8,128)(2,1)S(1)}, bf16[384,1280]{1,0:T(8,128)(2,1)S(1)}, u32[]{:S(2)}, u32[]{:S(2)}) collective-permute-start(bf16[384,1280]{1,0:T(8,128)(2,1)S(1)} %convolution_convert_fusion.8), channel_id=1, source_target_pairs={{0,8},{8,0},{1,9},{9,1},{2,10},{10,2},{3,11},{11,3},{4,12},{12,4},... | collective-permute-start | bytes 2949128 | tf_op jit(solution)/shard_map/ppermute | solution.py:40
  293.8 60.6 %collective-permute-start.26 = (bf16[2,320,1280]{2,1,0:T(8,128)(2,1)}, bf16[2,320,1280]{2,1,0:T(8,128)(2,1)}, u32[]{:S(2)}, u32[]{:S(2)}) collective-permute-start(bf16[2,320,1280]{2,1,0:T(8,128)(2,1)} %get-tuple-element.273), channel_id=1, source_target_pairs={{0,1},{1,0},{2,3},{3,2},{4,5},{5,4},{6,7},{7,6},{8,9},{9,8},{10,11... | collective-permute-start | bytes 4915208 | tf_op jit(solution)/shard_map/ppermute | solution.py:40
  314.5 18.4 %collective-permute-start.24 = (bf16[768,1280]{1,0:T(8,128)(2,1)}, bf16[768,1280]{1,0:T(8,128)(2,1)}, u32[]{:S(2)}, u32[]{:S(2)}) collective-permute-start(bf16[768,1280]{1,0:T(8,128)(2,1)} %pad_maximum_fusion.7), channel_id=1, source_target_pairs={{0,8},{8,0},{1,9},{9,1},{2,10},{10,2},{3,11},{11,3},{4,12},{12,4},... | collective-permute-start | bytes 5898248 | tf_op jit(solution)/shard_map/ppermute | solution.py:40
  324.7 37.7 %collective-permute-start.27 = (bf16[2,2,320,640]{3,2,1,0:T(8,128)(2,1)}, bf16[2,2,320,640]{3,2,1,0:T(8,128)(2,1)}, u32[]{:S(2)}, u32[]{:S(2)}) collective-permute-start(bf16[2,2,320,640]{3,2,1,0:T(8,128)(2,1)} %get-tuple-element.271), channel_id=1, source_target_pairs={{0,16},{16,0},{1,17},{17,1},{2,18},{18,2},{3,19},{19,3},{4,20},{20... | collective-permute-start | bytes 4915208 | tf_op jit(solution)/shard_map/ppermute | solution.py:40
  328.2 34.2 %collective-permute-start.25 = (bf16[384,1280]{1,0:T(8,128)(2,1)}, bf16[384,1280]{1,0:T(8,128)(2,1)}, u32[]{:S(2)}, u32[]{:S(2)}) collective-permute-start(bf16[384,1280]{1,0:T(8,128)(2,1)} %convert_element_type.313), channel_id=1, source_target_pairs={{0,2},{2,0},{1,3},{3,1},{4,6},{6,4},{5,7},{7,5},{8,10},{10,8},{9,1... | collective-permute-start | bytes 2949128 | tf_op jit(solution)/shard_map/ppermute | solution.py:40
  365.5 36.4 %collective-permute-start.30 = (bf16[2,320,640]{2,1,0:T(8,128)(2,1)}, bf16[2,320,640]{2,1,0:T(8,128)(2,1)}, u32[]{:S(2)}, u32[]{:S(2)}) collective-permute-start(bf16[2,320,640]{2,1,0:T(8,128)(2,1)} %get-tuple-element.283), channel_id=1, source_target_pairs={{0,16},{16,0},{1,17},{17,1},{2,18},{18,2},{3,19},{19,3},{4,20},{20... | collective-permute-start | bytes 2457608 | tf_op jit(solution)/shard_map/ppermute | solution.py:40
  370.2 31.7 %collective-permute-start.31 = (bf16[2,320,640]{2,1,0:T(8,128)(2,1)}, bf16[2,320,640]{2,1,0:T(8,128)(2,1)}, u32[]{:S(2)}, u32[]{:S(2)}) collective-permute-start(bf16[2,320,640]{2,1,0:T(8,128)(2,1)} %get-tuple-element.281), channel_id=1, source_target_pairs={{0,1},{1,0},{2,3},{3,2},{4,5},{5,4},{6,7},{7,6},{8,9},{9,8},{10,11... | collective-permute-start | bytes 2457608 | tf_op jit(solution)/shard_map/ppermute | solution.py:40
  371.7 27.4 %collective-permute-start.33 = (bf16[384,1280]{1,0:T(8,128)(2,1)}, bf16[384,1280]{1,0:T(8,128)(2,1)}, u32[]{:S(2)}, u32[]{:S(2)}) collective-permute-start(bf16[384,1280]{1,0:T(8,128)(2,1)} %add_convert_fusion.7), channel_id=1, source_target_pairs={{0,2},{2,0},{1,3},{3,1},{4,6},{6,4},{5,7},{7,5},{8,10},{10,8},{9,1... | collective-permute-start | bytes 2949128 | tf_op jit(solution)/shard_map/ppermute | solution.py:40
  404.5 23.7 %collective-permute-start.34 = (bf16[384,1280]{1,0:T(8,128)(2,1)S(1)}, bf16[384,1280]{1,0:T(8,128)(2,1)S(1)}, u32[]{:S(2)}, u32[]{:S(2)}) collective-permute-start(bf16[384,1280]{1,0:T(8,128)(2,1)S(1)} %add_convert_fusion.6), channel_id=1, source_target_pairs={{0,2},{2,0},{1,3},{3,1},{4,6},{6,4},{5,7},{7,5},{8,10},{10,8},{9,1... | collective-permute-start | bytes 2949128 | tf_op jit(solution)/shard_map/ppermute | solution.py:40
  432.0 64.3 %all-to-all-start.2 = ((bf16[8,160,384]{2,1,0:T(8,128)(2,1)}), bf16[8,160,384]{2,1,0:T(8,128)(2,1)S(1)}, u32[]{:S(2)}, u32[]{:S(2)}) async-start(bf16[8,160,384]{2,1,0:T(8,128)(2,1)} %bitcast.341), calls=%async_computation.2 | async-start | bytes 1966080 | tf_op jit(solution)/shard_map/all_to_all | solution.py:430
  439.9 19.8 %collective-permute-start.35 = (bf16[2,2,160,640]{3,2,1,0:T(8,128)(2,1)}, bf16[2,2,160,640]{3,2,1,0:T(8,128)(2,1)}, u32[]{:S(2)}, u32[]{:S(2)}) collective-permute-start(bf16[2,2,160,640]{3,2,1,0:T(8,128)(2,1)} %constant_dynamic-slice_fusion.14), channel_id=1, source_target_pairs={{0,16},{16,0},{1,17},{17,1},{2,18},{18,2},{3,19},{19,3},{4,20},{20... | collective-permute-start | bytes 2457608 | tf_op jit(solution)/shard_map/ppermute | solution.py:40
  448.2 23.3 %collective-permute-start.37 = (bf16[2,160,1280]{2,1,0:T(8,128)(2,1)}, bf16[2,160,1280]{2,1,0:T(8,128)(2,1)}, u32[]{:S(2)}, u32[]{:S(2)}) collective-permute-start(bf16[2,160,1280]{2,1,0:T(8,128)(2,1)} %dynamic-slice_bitcast_fusion.4), channel_id=1, source_target_pairs={{0,1},{1,0},{2,3},{3,2},{4,5},{5,4},{6,7},{7,6},{8,9},{9,8},{10,11... | collective-permute-start | bytes 2457608 | tf_op jit(solution)/shard_map/ppermute | solution.py:40
  453.0 26.5 %collective-permute-start.39 = (f32[2,2,2400]{2,1,0:T(2,128)S(1)}, f32[2,2,2400]{2,1,0:T(2,128)S(1)}, u32[]{:S(2)}, u32[]{:S(2)}) collective-permute-start(f32[2,2,2400]{2,1,0:T(2,128)S(1)} %concatenate.133), channel_id=1, source_target_pairs={{0,16},{16,0},{1,17},{17,1},{2,18},{18,2},{3,19},{19,3},{4,20},{20... | collective-permute-start | bytes 115208 | tf_op jit(solution)/shard_map/ppermute | solution.py:40
  456.5 39.8 %collective-permute-start.40 = (bf16[2,320,640]{2,1,0:T(8,128)(2,1)}, bf16[2,320,640]{2,1,0:T(8,128)(2,1)}, u32[]{:S(2)}, u32[]{:S(2)}) collective-permute-start(bf16[2,320,640]{2,1,0:T(8,128)(2,1)} %get-tuple-element.279), channel_id=1, source_target_pairs={{0,4},{4,0},{1,5},{5,1},{2,6},{6,2},{3,7},{7,3},{8,12},{12,8},{9,1... | collective-permute-start | bytes 2457608 | tf_op jit(solution)/shard_map/ppermute | solution.py:40
  462.3 34.0 %collective-permute-start.36 = (bf16[2,160,640]{2,1,0:T(8,128)(2,1)}, bf16[2,160,640]{2,1,0:T(8,128)(2,1)S(1)}, u32[]{:S(2)}, u32[]{:S(2)}) collective-permute-start(bf16[2,160,640]{2,1,0:T(8,128)(2,1)} %get-tuple-element.310), channel_id=1, source_target_pairs={{0,1},{1,0},{2,3},{3,2},{4,5},{5,4},{6,7},{7,6},{8,9},{9,8},{10,11... | collective-permute-start | bytes 1228808 | tf_op jit(solution)/shard_map/ppermute | solution.py:40
  473.9 22.5 %collective-permute-start.38 = (bf16[2,160,640]{2,1,0:T(8,128)(2,1)}, bf16[2,160,640]{2,1,0:T(8,128)(2,1)}, u32[]{:S(2)}, u32[]{:S(2)}) collective-permute-start(bf16[2,160,640]{2,1,0:T(8,128)(2,1)} %get-tuple-element.308), channel_id=1, source_target_pairs={{0,16},{16,0},{1,17},{17,1},{2,18},{18,2},{3,19},{19,3},{4,20},{20... | collective-permute-start | bytes 1228808 | tf_op jit(solution)/shard_map/ppermute | solution.py:40
  498.0 38.2 %all-to-all-start.3 = ((bf16[8,160,384]{2,1,0:T(8,128)(2,1)}), bf16[8,160,384]{2,1,0:T(8,128)(2,1)S(1)}, u32[]{:S(2)}, u32[]{:S(2)}) async-start(bf16[8,160,384]{2,1,0:T(8,128)(2,1)} %bitcast.91), calls=%async_computation.3 | async-start | bytes 1966080 | tf_op jit(solution)/shard_map/all_to_all | solution.py:430
  507.8 41.1 %collective-permute-start.44 = (bf16[2,160,640]{2,1,0:T(8,128)(2,1)}, bf16[2,160,640]{2,1,0:T(8,128)(2,1)}, u32[]{:S(2)}, u32[]{:S(2)}) collective-permute-start(bf16[2,160,640]{2,1,0:T(8,128)(2,1)} %get-tuple-element.306), channel_id=1, source_target_pairs={{0,4},{4,0},{1,5},{5,1},{2,6},{6,2},{3,7},{7,3},{8,12},{12,8},{9,1... | collective-permute-start | bytes 1228808 | tf_op jit(solution)/shard_map/ppermute | solution.py:40
  (110 other events, 852.3 us)
Sparse Core Ops, SparseCore 0:
  19.0 82.5 all-gather.5
  104.4 122.7 all-gather.3

commit v4 on v3

--- a/solution.py
+++ b/solution.py
@@ -613,9 +613,9 @@
 
     out_total = dot(active, grad_full, 0, 0).astype(BF).reshape(2, 2, half_units, width)
     in_total = dot(grad_hidden, normed_two, 0, 0).astype(BF).reshape(2, 2, half_units, width)
+    two_arrived, active, out_total, in_total = sync(send_far(far_two), active, out_total, in_total)
     out_half = send_units(out_total, "yh", 1)
     in_half = send_rows(in_total)
-    two_arrived, active = sync(send_far(far_two), active)
     grad_two = near_two + two_arrived
     grad_out = grad_low.astype(F32)
     grad_middle = grad_out + norm_backward(grad_two, normal_two, scale_two, gain_two)
@@ -664,7 +664,8 @@
     far_arrived, unit_sums = sync(far_arrived, unit_sums)
     unit_half = send_units(unit_sums, "zh", 1)
     context = jnp.concatenate([near_context, far_context], axis=0)
-    grads, near_one, delta_far, context, mid_full = sync(grads, near_one, delta_far, context, mid_full)
+    grads, near_one, delta_far, context, mid_rows = sync(grads, near_one, delta_far, context, mid_rows)
+    mid_full = jnp.concatenate(mid_rows, axis=0)
 
     def trim(total):
         return total.reshape(-1, part_heads, PAD, width)[:, :, :head_dim].reshape(-1, part_heads * head_dim, width)
@@ -684,8 +685,6 @@
     grad_tokens = norm_backward(grad_one, normal_one, scale_one, gain_one)
     last_part = (grad_middle + grad_tokens).astype(BF)
     moved_last = exchange(cut(last_part))
-    query_key_half = send_units(summed(query_key_half), "yh", 1)
-    value_attn_half = send_rows(summed(value_attn_half))
     delta = (attn_part + near_delta + delta_far + out_shift).astype(BF)
 
     full_sums = jnp.stack(
@@ -721,8 +720,12 @@
     full_size = full_sums[0, 0].size
     flat = jnp.concatenate([full_sums.reshape(2, 2, -1), part_sums.reshape(2, 2, -1)], axis=2)
     flat_pieces = pieces_of(flat, "x")
-    moved_last, query_key_half, value_attn_half, delta_blocks, flat_pieces, unit_half = sync(
-        moved_last, query_key_half, value_attn_half, cut(delta), flat_pieces, unit_half
+    query_key_half, value_attn_half, flat_pieces = sync(query_key_half, value_attn_half, flat_pieces)
+    query_key_half = send_units(summed(query_key_half), "yh", 1)
+    value_attn_half = send_rows(summed(value_attn_half))
+    flat_half = send_units(sum(flat_pieces), "yh", 1)
+    moved_last, query_key_half, value_attn_half, delta_blocks, flat_half, unit_half = sync(
+        moved_last, query_key_half, value_attn_half, cut(delta), flat_half, unit_half
     )
     moved_delta = exchange(delta_blocks)
     head_half = send_units(jnp.stack([summed(query_key_half), summed(value_attn_half)]), "zh", 1)
@@ -745,9 +748,9 @@
     def put(tokens, base=None):
         return put_positions(tokens, slot, pack_count, lanes, lines, base)
 
-    flat_half = send_units(sum(flat_pieces), "yh", 1)
+    flat_half = send_units(sum(flat_half), "zh", 0)
     input_grad, moved_delta, flat_half = sync(put(kept_tokens(moved_last)), moved_delta, flat_half)
-    flat = sum(send_units(sum(flat_half), "zh", 0))
+    flat = sum(flat_half)
     full_flat, part_flat = flat[:full_size], flat[full_size:]
 
     by_chip = full_flat.reshape(chips, -1)

time: 575 us -> 566 us (0.984)
    all_to_all x4, waiting for transfers between devices: 26 us -> 8.16 us  [exchange(): return lax.all_to_all(blocks, ('zh', 'zl', 'yh', 'yl'), 0, 0)]
    ppermute x50, waiting for transfers between devices: 155 us -> 168 us  [swap(): lax.ppermute(tensor, axis, [(i, i ^ step) for i in range(size_of(axis))])]
    unnamed x182 -> x185, local copies, waits for them, and re-layouts: 22.2 us -> 22.9 us
  transfers between devices with their start and end apart: 56 -> 56, of which waited for: 20 -> 21; matrix products, arithmetic and copies ran while one was open for 37% -> 36% of each run, Pallas kernels for 11% -> 11%
where the time goes in v4:
time: 566 us; the launch traced here: 562 us
  waiting for transfers between devices  176 us (31%)
  matrix products  99.2 us (18%)
  other arithmetic  74.6 us (13%)
  Pallas kernels  73.3 us (13%)
  local copies, waits for them, and re-layouts  68 us (12%)
  starting transfers between devices  53.6 us (9%)
  between operations  16.3 us (3%)
    ppermute x50, waiting for transfers between devices, swap(): lax.ppermute(tensor, axis, [(i, i ^ step) for i in range(size_of(axis))])  168 us
    dot_general x38, matrix products, dot(): lax.dot_general(first, second, (((left,), (right,)), ((), ())), preferred...  99.2 us
    ppermute x50, starting transfers between devices, swap(): lax.ppermute(tensor, axis, [(i, i ^ step) for i in range(size_of(axis))])  36.2 us
    pallas_call x2, Pallas kernels, attend_back(): pl.pallas_call(functools.partial(body, head_dim), grid=(heads,), in_specs...  28 us
    unnamed x185, local copies, waits for them, and re-layouts  22.9 us
    pallas_call x2, Pallas kernels, attend(): pl.pallas_call(forward_body, grid=(heads,), in_specs=[pl.BlockSpec((block...  22.9 us
    all_to_all x4, starting transfers between devices, exchange(): return lax.all_to_all(blocks, ('zh', 'zl', 'yh', 'yl'), 0, 0)  17.2 us
    pallas_call x2, Pallas kernels, put_positions(): pl.pallas_call(functools.partial(put_body, rows, lanes, lines, base is no...  12.8 us
  transfers between devices with their start and end apart: 56, of which 21 were waited for; matrix products, arithmetic and copies ran while one was open for 36% of the time, Pallas kernels for 11%

profile of v4, /device:TPU:0, one launch (start us, length us, event | category | flops | bytes accessed | tf_op | source)
XLA Modules:
  0.0 561.5 jit_solution(9271409214174239593)
XLA Ops:
  8.8 3.8 shard_map.305
  50.2 7.8 %all-to-all-done = bf16[8,160,384]{2,1,0:T(8,128)(2,1)S(1)} async-done(((bf16[8,160,384]{2,1,0:T(8,128)(2,1)}), bf16[8,160,384]{2,1,0:T(8,128)(2,1)S(1)}, u32[]{:S(2)}, u32[]{:S(2)}) %all-to-all-start) | async-done | bytes 983072 | tf_op jit(solution)/shard_map/all_to_all | solution.py:430
  74.2 28.5 %collective-permute-done.7 = bf16[384,1280]{1,0:T(8,128)(2,1)} collective-permute-done((bf16[384,1280]{1,0:T(8,128)(2,1)}, bf16[384,1280]{1,0:T(8,128)(2,1)}, u32[]{:S(2)}, u32[]{:S(2)}) %collective-permute-start.7) | collective-permute-done | bytes 983072 | tf_op jit(solution)/shard_map/ppermute | solution.py:40
  103.1 3.9 all-to-all-start.1
  113.1 6.5 %add_convert_fusion = bf16[768,1536]{1,0:T(8,128)(2,1)S(1)} fusion(bf16[2048,1280]{1,0:T(8,128)(2,1)S(1)} %shard_map.306, f32[768]{0:T(1024)S(1)} %get-tuple-element.359, f32[1536]{0:T(1024)S(1)} %get-tuple-element.367, f32[1536]{0:T(1024)S(1)} %get-tuple-element.366, f32[1536]{0:T(1024)S(1)} %copy-done.84, f32[1536]{0:T(1024)S(1)} %get-tuple-element.372, ...), kind=kOutput, calls=%fused_computation.6 | convolution fusion | flops 3030908928 | bytes 8294400 | tf_op jit(solution)/shard_map/dot_general | solution.py:22
  125.9 11.5 %shard_map.308 = (bf16[768,512]{1,0:T(8,128)(2,1)S(1)}, f32[768,512]{1,0:T(8,128)S(1)}, bf16[4,1536,768]{2,1,0:T(8,128)(2,1)}) custom-call(bf16[1536,1536]{1,0:T(8,128)(2,1)} %pad_maximum_fusion.query_ref.key_ref.value_ref.query.key.value, bf16[1536,1536]{1,0:T(8,128)(2,1)} %pad_maximum_fusion.query_ref.key_ref.value_ref.query.key.value, ...), custom_call_target="tpu_custom_call" | custom-call | flops 1000 | bytes 1000 | tf_op jit(solution)/shard_map/pallas_call | solution.py:262
  145.4 3.8 pad_maximum_fusion.1
  149.2 11.4 %shard_map.309 = (bf16[768,512]{1,0:T(8,128)(2,1)S(1)}, f32[768,512]{1,0:T(8,128)S(1)}, bf16[4,1536,768]{2,1,0:T(8,128)(2,1)}) custom-call(bf16[1536,1536]{1,0:T(8,128)(2,1)} %pad_maximum_fusion.query_ref.key_ref.value_ref.query.key.value, bf16[1536,1536]{1,0:T(8,128)(2,1)} %pad_maximum_fusion.query_ref.key_ref.value_ref.query.key.value, ...), custom_call_target="tpu_custom_call" | custom-call | flops 1000 | bytes 1000 | tf_op jit(solution)/shard_map/pallas_call | solution.py:262
  167.1 13.2 %collective-permute-done.11 = bf16[384,1280]{1,0:T(8,128)(2,1)} collective-permute-done((bf16[384,1280]{1,0:T(8,128)(2,1)}, bf16[384,1280]{1,0:T(8,128)(2,1)}, u32[]{:S(2)}, u32[]{:S(2)}) %collective-permute-start.11) | collective-permute-done | bytes 983072 | tf_op jit(solution)/shard_map/ppermute | solution.py:40
  188.7 4.3 fusion.169
  199.3 42.7 %collective-permute-done.16 = bf16[384,1280]{1,0:T(8,128)(2,1)} collective-permute-done((bf16[384,1280]{1,0:T(8,128)(2,1)}, bf16[384,1280]{1,0:T(8,128)(2,1)}, u32[]{:S(2)}, u32[]{:S(2)}) %collective-permute-start.16) | collective-permute-done | bytes 983072 | tf_op jit(solution)/shard_map/ppermute | solution.py:40
  245.5 4.1 multiply_convert_fusion.1
  250.3 5.6 fusion.26
  255.9 6.9 %collective-permute-done.17 = bf16[384,1280]{1,0:T(8,128)(2,1)} collective-permute-done((bf16[384,1280]{1,0:T(8,128)(2,1)}, bf16[384,1280]{1,0:T(8,128)(2,1)}, u32[]{:S(2)}, u32[]{:S(2)}) %collective-permute-start.17) | collective-permute-done | bytes 983072 | tf_op jit(solution)/shard_map/ppermute | solution.py:40
  266.0 4.7 multiply_convert_fusion
  270.6 5.0 fusion.27
  283.3 7.4 %convolution_convert_fusion.1 = bf16[1280,1280]{1,0:T(8,128)(2,1)S(1)} fusion(bf16[1536,1280]{1,0:T(8,128)(2,1)S(1)} %pad_maximum_fusion.3, bf16[384,1280]{1,0:T(8,128)(2,1)S(1)} %collective-permute-done.18, bf16[384,1280]{1,0:T(8,128)(2,1)} %collective-permute-done.16, bf16[384,1280]{1,0:T(8,128)(2,1)} %collective-permute-done.13, ...), kind=kOutput, calls=%fused_computation.2 | convolution fusion | flops 5050531840 | bytes 11141120 | tf_op jit(solution)/shard_map/dot_general | solution.py:22
  290.7 7.6 %convolution_convert_fusion = bf16[1280,1280]{1,0:T(8,128)(2,1)S(1)} fusion(bf16[1536,1280]{1,0:T(8,128)(2,1)S(1)} %pad_maximum_fusion.2, bf16[384,1280]{1,0:T(8,128)(2,1)} %collective-permute-done.19, bf16[384,1280]{1,0:T(8,128)(2,1)} %collective-permute-done.17, bf16[768,1280]{1,0:T(8,128)(2,1)S(1)} %copy-done.42), kind=kOutput, calls=%fused_computation.1 | convolution fusion | flops 5046599680 | bytes 11141120 | tf_op jit(solution)/shard_map/dot_general | solution.py:22
  299.7 5.7 %collective-permute-done.22 = bf16[384,1280]{1,0:T(8,128)(2,1)S(1)} collective-permute-done((bf16[384,1280]{1,0:T(8,128)(2,1)S(1)}, bf16[384,1280]{1,0:T(8,128)(2,1)S(1)}, u32[]{:S(2)}, u32[]{:S(2)}) %collective-permute-start.22) | collective-permute-done | bytes 983072 | tf_op jit(solution)/shard_map/ppermute | solution.py:40
  325.5 4.0 convolution_convert_fusion.12.grad
  332.6 3.9 convert_add_fusion.2
  340.1 13.5 %shard_map.312 = (bf16[768,512]{1,0:T(8,128)(2,1)}, f32[1536,512]{1,0:T(8,128)}, f32[1536,512]{1,0:T(8,128)}) custom-call(bf16[1536,1536]{1,0:T(8,128)(2,1)} %pad_maximum_fusion.query_ref.key_ref.value_ref.query.key.value, bf16[1536,1536]{1,0:T(8,128)(2,1)} %pad_maximum_fusion.query_ref.key_ref.value_ref.query.key.value, ...), custom_call_target="tpu_custom_call" | custom-call | flops 1000 | bytes 1000 | tf_op jit(solution)/shard_map/pallas_call | solution.py:350
  372.6 14.5 %shard_map.313 = bf16[3,1536,512]{2,1,0:T(8,128)(2,1)} custom-call(bf16[1536,1536]{1,0:T(8,128)(2,1)} %pad_maximum_fusion.query_ref.key_ref.value_ref.query.key.value, bf16[1536,1536]{1,0:T(8,128)(2,1)} %pad_maximum_fusion.query_ref.key_ref.value_ref.query.key.value, bf16[1536,1536]{1,0:T(8,128)(2,1)} %pad_maximum_fusion.query_ref.key_ref.value_ref.query.key.value, ...), custom_call_target="tpu_custom_call" | custom-call | flops 1000 | bytes 1000 | tf_op jit(solution)/shard_map/pallas_call | solution.py:350
  417.9 4.3 collective-permute-done.34
  425.8 6.0 %all-to-all-start.2 = ((bf16[8,160,384]{2,1,0:T(8,128)(2,1)}), bf16[8,160,384]{2,1,0:T(8,128)(2,1)S(1)}, u32[]{:S(2)}, u32[]{:S(2)}) async-start(bf16[8,160,384]{2,1,0:T(8,128)(2,1)} %bitcast.338), calls=%async_computation.2 | async-start | bytes 1966080 | tf_op jit(solution)/shard_map/all_to_all | solution.py:430
  455.1 8.8 %collective-permute-done.36 = bf16[2,160,1280]{2,1,0:T(8,128)(2,1)} collective-permute-done((bf16[2,160,1280]{2,1,0:T(8,128)(2,1)}, bf16[2,160,1280]{2,1,0:T(8,128)(2,1)}, u32[]{:S(2)}, u32[]{:S(2)}) %collective-permute-start.36) | collective-permute-done | bytes 819232 | tf_op jit(solution)/shard_map/ppermute | solution.py:40
  476.8 14.2 %collective-permute-done.41 = bf16[2,320,640]{2,1,0:T(8,128)(2,1)} collective-permute-done((bf16[2,320,640]{2,1,0:T(8,128)(2,1)}, bf16[2,320,640]{2,1,0:T(8,128)(2,1)}, u32[]{:S(2)}, u32[]{:S(2)}) %collective-permute-start.41) | collective-permute-done | bytes 819232 | tf_op jit(solution)/shard_map/ppermute | solution.py:40
  493.5 3.8 all-to-all-start.3
  509.0 6.4 %shard_map.314 = f32[375,1280]{1,0:T(8,128)} custom-call(bf16[2,2,2,160,384]{4,3,2,1,0:T(8,128)(2,1)S(1)} %maximum_bitcast_fusion.2.refs_0_), custom_call_target="tpu_custom_call" | custom-call | flops 1000 | bytes 1000 | tf_op jit(solution)/shard_map/pallas_call | solution.py:235
  515.4 16.8 %collective-permute-done.43 = f32[2400]{0:T(1024)S(1)} collective-permute-done((f32[2400]{0:T(1024)S(1)}, f32[2400]{0:T(1024)S(1)}, u32[]{:S(2)}, u32[]{:S(2)}) %collective-permute-start.43) | collective-permute-done | bytes 9632 | tf_op jit(solution)/shard_map/ppermute | solution.py:40
  536.3 4.5 collective-permute-done.45
  548.0 6.4 %shard_map.315 = f32[375,1280]{1,0:T(8,128)} custom-call(f32[375,1280]{1,0:T(8,128)S(1)} %copy-done.3, bf16[2,2,2,160,384]{4,3,2,1,0:T(8,128)(2,1)S(1)} %maximum_bitcast_fusion.3.refs_1_), custom_call_target="tpu_custom_call" | custom-call | flops 1000 | bytes 1000 | tf_op jit(solution)/shard_map/pallas_call | solution.py:235
  (521 shorter events, 253.9 us)
Async XLA Ops:
  7.2 102.8 %all-gather.6.cloned.1.call-start = ((), (), s32[]{:S(2)}) async-start(), calls=%async_computation.5 | async-start | bytes 3686400 | tf_op jit(solution)/shard_map/all_gather | solution.py:444
  22.7 21.2 %collective-permute-start.2 = (f32[2880]{0:T(1024)S(1)}, f32[2880]{0:T(1024)S(1)}, u32[]{:S(2)}, u32[]{:S(2)}) collective-permute-start(f32[2880]{0:T(1024)S(1)} %concatenate.104), channel_id=1, source_target_pairs={{0,4},{4,0},{1,5},{5,1},{2,6},{6,2},{3,7},{7,3},{8,12},{12,8},{9,1... | collective-permute-start | bytes 34568 | tf_op jit(solution)/shard_map/ppermute | solution.py:40
  25.3 32.8 %all-to-all-start = ((bf16[8,160,384]{2,1,0:T(8,128)(2,1)}), bf16[8,160,384]{2,1,0:T(8,128)(2,1)S(1)}, u32[]{:S(2)}, u32[]{:S(2)}) async-start(bf16[8,160,384]{2,1,0:T(8,128)(2,1)} %bitcast.6), calls=%async_computation | async-start | bytes 1966080 | tf_op jit(solution)/shard_map/all_to_all | solution.py:430
  28.9 213.1 %all-gather.4.cloned.1.call-start = ((), (), s32[]{:S(2)}) async-start(), calls=%async_computation.4 | async-start | bytes 7372800 | tf_op jit(solution)/shard_map/all_gather | solution.py:444
  32.9 39.0 %collective-permute-start.8 = (bf16[2,2,160,384]{3,2,1,0:T(8,128)(2,1)S(1)}, bf16[2,2,160,384]{3,2,1,0:T(8,128)(2,1)}, u32[]{:S(2)}, u32[]{:S(2)}) collective-permute-start(bf16[2,2,160,384]{3,2,1,0:T(8,128)(2,1)S(1)} %dynamic-slice_bitcast_fusion.8), channel_id=1, source_target_pairs={{0,8},{8,0},{1,9},{9,1},{2,10},{10,2},{3,11},{11,3},{4,12},{12,4},... | collective-permute-start | bytes 1474568 | tf_op jit(solution)/shard_map/ppermute | solution.py:40
  64.3 38.4 %collective-permute-start.7 = (bf16[384,1280]{1,0:T(8,128)(2,1)}, bf16[384,1280]{1,0:T(8,128)(2,1)}, u32[]{:S(2)}, u32[]{:S(2)}) collective-permute-start(bf16[384,1280]{1,0:T(8,128)(2,1)} %add_convert_fusion.11), channel_id=1, source_target_pairs={{0,2},{2,0},{1,3},{3,1},{4,6},{6,4},{5,7},{7,5},{8,10},{10,8},{9,1... | collective-permute-start | bytes 2949128 | tf_op jit(solution)/shard_map/ppermute | solution.py:40
  71.8 35.2 %collective-permute-start.4 = (bf16[384,1280]{1,0:T(8,128)(2,1)}, bf16[384,1280]{1,0:T(8,128)(2,1)}, u32[]{:S(2)}, u32[]{:S(2)}) collective-permute-start(bf16[384,1280]{1,0:T(8,128)(2,1)} %add_convert_fusion.11), channel_id=1, source_target_pairs={{0,8},{8,0},{1,9},{9,1},{2,10},{10,2},{3,11},{11,3},{4,12},{12,4},... | collective-permute-start | bytes 2949128 | tf_op jit(solution)/shard_map/ppermute | solution.py:40
  103.1 40.7 %all-to-all-start.1 = ((bf16[8,160,384]{2,1,0:T(8,128)(2,1)}), bf16[8,160,384]{2,1,0:T(8,128)(2,1)S(1)}, u32[]{:S(2)}, u32[]{:S(2)}) async-start(bf16[8,160,384]{2,1,0:T(8,128)(2,1)} %bitcast.43), calls=%async_computation.1 | async-start | bytes 1966080 | tf_op jit(solution)/shard_map/all_to_all | solution.py:430
  143.8 36.5 %collective-permute-start.11 = (bf16[384,1280]{1,0:T(8,128)(2,1)}, bf16[384,1280]{1,0:T(8,128)(2,1)}, u32[]{:S(2)}, u32[]{:S(2)}) collective-permute-start(bf16[384,1280]{1,0:T(8,128)(2,1)} %add_convert_fusion.10), channel_id=1, source_target_pairs={{0,2},{2,0},{1,3},{3,1},{4,6},{6,4},{5,7},{7,5},{8,10},{10,8},{9,1... | collective-permute-start | bytes 2949128 | tf_op jit(solution)/shard_map/ppermute | solution.py:40
  194.8 47.2 %collective-permute-start.16 = (bf16[384,1280]{1,0:T(8,128)(2,1)}, bf16[384,1280]{1,0:T(8,128)(2,1)}, u32[]{:S(2)}, u32[]{:S(2)}) collective-permute-start(bf16[384,1280]{1,0:T(8,128)(2,1)} %select_bitcast_fusion), channel_id=1, source_target_pairs={{0,2},{2,0},{1,3},{3,1},{4,6},{6,4},{5,7},{7,5},{8,10},{10,8},{9,1... | collective-permute-start | bytes 2949128 | tf_op jit(solution)/shard_map/ppermute | solution.py:40
  197.6 52.7 %collective-permute-start.13 = (bf16[384,1280]{1,0:T(8,128)(2,1)}, bf16[384,1280]{1,0:T(8,128)(2,1)}, u32[]{:S(2)}, u32[]{:S(2)}) collective-permute-start(bf16[384,1280]{1,0:T(8,128)(2,1)} %select_bitcast_fusion), channel_id=1, source_target_pairs={{0,8},{8,0},{1,9},{9,1},{2,10},{10,2},{3,11},{11,3},{4,12},{12,4},... | collective-permute-start | bytes 2949128 | tf_op jit(solution)/shard_map/ppermute | solution.py:40
  197.7 65.1 %collective-permute-start.17 = (bf16[384,1280]{1,0:T(8,128)(2,1)}, bf16[384,1280]{1,0:T(8,128)(2,1)}, u32[]{:S(2)}, u32[]{:S(2)}) collective-permute-start(bf16[384,1280]{1,0:T(8,128)(2,1)} %add_convert_fusion.9), channel_id=1, source_target_pairs={{0,2},{2,0},{1,3},{3,1},{4,6},{6,4},{5,7},{7,5},{8,10},{10,8},{9,1... | collective-permute-start | bytes 2949128 | tf_op jit(solution)/shard_map/ppermute | solution.py:40
  281.3 24.1 %collective-permute-start.22 = (bf16[384,1280]{1,0:T(8,128)(2,1)S(1)}, bf16[384,1280]{1,0:T(8,128)(2,1)S(1)}, u32[]{:S(2)}, u32[]{:S(2)}) collective-permute-start(bf16[384,1280]{1,0:T(8,128)(2,1)S(1)} %add_convert_fusion.8), channel_id=1, source_target_pairs={{0,2},{2,0},{1,3},{3,1},{4,6},{6,4},{5,7},{7,5},{8,10},{10,8},{9,1... | collective-permute-start | bytes 2949128 | tf_op jit(solution)/shard_map/ppermute | solution.py:40
  282.8 25.6 %collective-permute-start.21 = (bf16[384,1280]{1,0:T(8,128)(2,1)S(1)}, bf16[384,1280]{1,0:T(8,128)(2,1)S(1)}, u32[]{:S(2)}, u32[]{:S(2)}) collective-permute-start(bf16[384,1280]{1,0:T(8,128)(2,1)S(1)} %convolution_convert_fusion.7), channel_id=1, source_target_pairs={{0,8},{8,0},{1,9},{9,1},{2,10},{10,2},{3,11},{11,3},{4,12},{12,4},... | collective-permute-start | bytes 2949128 | tf_op jit(solution)/shard_map/ppermute | solution.py:40
  311.1 21.5 %collective-permute-start.24 = (bf16[768,1280]{1,0:T(8,128)(2,1)}, bf16[768,1280]{1,0:T(8,128)(2,1)}, u32[]{:S(2)}, u32[]{:S(2)}) collective-permute-start(bf16[768,1280]{1,0:T(8,128)(2,1)} %pad_maximum_fusion.7), channel_id=1, source_target_pairs={{0,8},{8,0},{1,9},{9,1},{2,10},{10,2},{3,11},{11,3},{4,12},{12,4},... | collective-permute-start | bytes 5898248 | tf_op jit(solution)/shard_map/ppermute | solution.py:40
  319.1 38.0 %collective-permute-start.26 = (bf16[2,320,1280]{2,1,0:T(8,128)(2,1)}, bf16[2,320,1280]{2,1,0:T(8,128)(2,1)}, u32[]{:S(2)}, u32[]{:S(2)}) collective-permute-start(bf16[2,320,1280]{2,1,0:T(8,128)(2,1)} %get-tuple-element.291), channel_id=1, source_target_pairs={{0,1},{1,0},{2,3},{3,2},{4,5},{5,4},{6,7},{7,6},{8,9},{9,8},{10,11... | collective-permute-start | bytes 4915208 | tf_op jit(solution)/shard_map/ppermute | solution.py:40
  322.8 37.7 %collective-permute-start.27 = (bf16[2,2,320,640]{3,2,1,0:T(8,128)(2,1)}, bf16[2,2,320,640]{3,2,1,0:T(8,128)(2,1)}, u32[]{:S(2)}, u32[]{:S(2)}) collective-permute-start(bf16[2,2,320,640]{3,2,1,0:T(8,128)(2,1)} %get-tuple-element.289), channel_id=1, source_target_pairs={{0,16},{16,0},{1,17},{17,1},{2,18},{18,2},{3,19},{19,3},{4,20},{20... | collective-permute-start | bytes 4915208 | tf_op jit(solution)/shard_map/ppermute | solution.py:40
  324.9 28.7 %collective-permute-start.25 = (bf16[384,1280]{1,0:T(8,128)(2,1)}, bf16[384,1280]{1,0:T(8,128)(2,1)}, u32[]{:S(2)}, u32[]{:S(2)}) collective-permute-start(bf16[384,1280]{1,0:T(8,128)(2,1)} %convert_element_type.312), channel_id=1, source_target_pairs={{0,2},{2,0},{1,3},{3,1},{4,6},{6,4},{5,7},{7,5},{8,10},{10,8},{9,1... | collective-permute-start | bytes 2949128 | tf_op jit(solution)/shard_map/ppermute | solution.py:40
  363.7 32.1 %collective-permute-start.30 = (bf16[2,320,640]{2,1,0:T(8,128)(2,1)}, bf16[2,320,640]{2,1,0:T(8,128)(2,1)}, u32[]{:S(2)}, u32[]{:S(2)}) collective-permute-start(bf16[2,320,640]{2,1,0:T(8,128)(2,1)} %get-tuple-element.305), channel_id=1, source_target_pairs={{0,16},{16,0},{1,17},{17,1},{2,18},{18,2},{3,19},{19,3},{4,20},{20... | collective-permute-start | bytes 2457608 | tf_op jit(solution)/shard_map/ppermute | solution.py:40
  368.2 27.6 %collective-permute-start.31 = (bf16[2,320,640]{2,1,0:T(8,128)(2,1)}, bf16[2,320,640]{2,1,0:T(8,128)(2,1)}, u32[]{:S(2)}, u32[]{:S(2)}) collective-permute-start(bf16[2,320,640]{2,1,0:T(8,128)(2,1)} %get-tuple-element.303), channel_id=1, source_target_pairs={{0,1},{1,0},{2,3},{3,2},{4,5},{5,4},{6,7},{7,6},{8,9},{9,8},{10,11... | collective-permute-start | bytes 2457608 | tf_op jit(solution)/shard_map/ppermute | solution.py:40
  368.8 24.2 %collective-permute-start.33 = (bf16[384,1280]{1,0:T(8,128)(2,1)}, bf16[384,1280]{1,0:T(8,128)(2,1)}, u32[]{:S(2)}, u32[]{:S(2)}) collective-permute-start(bf16[384,1280]{1,0:T(8,128)(2,1)} %add_convert_fusion.7), channel_id=1, source_target_pairs={{0,2},{2,0},{1,3},{3,1},{4,6},{6,4},{5,7},{7,5},{8,10},{10,8},{9,1... | collective-permute-start | bytes 2949128 | tf_op jit(solution)/shard_map/ppermute | solution.py:40
  398.4 23.7 %collective-permute-start.34 = (bf16[384,1280]{1,0:T(8,128)(2,1)S(1)}, bf16[384,1280]{1,0:T(8,128)(2,1)S(1)}, u32[]{:S(2)}, u32[]{:S(2)}) collective-permute-start(bf16[384,1280]{1,0:T(8,128)(2,1)S(1)} %add_convert_fusion.6), channel_id=1, source_target_pairs={{0,2},{2,0},{1,3},{3,1},{4,6},{6,4},{5,7},{7,5},{8,10},{10,8},{9,1... | collective-permute-start | bytes 2949128 | tf_op jit(solution)/shard_map/ppermute | solution.py:40
  425.8 65.2 %all-to-all-start.2 = ((bf16[8,160,384]{2,1,0:T(8,128)(2,1)}), bf16[8,160,384]{2,1,0:T(8,128)(2,1)S(1)}, u32[]{:S(2)}, u32[]{:S(2)}) async-start(bf16[8,160,384]{2,1,0:T(8,128)(2,1)} %bitcast.338), calls=%async_computation.2 | async-start | bytes 1966080 | tf_op jit(solution)/shard_map/all_to_all | solution.py:430
  435.0 20.2 %collective-permute-start.35 = (bf16[2,2,160,640]{3,2,1,0:T(8,128)(2,1)}, bf16[2,2,160,640]{3,2,1,0:T(8,128)(2,1)}, u32[]{:S(2)}, u32[]{:S(2)}) collective-permute-start(bf16[2,2,160,640]{3,2,1,0:T(8,128)(2,1)} %get-tuple-element.301), channel_id=1, source_target_pairs={{0,16},{16,0},{1,17},{17,1},{2,18},{18,2},{3,19},{19,3},{4,20},{20... | collective-permute-start | bytes 2457608 | tf_op jit(solution)/shard_map/ppermute | solution.py:40
  441.8 22.1 %collective-permute-start.36 = (bf16[2,160,1280]{2,1,0:T(8,128)(2,1)}, bf16[2,160,1280]{2,1,0:T(8,128)(2,1)}, u32[]{:S(2)}, u32[]{:S(2)}) collective-permute-start(bf16[2,160,1280]{2,1,0:T(8,128)(2,1)} %get-tuple-element.299), channel_id=1, source_target_pairs={{0,1},{1,0},{2,3},{3,2},{4,5},{5,4},{6,7},{7,6},{8,9},{9,8},{10,11... | collective-permute-start | bytes 2457608 | tf_op jit(solution)/shard_map/ppermute | solution.py:40
  450.1 40.9 %collective-permute-start.41 = (bf16[2,320,640]{2,1,0:T(8,128)(2,1)}, bf16[2,320,640]{2,1,0:T(8,128)(2,1)}, u32[]{:S(2)}, u32[]{:S(2)}) collective-permute-start(bf16[2,320,640]{2,1,0:T(8,128)(2,1)} %get-tuple-element.297), channel_id=1, source_target_pairs={{0,4},{4,0},{1,5},{5,1},{2,6},{6,2},{3,7},{7,3},{8,12},{12,8},{9,1... | collective-permute-start | bytes 2457608 | tf_op jit(solution)/shard_map/ppermute | solution.py:40
  466.4 24.6 %collective-permute-start.38 = (bf16[2,160,640]{2,1,0:T(8,128)(2,1)}, bf16[2,160,640]{2,1,0:T(8,128)(2,1)S(1)}, u32[]{:S(2)}, u32[]{:S(2)}) collective-permute-start(bf16[2,160,640]{2,1,0:T(8,128)(2,1)} %get-tuple-element.332), channel_id=1, source_target_pairs={{0,1},{1,0},{2,3},{3,2},{4,5},{5,4},{6,7},{7,6},{8,9},{9,8},{10,11... | collective-permute-start | bytes 1228808 | tf_op jit(solution)/shard_map/ppermute | solution.py:40
  469.1 22.0 %collective-permute-start.39 = (bf16[2,160,640]{2,1,0:T(8,128)(2,1)}, bf16[2,160,640]{2,1,0:T(8,128)(2,1)}, u32[]{:S(2)}, u32[]{:S(2)}) collective-permute-start(bf16[2,160,640]{2,1,0:T(8,128)(2,1)} %get-tuple-element.330), channel_id=1, source_target_pairs={{0,16},{16,0},{1,17},{17,1},{2,18},{18,2},{3,19},{19,3},{4,20},{20... | collective-permute-start | bytes 1228808 | tf_op jit(solution)/shard_map/ppermute | solution.py:40
  469.8 21.2 %collective-permute-start.40 = (f32[2,2400]{1,0:T(2,128)S(1)}, f32[2,2400]{1,0:T(2,128)S(1)}, u32[]{:S(2)}, u32[]{:S(2)}) collective-permute-start(f32[2,2400]{1,0:T(2,128)S(1)} %bitcast.366), channel_id=1, source_target_pairs={{0,1},{1,0},{2,3},{3,2},{4,5},{5,4},{6,7},{7,6},{8,9},{9,8},{10,11... | collective-permute-start | bytes 57608 | tf_op jit(solution)/shard_map/ppermute | solution.py:40
  493.5 38.7 %all-to-all-start.3 = ((bf16[8,160,384]{2,1,0:T(8,128)(2,1)}), bf16[8,160,384]{2,1,0:T(8,128)(2,1)S(1)}, u32[]{:S(2)}, u32[]{:S(2)}) async-start(bf16[8,160,384]{2,1,0:T(8,128)(2,1)} %bitcast.96), calls=%async_computation.3 | async-start | bytes 1966080 | tf_op jit(solution)/shard_map/all_to_all | solution.py:430
  497.4 34.8 %collective-permute-start.43 = (f32[2400]{0:T(1024)S(1)}, f32[2400]{0:T(1024)S(1)}, u32[]{:S(2)}, u32[]{:S(2)}) collective-permute-start(f32[2400]{0:T(1024)S(1)} %get-tuple-element.277), channel_id=1, source_target_pairs={{0,4},{4,0},{1,5},{5,1},{2,6},{6,2},{3,7},{7,3},{8,12},{12,8},{9,1... | collective-permute-start | bytes 28808 | tf_op jit(solution)/shard_map/ppermute | solution.py:40
  504.3 36.5 %collective-permute-start.45 = (bf16[2,160,640]{2,1,0:T(8,128)(2,1)}, bf16[2,160,640]{2,1,0:T(8,128)(2,1)}, u32[]{:S(2)}, u32[]{:S(2)}) collective-permute-start(bf16[2,160,640]{2,1,0:T(8,128)(2,1)} %get-tuple-element.328), channel_id=1, source_target_pairs={{0,4},{4,0},{1,5},{5,1},{2,6},{6,2},{3,7},{7,3},{8,12},{12,8},{9,1... | collective-permute-start | bytes 1228808 | tf_op jit(solution)/shard_map/ppermute | solution.py:40
  (111 other events, 835.4 us)
Sparse Core Ops, SparseCore 0:
  18.9 82.5 all-gather.5
  104.3 122.7 all-gather.3

commit v5 on v4

--- a/solution.py
+++ b/solution.py
@@ -575,9 +575,10 @@
     attn_part = near_sums[0] + far_total + attn_shift
     middle = tokens + attn_part
     normal_two, scale_two, normed_two_part = norm_forward(middle, gain_two, shift_two)
+    normed_two_part, grad_far = sync(normed_two_part, grad_far)
     two_near = with_core(normed_two_part)
     two_far = far_pieces(normed_two_part)
-    two_near, unit_stacked, grad_far = sync(two_near, unit_stacked, grad_far)
+    two_near, unit_stacked = sync(two_near, unit_stacked)
     in_weights = arrange_units(unit_stacked, 0)
     out_weights = arrange_units(unit_stacked, 1)
 

time: 566 us -> 561 us (level)
    unnamed x185 -> x189, local copies, waits for them, and re-layouts: 22.9 us -> 24.6 us
  transfers between devices with their start and end apart: 56 -> 56, of which waited for: 21 -> 22; matrix products, arithmetic and copies ran while one was open for 36% -> 37% of each run, Pallas kernels for 11% -> 11%
where the time goes in v5:
time: 561 us; the launch traced here: 557 us
  waiting for transfers between devices  171 us (30%)
  matrix products  98.2 us (18%)
  other arithmetic  74.7 us (13%)
  Pallas kernels  73.3 us (13%)
  local copies, waits for them, and re-layouts  69.7 us (12%)
  starting transfers between devices  53.1 us (9%)
  between operations  16.3 us (3%)
    ppermute x50, waiting for transfers between devices, swap(): lax.ppermute(tensor, axis, [(i, i ^ step) for i in range(size_of(axis))])  163 us
    dot_general x38, matrix products, dot(): lax.dot_general(first, second, (((left,), (right,)), ((), ())), preferred...  98.2 us
    ppermute x50, starting transfers between devices, swap(): lax.ppermute(tensor, axis, [(i, i ^ step) for i in range(size_of(axis))])  35.7 us
    pallas_call x2, Pallas kernels, attend_back(): pl.pallas_call(functools.partial(body, head_dim), grid=(heads,), in_specs...  28 us
    unnamed x189, local copies, waits for them, and re-layouts  24.6 us
    pallas_call x2, Pallas kernels, attend(): pl.pallas_call(forward_body, grid=(heads,), in_specs=[pl.BlockSpec((block...  22.9 us
    all_to_all x4, starting transfers between devices, exchange(): return lax.all_to_all(blocks, ('zh', 'zl', 'yh', 'yl'), 0, 0)  17.2 us
    pallas_call x2, Pallas kernels, put_positions(): pl.pallas_call(functools.partial(put_body, rows, lanes, lines, base is no...  12.8 us
  transfers between devices with their start and end apart: 56, of which 22 were waited for; matrix products, arithmetic and copies ran while one was open for 37% of the time, Pallas kernels for 11%

profile of v5, /device:TPU:0, one launch (start us, length us, event | category | flops | bytes accessed | tf_op | source)
XLA Modules:
  0.0 556.7 jit_solution(4966783410716684511)
XLA Ops:
  8.8 3.8 shard_map.305
  50.2 7.8 %all-to-all-done = bf16[8,160,384]{2,1,0:T(8,128)(2,1)S(1)} async-done(((bf16[8,160,384]{2,1,0:T(8,128)(2,1)}), bf16[8,160,384]{2,1,0:T(8,128)(2,1)S(1)}, u32[]{:S(2)}, u32[]{:S(2)}) %all-to-all-start) | async-done | bytes 983072 | tf_op jit(solution)/shard_map/all_to_all | solution.py:430
  74.2 28.5 %collective-permute-done.7 = bf16[384,1280]{1,0:T(8,128)(2,1)} collective-permute-done((bf16[384,1280]{1,0:T(8,128)(2,1)}, bf16[384,1280]{1,0:T(8,128)(2,1)}, u32[]{:S(2)}, u32[]{:S(2)}) %collective-permute-start.7) | collective-permute-done | bytes 983072 | tf_op jit(solution)/shard_map/ppermute | solution.py:40
  103.1 3.9 all-to-all-start.1
  113.1 6.5 %add_convert_fusion = bf16[768,1536]{1,0:T(8,128)(2,1)S(1)} fusion(bf16[2048,1280]{1,0:T(8,128)(2,1)S(1)} %shard_map.306, f32[768]{0:T(1024)S(1)} %get-tuple-element.361, f32[1536]{0:T(1024)S(1)} %get-tuple-element.369, f32[1536]{0:T(1024)S(1)} %get-tuple-element.368, f32[1536]{0:T(1024)S(1)} %copy-done.86, f32[1536]{0:T(1024)S(1)} %get-tuple-element.374, ...), kind=kOutput, calls=%fused_computation.6 | convolution fusion | flops 3030908928 | bytes 8294400 | tf_op jit(solution)/shard_map/dot_general | solution.py:22
  125.9 11.4 %shard_map.308 = (bf16[768,512]{1,0:T(8,128)(2,1)S(1)}, f32[768,512]{1,0:T(8,128)S(1)}, bf16[4,1536,768]{2,1,0:T(8,128)(2,1)}) custom-call(bf16[1536,1536]{1,0:T(8,128)(2,1)} %pad_maximum_fusion.query_ref.key_ref.value_ref.query.key.value, bf16[1536,1536]{1,0:T(8,128)(2,1)} %pad_maximum_fusion.query_ref.key_ref.value_ref.query.key.value, ...), custom_call_target="tpu_custom_call" | custom-call | flops 1000 | bytes 1000 | tf_op jit(solution)/shard_map/pallas_call | solution.py:262
  145.4 3.9 pad_maximum_fusion.1
  149.3 11.4 %shard_map.309 = (bf16[768,512]{1,0:T(8,128)(2,1)S(1)}, f32[768,512]{1,0:T(8,128)S(1)}, bf16[4,1536,768]{2,1,0:T(8,128)(2,1)}) custom-call(bf16[1536,1536]{1,0:T(8,128)(2,1)} %pad_maximum_fusion.query_ref.key_ref.value_ref.query.key.value, bf16[1536,1536]{1,0:T(8,128)(2,1)} %pad_maximum_fusion.query_ref.key_ref.value_ref.query.key.value, ...), custom_call_target="tpu_custom_call" | custom-call | flops 1000 | bytes 1000 | tf_op jit(solution)/shard_map/pallas_call | solution.py:262
  167.1 13.2 %collective-permute-done.11 = bf16[384,1280]{1,0:T(8,128)(2,1)} collective-permute-done((bf16[384,1280]{1,0:T(8,128)(2,1)}, bf16[384,1280]{1,0:T(8,128)(2,1)}, u32[]{:S(2)}, u32[]{:S(2)}) %collective-permute-start.11) | collective-permute-done | bytes 983072 | tf_op jit(solution)/shard_map/ppermute | solution.py:40
  188.7 4.3 fusion.169
  194.7 38.2 %collective-permute-done.14 = bf16[384,1280]{1,0:T(8,128)(2,1)S(1)} collective-permute-done((bf16[384,1280]{1,0:T(8,128)(2,1)}, bf16[384,1280]{1,0:T(8,128)(2,1)S(1)}, u32[]{:S(2)}, u32[]{:S(2)}) %collective-permute-start.14) | collective-permute-done | bytes 983072 | tf_op jit(solution)/shard_map/ppermute | solution.py:40
  241.3 4.1 multiply_convert_fusion.1
  246.0 5.6 %fusion.26 = bf16[768,1280]{1,0:T(8,128)(2,1)} fusion(f32[768,1280]{1,0:T(8,128)S(1)} %get-tuple-element.384, bf16[1280,1280]{1,0:T(8,128)(2,1)S(1)} %shard_map.310, bf16[384,1280]{1,0:T(8,128)(2,1)} %collective-permute-done.13, bf16[384,1280]{1,0:T(8,128)(2,1)} %select_bitcast_fusion), kind=kOutput, calls=%fused_computation.45 | convolution fusion | flops 2530344960 | bytes 11141120 | tf_op jit(solution)/shard_map/dot_general | solution.py:22
  251.6 7.0 %collective-permute-done.17 = bf16[384,1280]{1,0:T(8,128)(2,1)} collective-permute-done((bf16[384,1280]{1,0:T(8,128)(2,1)}, bf16[384,1280]{1,0:T(8,128)(2,1)}, u32[]{:S(2)}, u32[]{:S(2)}) %collective-permute-start.17) | collective-permute-done | bytes 983072 | tf_op jit(solution)/shard_map/ppermute | solution.py:40
  261.8 4.7 multiply_convert_fusion
  266.6 4.2 fusion.27
  278.4 7.1 %convolution_convert_fusion.1 = bf16[1280,1280]{1,0:T(8,128)(2,1)S(1)} fusion(bf16[1536,1280]{1,0:T(8,128)(2,1)S(1)} %pad_maximum_fusion.3, bf16[384,1280]{1,0:T(8,128)(2,1)S(1)} %collective-permute-done.18, bf16[384,1280]{1,0:T(8,128)(2,1)S(1)} %copy-done.85, bf16[384,1280]{1,0:T(8,128)(2,1)} %collective-permute-done.13, ...), kind=kOutput, calls=%fused_computation.2 | convolution fusion | flops 5050531840 | bytes 11141120 | tf_op jit(solution)/shard_map/dot_general | solution.py:22
  285.5 7.6 %convolution_convert_fusion = bf16[1280,1280]{1,0:T(8,128)(2,1)S(1)} fusion(bf16[1536,1280]{1,0:T(8,128)(2,1)S(1)} %pad_maximum_fusion.2, bf16[384,1280]{1,0:T(8,128)(2,1)} %collective-permute-done.19, bf16[384,1280]{1,0:T(8,128)(2,1)} %collective-permute-done.17, bf16[768,1280]{1,0:T(8,128)(2,1)S(1)} %copy-done.42), kind=kOutput, calls=%fused_computation.1 | convolution fusion | flops 5046599680 | bytes 11141120 | tf_op jit(solution)/shard_map/dot_general | solution.py:22
  294.5 6.0 %collective-permute-done.22 = bf16[384,1280]{1,0:T(8,128)(2,1)S(1)} collective-permute-done((bf16[384,1280]{1,0:T(8,128)(2,1)S(1)}, bf16[384,1280]{1,0:T(8,128)(2,1)S(1)}, u32[]{:S(2)}, u32[]{:S(2)}) %collective-permute-start.22) | collective-permute-done | bytes 983072 | tf_op jit(solution)/shard_map/ppermute | solution.py:40
  320.7 4.0 convolution_convert_fusion.12.grad
  327.7 3.9 convert_add_fusion.2
  335.3 13.5 %shard_map.312 = (bf16[768,512]{1,0:T(8,128)(2,1)}, f32[1536,512]{1,0:T(8,128)}, f32[1536,512]{1,0:T(8,128)}) custom-call(bf16[1536,1536]{1,0:T(8,128)(2,1)} %pad_maximum_fusion.query_ref.key_ref.value_ref.query.key.value, bf16[1536,1536]{1,0:T(8,128)(2,1)} %pad_maximum_fusion.query_ref.key_ref.value_ref.query.key.value, ...), custom_call_target="tpu_custom_call" | custom-call | flops 1000 | bytes 1000 | tf_op jit(solution)/shard_map/pallas_call | solution.py:350
  367.7 14.5 %shard_map.313 = bf16[3,1536,512]{2,1,0:T(8,128)(2,1)} custom-call(bf16[1536,1536]{1,0:T(8,128)(2,1)} %pad_maximum_fusion.query_ref.key_ref.value_ref.query.key.value, bf16[1536,1536]{1,0:T(8,128)(2,1)} %pad_maximum_fusion.query_ref.key_ref.value_ref.query.key.value, bf16[1536,1536]{1,0:T(8,128)(2,1)} %pad_maximum_fusion.query_ref.key_ref.value_ref.query.key.value, ...), custom_call_target="tpu_custom_call" | custom-call | flops 1000 | bytes 1000 | tf_op jit(solution)/shard_map/pallas_call | solution.py:350
  413.0 4.2 collective-permute-done.34
  420.9 6.0 %all-to-all-start.2 = ((bf16[8,160,384]{2,1,0:T(8,128)(2,1)}), bf16[8,160,384]{2,1,0:T(8,128)(2,1)S(1)}, u32[]{:S(2)}, u32[]{:S(2)}) async-start(bf16[8,160,384]{2,1,0:T(8,128)(2,1)} %bitcast.338), calls=%async_computation.2 | async-start | bytes 1966080 | tf_op jit(solution)/shard_map/all_to_all | solution.py:430
  450.3 8.8 %collective-permute-done.36 = bf16[2,160,1280]{2,1,0:T(8,128)(2,1)} collective-permute-done((bf16[2,160,1280]{2,1,0:T(8,128)(2,1)}, bf16[2,160,1280]{2,1,0:T(8,128)(2,1)}, u32[]{:S(2)}, u32[]{:S(2)}) %collective-permute-start.36) | collective-permute-done | bytes 819232 | tf_op jit(solution)/shard_map/ppermute | solution.py:40
  471.9 14.3 %collective-permute-done.41 = bf16[2,320,640]{2,1,0:T(8,128)(2,1)} collective-permute-done((bf16[2,320,640]{2,1,0:T(8,128)(2,1)}, bf16[2,320,640]{2,1,0:T(8,128)(2,1)}, u32[]{:S(2)}, u32[]{:S(2)}) %collective-permute-start.41) | collective-permute-done | bytes 819232 | tf_op jit(solution)/shard_map/ppermute | solution.py:40
  488.6 3.8 all-to-all-start.3
  504.2 6.4 %shard_map.314 = f32[375,1280]{1,0:T(8,128)} custom-call(bf16[2,2,2,160,384]{4,3,2,1,0:T(8,128)(2,1)S(1)} %maximum_bitcast_fusion.2.refs_0_), custom_call_target="tpu_custom_call" | custom-call | flops 1000 | bytes 1000 | tf_op jit(solution)/shard_map/pallas_call | solution.py:235
  510.5 16.8 %collective-permute-done.43 = f32[2400]{0:T(1024)S(1)} collective-permute-done((f32[2400]{0:T(1024)S(1)}, f32[2400]{0:T(1024)S(1)}, u32[]{:S(2)}, u32[]{:S(2)}) %collective-permute-start.43) | collective-permute-done | bytes 9632 | tf_op jit(solution)/shard_map/ppermute | solution.py:40
  531.5 4.5 collective-permute-done.45
  543.1 6.4 %shard_map.315 = f32[375,1280]{1,0:T(8,128)} custom-call(f32[375,1280]{1,0:T(8,128)S(1)} %copy-done.3, bf16[2,2,2,160,384]{4,3,2,1,0:T(8,128)(2,1)S(1)} %maximum_bitcast_fusion.3.refs_1_), custom_call_target="tpu_custom_call" | custom-call | flops 1000 | bytes 1000 | tf_op jit(solution)/shard_map/pallas_call | solution.py:235
  (525 shorter events, 254.0 us)
Async XLA Ops:
  7.2 102.8 %all-gather.6.cloned.1.call-start = ((), (), s32[]{:S(2)}) async-start(), calls=%async_computation.5 | async-start | bytes 3686400 | tf_op jit(solution)/shard_map/all_gather | solution.py:444
  22.7 21.2 %collective-permute-start.2 = (f32[2880]{0:T(1024)S(1)}, f32[2880]{0:T(1024)S(1)}, u32[]{:S(2)}, u32[]{:S(2)}) collective-permute-start(f32[2880]{0:T(1024)S(1)} %concatenate.104), channel_id=1, source_target_pairs={{0,4},{4,0},{1,5},{5,1},{2,6},{6,2},{3,7},{7,3},{8,12},{12,8},{9,1... | collective-permute-start | bytes 34568 | tf_op jit(solution)/shard_map/ppermute | solution.py:40
  25.3 32.8 %all-to-all-start = ((bf16[8,160,384]{2,1,0:T(8,128)(2,1)}), bf16[8,160,384]{2,1,0:T(8,128)(2,1)S(1)}, u32[]{:S(2)}, u32[]{:S(2)}) async-start(bf16[8,160,384]{2,1,0:T(8,128)(2,1)} %bitcast.6), calls=%async_computation | async-start | bytes 1966080 | tf_op jit(solution)/shard_map/all_to_all | solution.py:430
  28.8 208.2 %all-gather.4.cloned.1.call-start = ((), (), s32[]{:S(2)}) async-start(), calls=%async_computation.4 | async-start | bytes 7372800 | tf_op jit(solution)/shard_map/all_gather | solution.py:444
  32.9 39.0 %collective-permute-start.8 = (bf16[2,2,160,384]{3,2,1,0:T(8,128)(2,1)S(1)}, bf16[2,2,160,384]{3,2,1,0:T(8,128)(2,1)}, u32[]{:S(2)}, u32[]{:S(2)}) collective-permute-start(bf16[2,2,160,384]{3,2,1,0:T(8,128)(2,1)S(1)} %dynamic-slice_bitcast_fusion.8), channel_id=1, source_target_pairs={{0,8},{8,0},{1,9},{9,1},{2,10},{10,2},{3,11},{11,3},{4,12},{12,4},... | collective-permute-start | bytes 1474568 | tf_op jit(solution)/shard_map/ppermute | solution.py:40
  46.7 17.6 %collective-permute-start.16 = (bf16[640,320]{0,1:T(8,128)(2,1)}, bf16[640,320]{0,1:T(8,128)(2,1)}, u32[]{:S(2)}, u32[]{:S(2)}) collective-permute-start(bf16[640,320]{0,1:T(8,128)(2,1)} %dynamic-slice_bitcast_fusion.12), channel_id=1, source_target_pairs={{0,8},{8,0},{1,9},{9,1},{2,10},{10,2},{3,11},{11,3},{4,12},{12,4},... | collective-permute-start | bytes 1228808 | tf_op jit(solution)/shard_map/ppermute | solution.py:40
  64.3 38.4 %collective-permute-start.7 = (bf16[384,1280]{1,0:T(8,128)(2,1)}, bf16[384,1280]{1,0:T(8,128)(2,1)}, u32[]{:S(2)}, u32[]{:S(2)}) collective-permute-start(bf16[384,1280]{1,0:T(8,128)(2,1)} %add_convert_fusion.11), channel_id=1, source_target_pairs={{0,2},{2,0},{1,3},{3,1},{4,6},{6,4},{5,7},{7,5},{8,10},{10,8},{9,1... | collective-permute-start | bytes 2949128 | tf_op jit(solution)/shard_map/ppermute | solution.py:40
  71.8 35.2 %collective-permute-start.4 = (bf16[384,1280]{1,0:T(8,128)(2,1)}, bf16[384,1280]{1,0:T(8,128)(2,1)}, u32[]{:S(2)}, u32[]{:S(2)}) collective-permute-start(bf16[384,1280]{1,0:T(8,128)(2,1)} %add_convert_fusion.11), channel_id=1, source_target_pairs={{0,8},{8,0},{1,9},{9,1},{2,10},{10,2},{3,11},{11,3},{4,12},{12,4},... | collective-permute-start | bytes 2949128 | tf_op jit(solution)/shard_map/ppermute | solution.py:40
  103.1 40.7 %all-to-all-start.1 = ((bf16[8,160,384]{2,1,0:T(8,128)(2,1)}), bf16[8,160,384]{2,1,0:T(8,128)(2,1)S(1)}, u32[]{:S(2)}, u32[]{:S(2)}) async-start(bf16[8,160,384]{2,1,0:T(8,128)(2,1)} %bitcast.43), calls=%async_computation.1 | async-start | bytes 1966080 | tf_op jit(solution)/shard_map/all_to_all | solution.py:430
  143.7 36.5 %collective-permute-start.11 = (bf16[384,1280]{1,0:T(8,128)(2,1)}, bf16[384,1280]{1,0:T(8,128)(2,1)}, u32[]{:S(2)}, u32[]{:S(2)}) collective-permute-start(bf16[384,1280]{1,0:T(8,128)(2,1)} %add_convert_fusion.10), channel_id=1, source_target_pairs={{0,2},{2,0},{1,3},{3,1},{4,6},{6,4},{5,7},{7,5},{8,10},{10,8},{9,1... | collective-permute-start | bytes 2949128 | tf_op jit(solution)/shard_map/ppermute | solution.py:40
  186.0 46.9 %collective-permute-start.14 = (bf16[384,1280]{1,0:T(8,128)(2,1)}, bf16[384,1280]{1,0:T(8,128)(2,1)S(1)}, u32[]{:S(2)}, u32[]{:S(2)}) collective-permute-start(bf16[384,1280]{1,0:T(8,128)(2,1)} %select_bitcast_fusion), channel_id=1, source_target_pairs={{0,2},{2,0},{1,3},{3,1},{4,6},{6,4},{5,7},{7,5},{8,10},{10,8},{9,1... | collective-permute-start | bytes 2949128 | tf_op jit(solution)/shard_map/ppermute | solution.py:40
  234.1 24.5 %collective-permute-start.17 = (bf16[384,1280]{1,0:T(8,128)(2,1)}, bf16[384,1280]{1,0:T(8,128)(2,1)}, u32[]{:S(2)}, u32[]{:S(2)}) collective-permute-start(bf16[384,1280]{1,0:T(8,128)(2,1)} %add_convert_fusion.9), channel_id=1, source_target_pairs={{0,2},{2,0},{1,3},{3,1},{4,6},{6,4},{5,7},{7,5},{8,10},{10,8},{9,1... | collective-permute-start | bytes 2949128 | tf_op jit(solution)/shard_map/ppermute | solution.py:40
  276.4 24.1 %collective-permute-start.22 = (bf16[384,1280]{1,0:T(8,128)(2,1)S(1)}, bf16[384,1280]{1,0:T(8,128)(2,1)S(1)}, u32[]{:S(2)}, u32[]{:S(2)}) collective-permute-start(bf16[384,1280]{1,0:T(8,128)(2,1)S(1)} %add_convert_fusion.8), channel_id=1, source_target_pairs={{0,2},{2,0},{1,3},{3,1},{4,6},{6,4},{5,7},{7,5},{8,10},{10,8},{9,1... | collective-permute-start | bytes 2949128 | tf_op jit(solution)/shard_map/ppermute | solution.py:40
  278.2 25.4 %collective-permute-start.21 = (bf16[384,1280]{1,0:T(8,128)(2,1)S(1)}, bf16[384,1280]{1,0:T(8,128)(2,1)S(1)}, u32[]{:S(2)}, u32[]{:S(2)}) collective-permute-start(bf16[384,1280]{1,0:T(8,128)(2,1)S(1)} %convolution_convert_fusion.7), channel_id=1, source_target_pairs={{0,8},{8,0},{1,9},{9,1},{2,10},{10,2},{3,11},{11,3},{4,12},{12,4},... | collective-permute-start | bytes 2949128 | tf_op jit(solution)/shard_map/ppermute | solution.py:40
  306.2 21.5 %collective-permute-start.24 = (bf16[768,1280]{1,0:T(8,128)(2,1)}, bf16[768,1280]{1,0:T(8,128)(2,1)}, u32[]{:S(2)}, u32[]{:S(2)}) collective-permute-start(bf16[768,1280]{1,0:T(8,128)(2,1)} %pad_maximum_fusion.7), channel_id=1, source_target_pairs={{0,8},{8,0},{1,9},{9,1},{2,10},{10,2},{3,11},{11,3},{4,12},{12,4},... | collective-permute-start | bytes 5898248 | tf_op jit(solution)/shard_map/ppermute | solution.py:40
  314.2 38.0 %collective-permute-start.26 = (bf16[2,320,1280]{2,1,0:T(8,128)(2,1)}, bf16[2,320,1280]{2,1,0:T(8,128)(2,1)}, u32[]{:S(2)}, u32[]{:S(2)}) collective-permute-start(bf16[2,320,1280]{2,1,0:T(8,128)(2,1)} %get-tuple-element.293), channel_id=1, source_target_pairs={{0,1},{1,0},{2,3},{3,2},{4,5},{5,4},{6,7},{7,6},{8,9},{9,8},{10,11... | collective-permute-start | bytes 4915208 | tf_op jit(solution)/shard_map/ppermute | solution.py:40
  318.0 37.7 %collective-permute-start.27 = (bf16[2,2,320,640]{3,2,1,0:T(8,128)(2,1)}, bf16[2,2,320,640]{3,2,1,0:T(8,128)(2,1)}, u32[]{:S(2)}, u32[]{:S(2)}) collective-permute-start(bf16[2,2,320,640]{3,2,1,0:T(8,128)(2,1)} %get-tuple-element.291), channel_id=1, source_target_pairs={{0,16},{16,0},{1,17},{17,1},{2,18},{18,2},{3,19},{19,3},{4,20},{20... | collective-permute-start | bytes 4915208 | tf_op jit(solution)/shard_map/ppermute | solution.py:40
  320.0 28.7 %collective-permute-start.25 = (bf16[384,1280]{1,0:T(8,128)(2,1)}, bf16[384,1280]{1,0:T(8,128)(2,1)}, u32[]{:S(2)}, u32[]{:S(2)}) collective-permute-start(bf16[384,1280]{1,0:T(8,128)(2,1)} %convert_element_type.312), channel_id=1, source_target_pairs={{0,2},{2,0},{1,3},{3,1},{4,6},{6,4},{5,7},{7,5},{8,10},{10,8},{9,1... | collective-permute-start | bytes 2949128 | tf_op jit(solution)/shard_map/ppermute | solution.py:40
  358.8 32.0 %collective-permute-start.30 = (bf16[2,320,640]{2,1,0:T(8,128)(2,1)}, bf16[2,320,640]{2,1,0:T(8,128)(2,1)}, u32[]{:S(2)}, u32[]{:S(2)}) collective-permute-start(bf16[2,320,640]{2,1,0:T(8,128)(2,1)} %get-tuple-element.307), channel_id=1, source_target_pairs={{0,16},{16,0},{1,17},{17,1},{2,18},{18,2},{3,19},{19,3},{4,20},{20... | collective-permute-start | bytes 2457608 | tf_op jit(solution)/shard_map/ppermute | solution.py:40
  363.3 27.5 %collective-permute-start.31 = (bf16[2,320,640]{2,1,0:T(8,128)(2,1)}, bf16[2,320,640]{2,1,0:T(8,128)(2,1)}, u32[]{:S(2)}, u32[]{:S(2)}) collective-permute-start(bf16[2,320,640]{2,1,0:T(8,128)(2,1)} %get-tuple-element.305), channel_id=1, source_target_pairs={{0,1},{1,0},{2,3},{3,2},{4,5},{5,4},{6,7},{7,6},{8,9},{9,8},{10,11... | collective-permute-start | bytes 2457608 | tf_op jit(solution)/shard_map/ppermute | solution.py:40
  363.9 24.2 %collective-permute-start.33 = (bf16[384,1280]{1,0:T(8,128)(2,1)}, bf16[384,1280]{1,0:T(8,128)(2,1)}, u32[]{:S(2)}, u32[]{:S(2)}) collective-permute-start(bf16[384,1280]{1,0:T(8,128)(2,1)} %add_convert_fusion.7), channel_id=1, source_target_pairs={{0,2},{2,0},{1,3},{3,1},{4,6},{6,4},{5,7},{7,5},{8,10},{10,8},{9,1... | collective-permute-start | bytes 2949128 | tf_op jit(solution)/shard_map/ppermute | solution.py:40
  393.5 23.7 %collective-permute-start.34 = (bf16[384,1280]{1,0:T(8,128)(2,1)S(1)}, bf16[384,1280]{1,0:T(8,128)(2,1)S(1)}, u32[]{:S(2)}, u32[]{:S(2)}) collective-permute-start(bf16[384,1280]{1,0:T(8,128)(2,1)S(1)} %add_convert_fusion.6), channel_id=1, source_target_pairs={{0,2},{2,0},{1,3},{3,1},{4,6},{6,4},{5,7},{7,5},{8,10},{10,8},{9,1... | collective-permute-start | bytes 2949128 | tf_op jit(solution)/shard_map/ppermute | solution.py:40
  420.9 65.2 %all-to-all-start.2 = ((bf16[8,160,384]{2,1,0:T(8,128)(2,1)}), bf16[8,160,384]{2,1,0:T(8,128)(2,1)S(1)}, u32[]{:S(2)}, u32[]{:S(2)}) async-start(bf16[8,160,384]{2,1,0:T(8,128)(2,1)} %bitcast.338), calls=%async_computation.2 | async-start | bytes 1966080 | tf_op jit(solution)/shard_map/all_to_all | solution.py:430
  430.1 20.2 %collective-permute-start.35 = (bf16[2,2,160,640]{3,2,1,0:T(8,128)(2,1)}, bf16[2,2,160,640]{3,2,1,0:T(8,128)(2,1)}, u32[]{:S(2)}, u32[]{:S(2)}) collective-permute-start(bf16[2,2,160,640]{3,2,1,0:T(8,128)(2,1)} %get-tuple-element.303), channel_id=1, source_target_pairs={{0,16},{16,0},{1,17},{17,1},{2,18},{18,2},{3,19},{19,3},{4,20},{20... | collective-permute-start | bytes 2457608 | tf_op jit(solution)/shard_map/ppermute | solution.py:40
  436.9 22.2 %collective-permute-start.36 = (bf16[2,160,1280]{2,1,0:T(8,128)(2,1)}, bf16[2,160,1280]{2,1,0:T(8,128)(2,1)}, u32[]{:S(2)}, u32[]{:S(2)}) collective-permute-start(bf16[2,160,1280]{2,1,0:T(8,128)(2,1)} %get-tuple-element.301), channel_id=1, source_target_pairs={{0,1},{1,0},{2,3},{3,2},{4,5},{5,4},{6,7},{7,6},{8,9},{9,8},{10,11... | collective-permute-start | bytes 2457608 | tf_op jit(solution)/shard_map/ppermute | solution.py:40
  445.2 40.9 %collective-permute-start.41 = (bf16[2,320,640]{2,1,0:T(8,128)(2,1)}, bf16[2,320,640]{2,1,0:T(8,128)(2,1)}, u32[]{:S(2)}, u32[]{:S(2)}) collective-permute-start(bf16[2,320,640]{2,1,0:T(8,128)(2,1)} %get-tuple-element.299), channel_id=1, source_target_pairs={{0,4},{4,0},{1,5},{5,1},{2,6},{6,2},{3,7},{7,3},{8,12},{12,8},{9,1... | collective-permute-start | bytes 2457608 | tf_op jit(solution)/shard_map/ppermute | solution.py:40
  461.6 24.6 %collective-permute-start.38 = (bf16[2,160,640]{2,1,0:T(8,128)(2,1)}, bf16[2,160,640]{2,1,0:T(8,128)(2,1)S(1)}, u32[]{:S(2)}, u32[]{:S(2)}) collective-permute-start(bf16[2,160,640]{2,1,0:T(8,128)(2,1)} %get-tuple-element.334), channel_id=1, source_target_pairs={{0,1},{1,0},{2,3},{3,2},{4,5},{5,4},{6,7},{7,6},{8,9},{9,8},{10,11... | collective-permute-start | bytes 1228808 | tf_op jit(solution)/shard_map/ppermute | solution.py:40
  464.2 22.0 %collective-permute-start.39 = (bf16[2,160,640]{2,1,0:T(8,128)(2,1)}, bf16[2,160,640]{2,1,0:T(8,128)(2,1)}, u32[]{:S(2)}, u32[]{:S(2)}) collective-permute-start(bf16[2,160,640]{2,1,0:T(8,128)(2,1)} %get-tuple-element.332), channel_id=1, source_target_pairs={{0,16},{16,0},{1,17},{17,1},{2,18},{18,2},{3,19},{19,3},{4,20},{20... | collective-permute-start | bytes 1228808 | tf_op jit(solution)/shard_map/ppermute | solution.py:40
  464.9 21.2 %collective-permute-start.40 = (f32[2,2400]{1,0:T(2,128)S(1)}, f32[2,2400]{1,0:T(2,128)S(1)}, u32[]{:S(2)}, u32[]{:S(2)}) collective-permute-start(f32[2,2400]{1,0:T(2,128)S(1)} %bitcast.366), channel_id=1, source_target_pairs={{0,1},{1,0},{2,3},{3,2},{4,5},{5,4},{6,7},{7,6},{8,9},{9,8},{10,11... | collective-permute-start | bytes 57608 | tf_op jit(solution)/shard_map/ppermute | solution.py:40
  488.6 38.7 %all-to-all-start.3 = ((bf16[8,160,384]{2,1,0:T(8,128)(2,1)}), bf16[8,160,384]{2,1,0:T(8,128)(2,1)S(1)}, u32[]{:S(2)}, u32[]{:S(2)}) async-start(bf16[8,160,384]{2,1,0:T(8,128)(2,1)} %bitcast.96), calls=%async_computation.3 | async-start | bytes 1966080 | tf_op jit(solution)/shard_map/all_to_all | solution.py:430
  492.5 34.8 %collective-permute-start.43 = (f32[2400]{0:T(1024)S(1)}, f32[2400]{0:T(1024)S(1)}, u32[]{:S(2)}, u32[]{:S(2)}) collective-permute-start(f32[2400]{0:T(1024)S(1)} %get-tuple-element.279), channel_id=1, source_target_pairs={{0,4},{4,0},{1,5},{5,1},{2,6},{6,2},{3,7},{7,3},{8,12},{12,8},{9,1... | collective-permute-start | bytes 28808 | tf_op jit(solution)/shard_map/ppermute | solution.py:40
  499.4 36.5 %collective-permute-start.45 = (bf16[2,160,640]{2,1,0:T(8,128)(2,1)}, bf16[2,160,640]{2,1,0:T(8,128)(2,1)}, u32[]{:S(2)}, u32[]{:S(2)}) collective-permute-start(bf16[2,160,640]{2,1,0:T(8,128)(2,1)} %get-tuple-element.330), channel_id=1, source_target_pairs={{0,4},{4,0},{1,5},{5,1},{2,6},{6,2},{3,7},{7,3},{8,12},{12,8},{9,1... | collective-permute-start | bytes 1228808 | tf_op jit(solution)/shard_map/ppermute | solution.py:40
  (113 other events, 792.7 us)
Sparse Core Ops, SparseCore 0:
  18.9 82.5 all-gather.5
  104.3 122.7 all-gather.3

commit v6 on v5

--- a/solution.py
+++ b/solution.py
@@ -751,7 +751,7 @@
 
     flat_half = send_units(sum(flat_half), "zh", 0)
     input_grad, moved_delta, flat_half = sync(put(kept_tokens(moved_last)), moved_delta, flat_half)
-    flat = sum(flat_half)
+    delta_tokens, head_half, flat = sync(kept_tokens(moved_delta), head_half, sum(flat_half))
     full_flat, part_flat = flat[:full_size], flat[full_size:]
 
     by_chip = full_flat.reshape(chips, -1)
@@ -761,8 +761,7 @@
     unit_cores = two_cores(summed(unit_half), True)
     grad_out_w = unit_cores[0].reshape(units, rows)
     grad_in_w = unit_cores[1].reshape(units, rows).T
-    layer_out = put(kept_tokens(moved_delta), inputs)
-    input_grad, head_half, mine = sync(input_grad, head_half, mine)
+    layer_out = put(delta_tokens, inputs)
     head_cores = two_cores(summed(head_half), split)
     head_cores = head_cores.reshape(2, -1, 2, part_heads * head_dim, rows)
     grad_query_w, grad_key_w, grad_value_w, grad_attn_w = (

time: 561 us -> 560 us (level)
    unnamed x189 -> x183, local copies, waits for them, and re-layouts: 24.6 us -> 23.1 us
  transfers between devices with their start and end apart: 56 -> 56, of which waited for: 22 -> 22; matrix products, arithmetic and copies ran while one was open for 37% -> 37% of each run, Pallas kernels for 11% -> 13%
where the time goes in v6:
time: 560 us; the launch traced here: 555 us
  waiting for transfers between devices  170 us (30%)
  matrix products  98.2 us (18%)
  other arithmetic  75.8 us (14%)
  Pallas kernels  73.3 us (13%)
  local copies, waits for them, and re-layouts  68.2 us (12%)
  starting transfers between devices  53.4 us (10%)
  between operations  16.3 us (3%)
    ppermute x50, waiting for transfers between devices, swap(): lax.ppermute(tensor, axis, [(i, i ^ step) for i in range(size_of(axis))])  162 us
    dot_general x38, matrix products, dot(): lax.dot_general(first, second, (((left,), (right,)), ((), ())), preferred...  98.2 us
    ppermute x50, starting transfers between devices, swap(): lax.ppermute(tensor, axis, [(i, i ^ step) for i in range(size_of(axis))])  35.9 us
    pallas_call x2, Pallas kernels, attend_back(): pl.pallas_call(functools.partial(body, head_dim), grid=(heads,), in_specs...  28 us
    unnamed x183, local copies, waits for them, and re-layouts  23.1 us
    pallas_call x2, Pallas kernels, attend(): pl.pallas_call(forward_body, grid=(heads,), in_specs=[pl.BlockSpec((block...  22.9 us
    all_to_all x4, starting transfers between devices, exchange(): return lax.all_to_all(blocks, ('zh', 'zl', 'yh', 'yl'), 0, 0)  17.3 us
    pallas_call x2, Pallas kernels, put_positions(): pl.pallas_call(functools.partial(put_body, rows, lanes, lines, base is no...  12.8 us
  transfers between devices with their start and end apart: 56, of which 22 were waited for; matrix products, arithmetic and copies ran while one was open for 37% of the time, Pallas kernels for 13%

profile of v6, /device:TPU:0, one launch (start us, length us, event | category | flops | bytes accessed | tf_op | source)
XLA Modules:
  0.0 554.9 jit_solution(2906556437504911754)
XLA Ops:
  8.8 3.8 shard_map.305
  29.1 3.8 shard_map.307
  50.2 7.8 %all-to-all-done = bf16[8,160,384]{2,1,0:T(8,128)(2,1)S(1)} async-done(((bf16[8,160,384]{2,1,0:T(8,128)(2,1)}), bf16[8,160,384]{2,1,0:T(8,128)(2,1)S(1)}, u32[]{:S(2)}, u32[]{:S(2)}) %all-to-all-start) | async-done | bytes 983072 | tf_op jit(solution)/shard_map/all_to_all | solution.py:430
  74.2 28.5 %collective-permute-done.7 = bf16[384,1280]{1,0:T(8,128)(2,1)} collective-permute-done((bf16[384,1280]{1,0:T(8,128)(2,1)}, bf16[384,1280]{1,0:T(8,128)(2,1)}, u32[]{:S(2)}, u32[]{:S(2)}) %collective-permute-start.7) | collective-permute-done | bytes 983072 | tf_op jit(solution)/shard_map/ppermute | solution.py:40
  103.1 3.9 all-to-all-start.1
  113.1 6.5 %add_convert_fusion = bf16[768,1536]{1,0:T(8,128)(2,1)S(1)} fusion(bf16[2048,1280]{1,0:T(8,128)(2,1)S(1)} %shard_map.306, f32[768]{0:T(1024)S(1)} %get-tuple-element.361, f32[1536]{0:T(1024)S(1)} %get-tuple-element.369, f32[1536]{0:T(1024)S(1)} %get-tuple-element.368, f32[1536]{0:T(1024)S(1)} %copy-done.83, f32[1536]{0:T(1024)S(1)} %get-tuple-element.374, ...), kind=kOutput, calls=%fused_computation.6 | convolution fusion | flops 3030908928 | bytes 8294400 | tf_op jit(solution)/shard_map/dot_general | solution.py:22
  125.8 11.4 %shard_map.308 = (bf16[768,512]{1,0:T(8,128)(2,1)S(1)}, f32[768,512]{1,0:T(8,128)S(1)}, bf16[4,1536,768]{2,1,0:T(8,128)(2,1)}) custom-call(bf16[1536,1536]{1,0:T(8,128)(2,1)} %pad_maximum_fusion.query_ref.key_ref.value_ref.query.key.value, bf16[1536,1536]{1,0:T(8,128)(2,1)} %pad_maximum_fusion.query_ref.key_ref.value_ref.query.key.value, ...), custom_call_target="tpu_custom_call" | custom-call | flops 1000 | bytes 1000 | tf_op jit(solution)/shard_map/pallas_call | solution.py:262
  145.4 3.8 pad_maximum_fusion.1
  149.2 11.4 %shard_map.309 = (bf16[768,512]{1,0:T(8,128)(2,1)S(1)}, f32[768,512]{1,0:T(8,128)S(1)}, bf16[4,1536,768]{2,1,0:T(8,128)(2,1)}) custom-call(bf16[1536,1536]{1,0:T(8,128)(2,1)} %pad_maximum_fusion.query_ref.key_ref.value_ref.query.key.value, bf16[1536,1536]{1,0:T(8,128)(2,1)} %pad_maximum_fusion.query_ref.key_ref.value_ref.query.key.value, ...), custom_call_target="tpu_custom_call" | custom-call | flops 1000 | bytes 1000 | tf_op jit(solution)/shard_map/pallas_call | solution.py:262
  167.1 13.2 %collective-permute-done.11 = bf16[384,1280]{1,0:T(8,128)(2,1)} collective-permute-done((bf16[384,1280]{1,0:T(8,128)(2,1)}, bf16[384,1280]{1,0:T(8,128)(2,1)}, u32[]{:S(2)}, u32[]{:S(2)}) %collective-permute-start.11) | collective-permute-done | bytes 983072 | tf_op jit(solution)/shard_map/ppermute | solution.py:40
  188.7 4.3 fusion.169
  194.7 38.2 %collective-permute-done.14 = bf16[384,1280]{1,0:T(8,128)(2,1)S(1)} collective-permute-done((bf16[384,1280]{1,0:T(8,128)(2,1)}, bf16[384,1280]{1,0:T(8,128)(2,1)S(1)}, u32[]{:S(2)}, u32[]{:S(2)}) %collective-permute-start.14) | collective-permute-done | bytes 983072 | tf_op jit(solution)/shard_map/ppermute | solution.py:40
  241.3 4.1 multiply_convert_fusion.1
  246.0 5.6 %fusion.26 = bf16[768,1280]{1,0:T(8,128)(2,1)} fusion(f32[768,1280]{1,0:T(8,128)S(1)} %get-tuple-element.384, bf16[1280,1280]{1,0:T(8,128)(2,1)S(1)} %shard_map.310, bf16[384,1280]{1,0:T(8,128)(2,1)} %collective-permute-done.13, bf16[384,1280]{1,0:T(8,128)(2,1)} %select_bitcast_fusion), kind=kOutput, calls=%fused_computation.45 | convolution fusion | flops 2530344960 | bytes 11141120 | tf_op jit(solution)/shard_map/dot_general | solution.py:22
  251.7 7.0 %collective-permute-done.17 = bf16[384,1280]{1,0:T(8,128)(2,1)} collective-permute-done((bf16[384,1280]{1,0:T(8,128)(2,1)}, bf16[384,1280]{1,0:T(8,128)(2,1)}, u32[]{:S(2)}, u32[]{:S(2)}) %collective-permute-start.17) | collective-permute-done | bytes 983072 | tf_op jit(solution)/shard_map/ppermute | solution.py:40
  261.9 4.7 multiply_convert_fusion
  266.6 4.2 fusion.27
  278.4 7.1 %convolution_convert_fusion.1 = bf16[1280,1280]{1,0:T(8,128)(2,1)S(1)} fusion(bf16[1536,1280]{1,0:T(8,128)(2,1)S(1)} %pad_maximum_fusion.3, bf16[384,1280]{1,0:T(8,128)(2,1)S(1)} %collective-permute-done.18, bf16[384,1280]{1,0:T(8,128)(2,1)S(1)} %copy-done.82, bf16[384,1280]{1,0:T(8,128)(2,1)} %collective-permute-done.13, ...), kind=kOutput, calls=%fused_computation.2 | convolution fusion | flops 5050531840 | bytes 11141120 | tf_op jit(solution)/shard_map/dot_general | solution.py:22
  285.5 7.6 %convolution_convert_fusion = bf16[1280,1280]{1,0:T(8,128)(2,1)S(1)} fusion(bf16[1536,1280]{1,0:T(8,128)(2,1)S(1)} %pad_maximum_fusion.2, bf16[384,1280]{1,0:T(8,128)(2,1)} %collective-permute-done.19, bf16[384,1280]{1,0:T(8,128)(2,1)} %collective-permute-done.17, bf16[768,1280]{1,0:T(8,128)(2,1)S(1)} %copy-done.41), kind=kOutput, calls=%fused_computation.1 | convolution fusion | flops 5046599680 | bytes 11141120 | tf_op jit(solution)/shard_map/dot_general | solution.py:22
  294.5 6.0 %collective-permute-done.22 = bf16[384,1280]{1,0:T(8,128)(2,1)S(1)} collective-permute-done((bf16[384,1280]{1,0:T(8,128)(2,1)S(1)}, bf16[384,1280]{1,0:T(8,128)(2,1)S(1)}, u32[]{:S(2)}, u32[]{:S(2)}) %collective-permute-start.22) | collective-permute-done | bytes 983072 | tf_op jit(solution)/shard_map/ppermute | solution.py:40
  320.7 4.0 convolution_convert_fusion.12.grad
  327.8 3.9 convert_add_fusion.2
  335.3 13.5 %shard_map.312 = (bf16[768,512]{1,0:T(8,128)(2,1)}, f32[1536,512]{1,0:T(8,128)}, f32[1536,512]{1,0:T(8,128)}) custom-call(bf16[1536,1536]{1,0:T(8,128)(2,1)} %pad_maximum_fusion.query_ref.key_ref.value_ref.query.key.value, bf16[1536,1536]{1,0:T(8,128)(2,1)} %pad_maximum_fusion.query_ref.key_ref.value_ref.query.key.value, ...), custom_call_target="tpu_custom_call" | custom-call | flops 1000 | bytes 1000 | tf_op jit(solution)/shard_map/pallas_call | solution.py:350
  367.7 14.5 %shard_map.313 = bf16[3,1536,512]{2,1,0:T(8,128)(2,1)} custom-call(bf16[1536,1536]{1,0:T(8,128)(2,1)} %pad_maximum_fusion.query_ref.key_ref.value_ref.query.key.value, bf16[1536,1536]{1,0:T(8,128)(2,1)} %pad_maximum_fusion.query_ref.key_ref.value_ref.query.key.value, bf16[1536,1536]{1,0:T(8,128)(2,1)} %pad_maximum_fusion.query_ref.key_ref.value_ref.query.key.value, ...), custom_call_target="tpu_custom_call" | custom-call | flops 1000 | bytes 1000 | tf_op jit(solution)/shard_map/pallas_call | solution.py:350
  413.0 4.3 collective-permute-done.34
  420.9 6.0 %all-to-all-start.2 = ((bf16[8,160,384]{2,1,0:T(8,128)(2,1)}), bf16[8,160,384]{2,1,0:T(8,128)(2,1)S(1)}, u32[]{:S(2)}, u32[]{:S(2)}) async-start(bf16[8,160,384]{2,1,0:T(8,128)(2,1)} %bitcast.338), calls=%async_computation.2 | async-start | bytes 1966080 | tf_op jit(solution)/shard_map/all_to_all | solution.py:430
  450.3 8.8 %collective-permute-done.36 = bf16[2,160,1280]{2,1,0:T(8,128)(2,1)} collective-permute-done((bf16[2,160,1280]{2,1,0:T(8,128)(2,1)}, bf16[2,160,1280]{2,1,0:T(8,128)(2,1)}, u32[]{:S(2)}, u32[]{:S(2)}) %collective-permute-start.36) | collective-permute-done | bytes 819232 | tf_op jit(solution)/shard_map/ppermute | solution.py:40
  471.9 14.2 %collective-permute-done.41 = bf16[2,320,640]{2,1,0:T(8,128)(2,1)} collective-permute-done((bf16[2,320,640]{2,1,0:T(8,128)(2,1)}, bf16[2,320,640]{2,1,0:T(8,128)(2,1)}, u32[]{:S(2)}, u32[]{:S(2)}) %collective-permute-start.41) | collective-permute-done | bytes 819232 | tf_op jit(solution)/shard_map/ppermute | solution.py:40
  486.2 3.8 all-to-all-start.3
  498.9 6.4 %shard_map.314 = f32[375,1280]{1,0:T(8,128)} custom-call(bf16[2,2,2,160,384]{4,3,2,1,0:T(8,128)(2,1)S(1)} %maximum_bitcast_fusion.2.refs_0_), custom_call_target="tpu_custom_call" | custom-call | flops 1000 | bytes 1000 | tf_op jit(solution)/shard_map/pallas_call | solution.py:235
  505.3 19.7 %collective-permute-done.43 = f32[2400]{0:T(1024)S(1)} collective-permute-done((f32[2400]{0:T(1024)S(1)}, f32[2400]{0:T(1024)S(1)}, u32[]{:S(2)}, u32[]{:S(2)}) %collective-permute-start.43) | collective-permute-done | bytes 9632 | tf_op jit(solution)/shard_map/ppermute | solution.py:40
  536.6 6.5 %shard_map.315 = f32[375,1280]{1,0:T(8,128)} custom-call(f32[375,1280]{1,0:T(8,128)S(1)} %copy-done.3, bf16[2,2,2,160,384]{4,3,2,1,0:T(8,128)(2,1)S(1)} %maximum_bitcast_fusion.3.refs_1_), custom_call_target="tpu_custom_call" | custom-call | flops 1000 | bytes 1000 | tf_op jit(solution)/shard_map/pallas_call | solution.py:235
  (519 shorter events, 250.1 us)
Async XLA Ops:
  7.2 102.8 %all-gather.6.cloned.1.call-start = ((), (), s32[]{:S(2)}) async-start(), calls=%async_computation.5 | async-start | bytes 3686400 | tf_op jit(solution)/shard_map/all_gather | solution.py:444
  22.7 21.2 %collective-permute-start.2 = (f32[2880]{0:T(1024)S(1)}, f32[2880]{0:T(1024)S(1)}, u32[]{:S(2)}, u32[]{:S(2)}) collective-permute-start(f32[2880]{0:T(1024)S(1)} %concatenate.104), channel_id=1, source_target_pairs={{0,4},{4,0},{1,5},{5,1},{2,6},{6,2},{3,7},{7,3},{8,12},{12,8},{9,1... | collective-permute-start | bytes 34568 | tf_op jit(solution)/shard_map/ppermute | solution.py:40
  25.3 32.8 %all-to-all-start = ((bf16[8,160,384]{2,1,0:T(8,128)(2,1)}), bf16[8,160,384]{2,1,0:T(8,128)(2,1)S(1)}, u32[]{:S(2)}, u32[]{:S(2)}) async-start(bf16[8,160,384]{2,1,0:T(8,128)(2,1)} %bitcast.6), calls=%async_computation | async-start | bytes 1966080 | tf_op jit(solution)/shard_map/all_to_all | solution.py:430
  28.9 208.2 %all-gather.4.cloned.1.call-start = ((), (), s32[]{:S(2)}) async-start(), calls=%async_computation.4 | async-start | bytes 7372800 | tf_op jit(solution)/shard_map/all_gather | solution.py:444
  32.9 39.0 %collective-permute-start.8 = (bf16[2,2,160,384]{3,2,1,0:T(8,128)(2,1)S(1)}, bf16[2,2,160,384]{3,2,1,0:T(8,128)(2,1)}, u32[]{:S(2)}, u32[]{:S(2)}) collective-permute-start(bf16[2,2,160,384]{3,2,1,0:T(8,128)(2,1)S(1)} %dynamic-slice_bitcast_fusion.8), channel_id=1, source_target_pairs={{0,8},{8,0},{1,9},{9,1},{2,10},{10,2},{3,11},{11,3},{4,12},{12,4},... | collective-permute-start | bytes 1474568 | tf_op jit(solution)/shard_map/ppermute | solution.py:40
  64.3 38.4 %collective-permute-start.7 = (bf16[384,1280]{1,0:T(8,128)(2,1)}, bf16[384,1280]{1,0:T(8,128)(2,1)}, u32[]{:S(2)}, u32[]{:S(2)}) collective-permute-start(bf16[384,1280]{1,0:T(8,128)(2,1)} %add_convert_fusion.11), channel_id=1, source_target_pairs={{0,2},{2,0},{1,3},{3,1},{4,6},{6,4},{5,7},{7,5},{8,10},{10,8},{9,1... | collective-permute-start | bytes 2949128 | tf_op jit(solution)/shard_map/ppermute | solution.py:40
  71.8 35.2 %collective-permute-start.4 = (bf16[384,1280]{1,0:T(8,128)(2,1)}, bf16[384,1280]{1,0:T(8,128)(2,1)}, u32[]{:S(2)}, u32[]{:S(2)}) collective-permute-start(bf16[384,1280]{1,0:T(8,128)(2,1)} %add_convert_fusion.11), channel_id=1, source_target_pairs={{0,8},{8,0},{1,9},{9,1},{2,10},{10,2},{3,11},{11,3},{4,12},{12,4},... | collective-permute-start | bytes 2949128 | tf_op jit(solution)/shard_map/ppermute | solution.py:40
  103.1 40.7 %all-to-all-start.1 = ((bf16[8,160,384]{2,1,0:T(8,128)(2,1)}), bf16[8,160,384]{2,1,0:T(8,128)(2,1)S(1)}, u32[]{:S(2)}, u32[]{:S(2)}) async-start(bf16[8,160,384]{2,1,0:T(8,128)(2,1)} %bitcast.43), calls=%async_computation.1 | async-start | bytes 1966080 | tf_op jit(solution)/shard_map/all_to_all | solution.py:430
  143.8 36.5 %collective-permute-start.11 = (bf16[384,1280]{1,0:T(8,128)(2,1)}, bf16[384,1280]{1,0:T(8,128)(2,1)}, u32[]{:S(2)}, u32[]{:S(2)}) collective-permute-start(bf16[384,1280]{1,0:T(8,128)(2,1)} %add_convert_fusion.10), channel_id=1, source_target_pairs={{0,2},{2,0},{1,3},{3,1},{4,6},{6,4},{5,7},{7,5},{8,10},{10,8},{9,1... | collective-permute-start | bytes 2949128 | tf_op jit(solution)/shard_map/ppermute | solution.py:40
  186.0 46.9 %collective-permute-start.14 = (bf16[384,1280]{1,0:T(8,128)(2,1)}, bf16[384,1280]{1,0:T(8,128)(2,1)S(1)}, u32[]{:S(2)}, u32[]{:S(2)}) collective-permute-start(bf16[384,1280]{1,0:T(8,128)(2,1)} %select_bitcast_fusion), channel_id=1, source_target_pairs={{0,2},{2,0},{1,3},{3,1},{4,6},{6,4},{5,7},{7,5},{8,10},{10,8},{9,1... | collective-permute-start | bytes 2949128 | tf_op jit(solution)/shard_map/ppermute | solution.py:40
  234.2 24.5 %collective-permute-start.17 = (bf16[384,1280]{1,0:T(8,128)(2,1)}, bf16[384,1280]{1,0:T(8,128)(2,1)}, u32[]{:S(2)}, u32[]{:S(2)}) collective-permute-start(bf16[384,1280]{1,0:T(8,128)(2,1)} %add_convert_fusion.9), channel_id=1, source_target_pairs={{0,2},{2,0},{1,3},{3,1},{4,6},{6,4},{5,7},{7,5},{8,10},{10,8},{9,1... | collective-permute-start | bytes 2949128 | tf_op jit(solution)/shard_map/ppermute | solution.py:40
  276.4 24.1 %collective-permute-start.22 = (bf16[384,1280]{1,0:T(8,128)(2,1)S(1)}, bf16[384,1280]{1,0:T(8,128)(2,1)S(1)}, u32[]{:S(2)}, u32[]{:S(2)}) collective-permute-start(bf16[384,1280]{1,0:T(8,128)(2,1)S(1)} %add_convert_fusion.8), channel_id=1, source_target_pairs={{0,2},{2,0},{1,3},{3,1},{4,6},{6,4},{5,7},{7,5},{8,10},{10,8},{9,1... | collective-permute-start | bytes 2949128 | tf_op jit(solution)/shard_map/ppermute | solution.py:40
  278.2 25.4 %collective-permute-start.21 = (bf16[384,1280]{1,0:T(8,128)(2,1)S(1)}, bf16[384,1280]{1,0:T(8,128)(2,1)S(1)}, u32[]{:S(2)}, u32[]{:S(2)}) collective-permute-start(bf16[384,1280]{1,0:T(8,128)(2,1)S(1)} %convolution_convert_fusion.7), channel_id=1, source_target_pairs={{0,8},{8,0},{1,9},{9,1},{2,10},{10,2},{3,11},{11,3},{4,12},{12,4},... | collective-permute-start | bytes 2949128 | tf_op jit(solution)/shard_map/ppermute | solution.py:40
  306.2 21.6 %collective-permute-start.24 = (bf16[768,1280]{1,0:T(8,128)(2,1)}, bf16[768,1280]{1,0:T(8,128)(2,1)}, u32[]{:S(2)}, u32[]{:S(2)}) collective-permute-start(bf16[768,1280]{1,0:T(8,128)(2,1)} %pad_maximum_fusion.7), channel_id=1, source_target_pairs={{0,8},{8,0},{1,9},{9,1},{2,10},{10,2},{3,11},{11,3},{4,12},{12,4},... | collective-permute-start | bytes 5898248 | tf_op jit(solution)/shard_map/ppermute | solution.py:40
  314.3 38.0 %collective-permute-start.26 = (bf16[2,320,1280]{2,1,0:T(8,128)(2,1)}, bf16[2,320,1280]{2,1,0:T(8,128)(2,1)}, u32[]{:S(2)}, u32[]{:S(2)}) collective-permute-start(bf16[2,320,1280]{2,1,0:T(8,128)(2,1)} %get-tuple-element.293), channel_id=1, source_target_pairs={{0,1},{1,0},{2,3},{3,2},{4,5},{5,4},{6,7},{7,6},{8,9},{9,8},{10,11... | collective-permute-start | bytes 4915208 | tf_op jit(solution)/shard_map/ppermute | solution.py:40
  318.0 37.7 %collective-permute-start.27 = (bf16[2,2,320,640]{3,2,1,0:T(8,128)(2,1)}, bf16[2,2,320,640]{3,2,1,0:T(8,128)(2,1)}, u32[]{:S(2)}, u32[]{:S(2)}) collective-permute-start(bf16[2,2,320,640]{3,2,1,0:T(8,128)(2,1)} %get-tuple-element.291), channel_id=1, source_target_pairs={{0,16},{16,0},{1,17},{17,1},{2,18},{18,2},{3,19},{19,3},{4,20},{20... | collective-permute-start | bytes 4915208 | tf_op jit(solution)/shard_map/ppermute | solution.py:40
  320.1 28.7 %collective-permute-start.25 = (bf16[384,1280]{1,0:T(8,128)(2,1)}, bf16[384,1280]{1,0:T(8,128)(2,1)}, u32[]{:S(2)}, u32[]{:S(2)}) collective-permute-start(bf16[384,1280]{1,0:T(8,128)(2,1)} %convert_element_type.312), channel_id=1, source_target_pairs={{0,2},{2,0},{1,3},{3,1},{4,6},{6,4},{5,7},{7,5},{8,10},{10,8},{9,1... | collective-permute-start | bytes 2949128 | tf_op jit(solution)/shard_map/ppermute | solution.py:40
  358.8 32.0 %collective-permute-start.30 = (bf16[2,320,640]{2,1,0:T(8,128)(2,1)}, bf16[2,320,640]{2,1,0:T(8,128)(2,1)}, u32[]{:S(2)}, u32[]{:S(2)}) collective-permute-start(bf16[2,320,640]{2,1,0:T(8,128)(2,1)} %get-tuple-element.307), channel_id=1, source_target_pairs={{0,16},{16,0},{1,17},{17,1},{2,18},{18,2},{3,19},{19,3},{4,20},{20... | collective-permute-start | bytes 2457608 | tf_op jit(solution)/shard_map/ppermute | solution.py:40
  363.4 27.5 %collective-permute-start.31 = (bf16[2,320,640]{2,1,0:T(8,128)(2,1)}, bf16[2,320,640]{2,1,0:T(8,128)(2,1)}, u32[]{:S(2)}, u32[]{:S(2)}) collective-permute-start(bf16[2,320,640]{2,1,0:T(8,128)(2,1)} %get-tuple-element.305), channel_id=1, source_target_pairs={{0,1},{1,0},{2,3},{3,2},{4,5},{5,4},{6,7},{7,6},{8,9},{9,8},{10,11... | collective-permute-start | bytes 2457608 | tf_op jit(solution)/shard_map/ppermute | solution.py:40
  363.9 24.2 %collective-permute-start.33 = (bf16[384,1280]{1,0:T(8,128)(2,1)}, bf16[384,1280]{1,0:T(8,128)(2,1)}, u32[]{:S(2)}, u32[]{:S(2)}) collective-permute-start(bf16[384,1280]{1,0:T(8,128)(2,1)} %add_convert_fusion.7), channel_id=1, source_target_pairs={{0,2},{2,0},{1,3},{3,1},{4,6},{6,4},{5,7},{7,5},{8,10},{10,8},{9,1... | collective-permute-start | bytes 2949128 | tf_op jit(solution)/shard_map/ppermute | solution.py:40
  393.5 23.7 %collective-permute-start.34 = (bf16[384,1280]{1,0:T(8,128)(2,1)S(1)}, bf16[384,1280]{1,0:T(8,128)(2,1)S(1)}, u32[]{:S(2)}, u32[]{:S(2)}) collective-permute-start(bf16[384,1280]{1,0:T(8,128)(2,1)S(1)} %add_convert_fusion.6), channel_id=1, source_target_pairs={{0,2},{2,0},{1,3},{3,1},{4,6},{6,4},{5,7},{7,5},{8,10},{10,8},{9,1... | collective-permute-start | bytes 2949128 | tf_op jit(solution)/shard_map/ppermute | solution.py:40
  420.9 65.2 %all-to-all-start.2 = ((bf16[8,160,384]{2,1,0:T(8,128)(2,1)}), bf16[8,160,384]{2,1,0:T(8,128)(2,1)S(1)}, u32[]{:S(2)}, u32[]{:S(2)}) async-start(bf16[8,160,384]{2,1,0:T(8,128)(2,1)} %bitcast.338), calls=%async_computation.2 | async-start | bytes 1966080 | tf_op jit(solution)/shard_map/all_to_all | solution.py:430
  430.1 20.2 %collective-permute-start.35 = (bf16[2,2,160,640]{3,2,1,0:T(8,128)(2,1)}, bf16[2,2,160,640]{3,2,1,0:T(8,128)(2,1)}, u32[]{:S(2)}, u32[]{:S(2)}) collective-permute-start(bf16[2,2,160,640]{3,2,1,0:T(8,128)(2,1)} %get-tuple-element.303), channel_id=1, source_target_pairs={{0,16},{16,0},{1,17},{17,1},{2,18},{18,2},{3,19},{19,3},{4,20},{20... | collective-permute-start | bytes 2457608 | tf_op jit(solution)/shard_map/ppermute | solution.py:40
  437.0 22.1 %collective-permute-start.36 = (bf16[2,160,1280]{2,1,0:T(8,128)(2,1)}, bf16[2,160,1280]{2,1,0:T(8,128)(2,1)}, u32[]{:S(2)}, u32[]{:S(2)}) collective-permute-start(bf16[2,160,1280]{2,1,0:T(8,128)(2,1)} %get-tuple-element.301), channel_id=1, source_target_pairs={{0,1},{1,0},{2,3},{3,2},{4,5},{5,4},{6,7},{7,6},{8,9},{9,8},{10,11... | collective-permute-start | bytes 2457608 | tf_op jit(solution)/shard_map/ppermute | solution.py:40
  445.3 40.9 %collective-permute-start.41 = (bf16[2,320,640]{2,1,0:T(8,128)(2,1)}, bf16[2,320,640]{2,1,0:T(8,128)(2,1)}, u32[]{:S(2)}, u32[]{:S(2)}) collective-permute-start(bf16[2,320,640]{2,1,0:T(8,128)(2,1)} %get-tuple-element.299), channel_id=1, source_target_pairs={{0,4},{4,0},{1,5},{5,1},{2,6},{6,2},{3,7},{7,3},{8,12},{12,8},{9,1... | collective-permute-start | bytes 2457608 | tf_op jit(solution)/shard_map/ppermute | solution.py:40
  461.6 24.6 %collective-permute-start.38 = (bf16[2,160,640]{2,1,0:T(8,128)(2,1)}, bf16[2,160,640]{2,1,0:T(8,128)(2,1)S(1)}, u32[]{:S(2)}, u32[]{:S(2)}) collective-permute-start(bf16[2,160,640]{2,1,0:T(8,128)(2,1)} %get-tuple-element.334), channel_id=1, source_target_pairs={{0,1},{1,0},{2,3},{3,2},{4,5},{5,4},{6,7},{7,6},{8,9},{9,8},{10,11... | collective-permute-start | bytes 1228808 | tf_op jit(solution)/shard_map/ppermute | solution.py:40
  464.2 21.9 %collective-permute-start.39 = (bf16[2,160,640]{2,1,0:T(8,128)(2,1)}, bf16[2,160,640]{2,1,0:T(8,128)(2,1)}, u32[]{:S(2)}, u32[]{:S(2)}) collective-permute-start(bf16[2,160,640]{2,1,0:T(8,128)(2,1)} %get-tuple-element.332), channel_id=1, source_target_pairs={{0,16},{16,0},{1,17},{17,1},{2,18},{18,2},{3,19},{19,3},{4,20},{20... | collective-permute-start | bytes 1228808 | tf_op jit(solution)/shard_map/ppermute | solution.py:40
  465.0 21.2 %collective-permute-start.40 = (f32[2,2400]{1,0:T(2,128)S(1)}, f32[2,2400]{1,0:T(2,128)S(1)}, u32[]{:S(2)}, u32[]{:S(2)}) collective-permute-start(f32[2,2400]{1,0:T(2,128)S(1)} %bitcast.367), channel_id=1, source_target_pairs={{0,1},{1,0},{2,3},{3,2},{4,5},{5,4},{6,7},{7,6},{8,9},{9,8},{10,11... | collective-permute-start | bytes 57608 | tf_op jit(solution)/shard_map/ppermute | solution.py:40
  486.2 38.8 %all-to-all-start.3 = ((bf16[8,160,384]{2,1,0:T(8,128)(2,1)}), bf16[8,160,384]{2,1,0:T(8,128)(2,1)S(1)}, u32[]{:S(2)}, u32[]{:S(2)}) async-start(bf16[8,160,384]{2,1,0:T(8,128)(2,1)} %bitcast.339), calls=%async_computation.3 | async-start | bytes 1966080 | tf_op jit(solution)/shard_map/all_to_all | solution.py:430
  490.4 34.6 %collective-permute-start.43 = (f32[2400]{0:T(1024)S(1)}, f32[2400]{0:T(1024)S(1)}, u32[]{:S(2)}, u32[]{:S(2)}) collective-permute-start(f32[2400]{0:T(1024)S(1)} %get-tuple-element.279), channel_id=1, source_target_pairs={{0,4},{4,0},{1,5},{5,1},{2,6},{6,2},{3,7},{7,3},{8,12},{12,8},{9,1... | collective-permute-start | bytes 28808 | tf_op jit(solution)/shard_map/ppermute | solution.py:40
  496.0 30.0 %collective-permute-start.49 = (bf16[2,320,320]{2,1,0:T(8,128)(2,1)}, bf16[2,320,320]{2,1,0:T(8,128)(2,1)}, u32[]{:S(2)}, u32[]{:S(2)}) collective-permute-start(bf16[2,320,320]{2,1,0:T(8,128)(2,1)} %constant_dynamic-slice_fusion), channel_id=1, source_target_pairs={{0,8},{8,0},{1,9},{9,1},{2,10},{10,2},{3,11},{11,3},{4,12},{12,4},... | collective-permute-start | bytes 1228808 | tf_op jit(solution)/shard_map/ppermute | solution.py:40
  498.5 34.1 %collective-permute-start.45 = (bf16[2,160,640]{2,1,0:T(8,128)(2,1)}, bf16[2,160,640]{2,1,0:T(8,128)(2,1)}, u32[]{:S(2)}, u32[]{:S(2)}) collective-permute-start(bf16[2,160,640]{2,1,0:T(8,128)(2,1)} %get-tuple-element.330), channel_id=1, source_target_pairs={{0,4},{4,0},{1,5},{5,1},{2,6},{6,2},{3,7},{7,3},{8,12},{12,8},{9,1... | collective-permute-start | bytes 1228808 | tf_op jit(solution)/shard_map/ppermute | solution.py:40
  (110 other events, 774.2 us)
Sparse Core Ops, SparseCore 0:
  18.9 82.5 all-gather.5
  104.3 122.7 all-gather.3
